TPU v7x, 32 devices: a whole 2x2x4 slice. The times are simulated.
32 devices in a mesh: blk: 8 (over z, x), lon: 4 (over y, core).
Axes of the slice: x: 2, y: 2, z: 4, core: 2. Of those that a mesh axis runs over, the one named last changes fastest.
Arguments:
- nodes: float32 [64, 256, 512], P(None, 'blk', 'lon'), may hold values from -6 to 6
- edges: float32 [64, 6, 256, 512], P(None, None, 'blk', 'lon'), may hold values from -6 to 6
- latent_mean: float32 [64, 256, 512], P(None, 'blk', 'lon'), may hold values from -3 to 3
- latent_logstd: float32 [64, 256, 512], P(None, 'blk', 'lon'), may hold values from -1 to 0
- latent_noise: float32 [64, 256, 512], P(None, 'blk', 'lon'), may hold values from -6 to 6
- kl_weight: float32 [1], replicated, may hold values from 0.5 to 2
- band_counts: int32 [8], replicated, may hold values from 32 to 128, as said below
- neighbors: int32 [6, 256, 512], P(None, 'blk', 'lon'), may hold values from 0 to 4419, as said below
- edge_mask: int32 [6, 256, 512], P(None, 'blk', 'lon'), may hold values 0 or 1
- w_edge_in: float32 [64, 192], replicated, may hold values from -0.4375 to 0.4375
- b_edge_in: float32 [64], replicated, may hold values from -3 to 3
- w_edge_out: float32 [64, 64], replicated, may hold values from -0.75 to 0.75
- b_edge_out: float32 [64], replicated, may hold values from -3 to 3
- edge_gain: float32 [64], replicated, may hold values from 0.5 to 1.5
- edge_shift: float32 [64], replicated, may hold values from -3 to 3
- w_node_in: float32 [64, 128], replicated, may hold values from -0.5 to 0.5
- b_node_in: float32 [64], replicated, may hold values from -3 to 3
- w_node_out: float32 [64, 64], replicated, may hold values from -0.75 to 0.75
- b_node_out: float32 [64], replicated, may hold values from -3 to 3
- node_gain: float32 [64], replicated, may hold values from 0.5 to 1.5
- node_shift: float32 [64], replicated, may hold values from -3 to 3
- cotangent: float32 [64, 256, 512], P(None, 'blk', 'lon'), may hold values from -6 to 6
Outputs:
- new_states: float32 [64, 256, 512], P(None, 'blk', 'lon')
- kl_value: float32 [1], replicated
- grad_nodes: float32 [64, 256, 512], P(None, 'blk', 'lon')
- grad_edges: float32 [64, 6, 256, 512], P(None, None, 'blk', 'lon')
- grad_mean: float32 [64, 256, 512], P(None, 'blk', 'lon')
- grad_logstd: float32 [64, 256, 512], P(None, 'blk', 'lon')
- grad_w_edge_in: float32 [64, 192], replicated
- grad_b_edge_in: float32 [64], replicated
- grad_w_edge_out: float32 [64, 64], replicated
- grad_b_edge_out: float32 [64], replicated
- grad_edge_gain: float32 [64], replicated
- grad_edge_shift: float32 [64], replicated
- grad_w_node_in: float32 [64, 128], replicated
- grad_b_node_in: float32 [64], replicated
- grad_w_node_out: float32 [64, 64], replicated
- grad_b_node_out: float32 [64], replicated
- grad_node_gain: float32 [64], replicated
- grad_node_shift: float32 [64], replicated
Inputs may be any that keep to these rules, and one draw needn't show every extreme that they name: `band_counts`: band 8 // 2 holds 128 valid nodes a row and band 0 holds 32; the end bands hold fewer than the middle ones. `neighbors`: the entry for receiver at local row r and column c is er * 130 + ec, naming one of the eight cells around (r + 1, c + 1) in the device's block extended by one cell on every side.
All inputs are finite; a program needn't handle non-finite values. No bound on the sum of `edge_mask` on one device may be relied on, other than what follows from the above.
Results may differ from a plain program's by a relative error of at most 0.0003.
Values sent between devices are 32-bit elements; how exact they have to be, the bound alone decides.
A program may use at most 192 MiB of HBM per device.

v0:
```python
import functools

import jax
import jax.numpy as jnp
from jax import lax
from jax.experimental import pallas as pl
from jax.experimental.pallas import tpu as pltpu
from jax.sharding import PartitionSpec as P

F32 = jnp.float32
BF16 = jnp.bfloat16
MESH = pl.DeviceIdType.MESH
D = 64
LANES = 128
NBR = 6
EPS = 1e-05
HBM = pl.BlockSpec(memory_space=pltpu.HBM)
VMEM = pl.BlockSpec(memory_space=pltpu.VMEM)
SMEM = pl.BlockSpec(memory_space=pltpu.SMEM)

WINDOWS = ((-1, -1), (-1, 0), (-1, 1), (0, -1), (0, 1), (1, -1), (1, 0), (1, 1))


def halves(value):
    high = value.astype(BF16)
    return high, (value - high.astype(F32)).astype(BF16)


def weight_pack(weight, bias=None):
    high, low = halves(weight)
    if bias is None:
        return jnp.concatenate([high, high, low], axis=1)
    bias_high, bias_low = halves(bias)
    place = lax.broadcasted_iota(jnp.int32, (weight.shape[0], 16), 1)
    wide = jnp.where(
        place == 0, bias_high.astype(F32), jnp.where(place == 1, bias_low.astype(F32), 0.0)
    )
    return jnp.concatenate([high, high, wide.astype(BF16), low], axis=1)


def mxu(left, right):
    return jnp.dot(left, right, preferred_element_type=F32)


def outer(left, right):
    return lax.dot_general(
        left, right, (((1,), (1,)), ((), ())), preferred_element_type=F32
    )


def exact(left, right, dims):
    return lax.dot_general(
        left,
        right,
        (dims, ((), ())),
        precision=lax.Precision.HIGHEST,
        preferred_element_type=F32,
    )


def eye():
    return lax.broadcasted_iota(jnp.int32, (D, D), 0) == lax.broadcasted_iota(
        jnp.int32, (D, D), 1
    )


def to_column(row):
    return jnp.sum(jnp.where(eye(), row, 0.0), axis=1, keepdims=True)


def to_row(column):
    return jnp.sum(jnp.where(eye(), column, 0.0), axis=0, keepdims=True)


def lane_ids(rows=D):
    return lax.broadcasted_iota(jnp.int32, (rows, LANES), 1)


def halo_kernel(
    n_blk,
    n_lon,
    counts,
    nodes,
    mean,
    logstd,
    noise,
    w_ei,
    w_eo,
    w_ni,
    w_no,
    vectors,
    state,
    west_out,
    east_out,
    diverged,
    a_edge,
    a_state,
    a_hidden,
    a_edge_t,
    a_send_t,
    a_recv_t,
    a_node_in,
    a_node_out,
    a_node_out_t,
    a_node_in_t,
    columns,
    buf,
    tiles,
    landing,
    in_sem,
    send_sem,
    recv_sem,
):
    rows = nodes.shape[1]
    blk = lax.axis_index("blk")
    lon = lax.axis_index("lon")
    up = lax.rem(blk + n_blk - 1, n_blk)
    down = lax.rem(blk + 1, n_blk)
    west = lax.rem(lon + n_lon - 1, n_lon)
    east = lax.rem(lon + 1, n_lon)
    around = (
        (up, lon),
        (down, lon),
        (blk, west),
        (blk, east),
        (up, west),
        (up, east),
        (down, west),
        (down, east),
    )
    n_groups = in_sem.shape[0]
    group = rows // n_groups
    for g in range(n_groups):
        for r in range(g * group, (g + 1) * group):
            for which, source in enumerate((nodes, mean, logstd, noise)):
                pltpu.make_async_copy(
                    source.at[:, r, :], buf.at[r, which], in_sem.at[g]
                ).start()
    barrier = pltpu.get_barrier_semaphore()
    for place in around:
        pl.semaphore_signal(barrier, inc=1, device_id=place, device_id_type=MESH)

    lane = lane_ids()
    count = counts[blk]
    inside = lane < count
    total = jnp.zeros((D, LANES), F32)
    west_tile = jnp.zeros((D, LANES), F32)
    east_tile = jnp.zeros((D, LANES), F32)
    for g in range(n_groups):
        span = pl.ds(g * group, group)
        pltpu.make_async_copy(buf.at[span], buf.at[span], in_sem.at[g]).wait()
        for r in range(g * group, (g + 1) * group):
            mean_r = buf[r, 1]
            logstd_r = buf[r, 2]
            spread = jnp.exp(logstd_r)
            value = buf[r, 0] + mean_r + spread * buf[r, 3]
            state[r + 1] = value
            term = mean_r * mean_r + spread * spread - 1.0 - 2.0 * logstd_r
            total += jnp.where(inside, term, 0.0)
            moved = pltpu.roll(value, r + 1, 1)
            west_tile = jnp.where(lane == r + 1, moved, west_tile)
            east_tile = jnp.where(lane == r, moved, east_tile)
            if r == 0:
                tiles[0] = value
            if r == rows - 1:
                tiles[1] = value
    tiles[2] = west_tile
    tiles[3] = east_tile
    diverged[...] = jnp.broadcast_to(
        0.5 * jnp.sum(total, axis=1, keepdims=True), (D, LANES)
    )
    pl.semaphore_wait(barrier, 8)
    copies = []
    for slot, (place, tile) in enumerate(zip(around, (0, 1, 2, 3, 0, 0, 1, 1))):
        copies.append(
            pltpu.make_async_remote_copy(
                src_ref=tiles.at[tile],
                dst_ref=landing.at[slot],
                send_sem=send_sem.at[slot],
                recv_sem=recv_sem.at[slot],
                device_id=place,
                device_id_type=MESH,
            )
        )
        copies[-1].start()

    rows_of = [vectors[i] for i in range(8)]
    b_ei, b_eo, gain_e, shift_e, b_ni, b_no, gain_n, shift_n = [
        to_column(row) for row in rows_of
    ]
    for i, column in enumerate((0.5 * b_ei, gain_e, shift_e, 0.5 * b_ni, gain_n, shift_n)):
        columns[i] = jnp.broadcast_to(column, (D, LANES))
    w_in = w_ei[...]
    w_e, w_s, w_r = w_in[:, :D], w_in[:, D : 2 * D], w_in[:, 2 * D :]
    a_edge[...] = weight_pack(0.5 * w_e)
    a_state[...] = jnp.concatenate([weight_pack(0.5 * w_s), weight_pack(0.5 * w_r)], axis=0)
    w_o = w_eo[...]
    w_oc = w_o - jnp.mean(w_o, axis=0, keepdims=True)
    b_oc = b_eo - jnp.mean(b_eo, axis=0, keepdims=True)
    back = 0.5 * exact(w_o, w_oc, ((0,), (0,)))
    b_back = 0.5 * exact(w_o, b_oc, ((0,), (0,)))
    a_hidden[...] = jnp.concatenate(
        [weight_pack(w_oc, b_oc), weight_pack(back, b_back)], axis=0
    )
    a_edge_t[...] = weight_pack(w_e.T)
    a_send_t[...] = weight_pack(w_s.T)
    a_recv_t[...] = weight_pack(w_r.T)
    w_n = w_ni[...]
    a_node_in[...] = weight_pack(0.5 * w_n)
    w_no_v = w_no[...]
    a_node_out[...] = weight_pack(
        w_no_v - jnp.mean(w_no_v, axis=0, keepdims=True),
        b_no - jnp.mean(b_no, axis=0, keepdims=True),
    )
    a_node_out_t[...] = weight_pack(0.5 * w_no_v.T)
    w_nt = w_n.T
    scaled = gain_e * w_nt[D:]
    scaled = scaled - jnp.mean(scaled, axis=0, keepdims=True)
    a_node_in_t[...] = jnp.concatenate(
        [
            weight_pack(w_nt),
            weight_pack(scaled),
            weight_pack(0.5 * exact(w_o, scaled, ((0,), (0,)))),
        ],
        axis=0,
    )

    for copy in copies:
        copy.wait()
    state[rows + 1] = landing[0]
    state[0] = landing[1]
    from_east = landing[2]
    from_west = landing[3]
    corner = lambda slot, at, to: jnp.where(
        lane == to, pltpu.roll(landing[slot], (to - at) % LANES, 1), 0.0
    )
    east_out[...] = (
        pltpu.roll(jnp.where((lane >= 1) & (lane <= rows), from_east, 0.0), LANES - 1, 1)
        + corner(4, 0, rows)
        + corner(6, 0, LANES - 1)
    )
    west_out[...] = (
        pltpu.roll(jnp.where(lane < rows, from_west, 0.0), 1, 1)
        + corner(5, LANES - 1, rows + 1)
        + corner(7, LANES - 1, 0)
    )


def halo_call(n_blk, n_lon, counts, nodes, mean, logstd, noise, w_ei, w_eo, w_ni, w_no, vectors):
    rows = nodes.shape[1]
    tile = jax.ShapeDtypeStruct((D, LANES), F32)
    pack = lambda *shape: jax.ShapeDtypeStruct(shape, BF16)
    return pl.pallas_call(
        functools.partial(halo_kernel, n_blk, n_lon),
        name="state_halo",
        out_shape=(
            jax.ShapeDtypeStruct((rows + 2, D, LANES), F32),
            tile,
            tile,
            tile,
            pack(D, 3 * D),
            pack(2 * D, 3 * D),
            pack(2 * D, 3 * D + 16),
            pack(D, 3 * D),
            pack(D, 3 * D),
            pack(D, 3 * D),
            pack(D, 6 * D),
            pack(D, 3 * D + 16),
            pack(D, 3 * D),
            pack(4 * D, 3 * D),
            jax.ShapeDtypeStruct((6, D, LANES), F32),
        ),
        in_specs=[SMEM] + [HBM] * 4 + [VMEM] * 5,
        out_specs=[VMEM] * 15,
        scratch_shapes=[
            pltpu.VMEM((rows, 4, D, LANES), F32),
            pltpu.VMEM((4, D, LANES), F32),
            pltpu.VMEM((8, D, LANES), F32),
            pltpu.SemaphoreType.DMA((4,)),
            pltpu.SemaphoreType.DMA((8,)),
            pltpu.SemaphoreType.DMA((8,)),
        ],
        compiler_params=pltpu.CompilerParams(
            collective_id=0, has_side_effects=True, vmem_limit_bytes=32 * 2**20
        ),
    )(counts, nodes, mean, logstd, noise, w_ei, w_eo, w_ni, w_no, vectors)


def layer_kernel(
    counts,
    place,
    edges,
    cotangent,
    neighbors,
    edge_mask,
    state,
    west_col,
    east_col,
    diverged,
    a_edge,
    a_state,
    a_hidden,
    a_edge_t,
    a_send_t,
    a_recv_t,
    a_node_in,
    a_node_out,
    a_node_out_t,
    a_node_in_t,
    columns,
    new_states,
    grad_edges,
    part_nodes,
    row_halo,
    col_halo,
    packed,
    xb,
    xs,
    hs,
    cb,
    db,
    slope,
    windows,
    receiver,
    codes,
    valid,
    inverse,
    summed,
    qc_ref,
    qo_ref,
    cot,
    fresh,
    placed,
    grad_recv,
    acc_edge,
    acc_hidden,
    acc_send,
    acc_recv,
    acc_nin,
    acc_nout,
    acc_vec,
    edge_sem,
    cot_sem,
    out_sem,
    new_sem,
):
    rows = edges.shape[2]
    wide = NBR * LANES
    unroll = 2
    lane = lane_ids()
    lane8 = lane_ids(8)

    for r in range(rows):
        for k in range(NBR):
            pltpu.make_async_copy(
                edges.at[:, k, r, :],
                xb.at[r, :, pl.ds(k * LANES, LANES)],
                edge_sem.at[r],
            ).start()
    for r in range(rows):
        pltpu.make_async_copy(cotangent.at[:, r, :], cot.at[r], cot_sem).start()

    count_here, count_prev, count_next = counts[place[0]], counts[place[1]], counts[place[2]]
    row_id = lax.broadcasted_iota(jnp.int32, (rows, LANES), 0)
    col_id = lax.broadcasted_iota(jnp.int32, (rows, LANES), 1)
    above = jnp.where(row_id == 0, count_prev, count_here)
    below = jnp.where(row_id == rows - 1, count_next, count_here)
    codes[...] = jnp.zeros_like(codes)
    valid[...] = jnp.zeros_like(valid)
    inverse[...] = jnp.zeros_like(inverse)
    for k in range(NBR):
        delta = neighbors[k] - (row_id * (LANES + 2) + col_id)
        first = delta < LANES + 2
        middle = delta < 2 * (LANES + 2)
        step = jnp.where(
            first, delta, jnp.where(middle, delta - (LANES + 2), delta - 2 * (LANES + 2))
        )
        code = jnp.where(first, step, jnp.where(middle, 3 + (step >> 1), 5 + step))
        owner = col_id + step - 1
        owner = jnp.where(owner < 0, LANES - 1, jnp.where(owner >= LANES, 0, owner))
        limit = jnp.where(first, above, jnp.where(middle, count_here, below))
        codes[:, k, :] = code
        valid[:, k, :] = jnp.where(
            (col_id < count_here) & (owner < limit), edge_mask[k].astype(F32), 0.0
        )

    half_bias = columns[0]
    sides = []
    for column in (west_col, east_col):
        high, low = halves(column[...])
        sides.append(mxu(a_state[:D], jnp.concatenate([high, low, high], axis=0)))
    west_side, east_side = sides

    def project(t):
        high, low = halves(state[t])
        both = mxu(a_state[...], jnp.concatenate([high, low, high], axis=0))
        send = both[:D]
        windows[t, 1] = send
        mix = pltpu.roll(
            jnp.where(lane == t, west_side, east_side), lax.rem(LANES - t, LANES), 1
        )
        windows[t, 0] = jnp.where(lane == 0, mix, pltpu.roll(send, 1, 1))
        windows[t, 2] = jnp.where(lane == LANES - 1, mix, pltpu.roll(send, LANES - 1, 1))
        receiver[t] = both[D:] + half_bias

    lax.fori_loop(0, (rows + 2) // 2, lambda i, _: (project(2 * i), project(2 * i + 1))[0], None)

    ones16 = jnp.where(
        lax.broadcasted_iota(jnp.int32, (16, wide), 0) < 2, 1.0, 0.0
    ).astype(BF16)

    def forward_row(r):
        pltpu.make_async_copy(xb.at[r], xb.at[r], edge_sem.at[r]).wait()
        x_high, x_low = halves(xb[r])
        xs[r, :D] = x_high
        xs[r, D:] = x_low
        from_edge = mxu(a_edge[...], jnp.concatenate([x_high, x_low, x_high], axis=0))
        hidden = [[None] * 8 for _ in range(NBR)]
        for pair in ((0, 1), (2, 3), (4, 5)):
            masks = {}
            for k in pair:
                code = jnp.broadcast_to(codes[r, pl.ds(k, 1), :], (8, LANES))
                masks[k] = ((code & 1) != 0, (code & 2) != 0, (code & 4) != 0)
            for f in range(8):
                part = pl.ds(8 * f, 8)
                w = [windows[r + 1 + dr, 1 + dc, part, :] for dr, dc in WINDOWS]
                base = receiver[r + 1, part, :]
                for k in pair:
                    b0, b1, b2 = masks[k]
                    low = jnp.where(b1, jnp.where(b0, w[3], w[2]), jnp.where(b0, w[1], w[0]))
                    top = jnp.where(b1, jnp.where(b0, w[7], w[6]), jnp.where(b0, w[5], w[4]))
                    pre = (
                        from_edge[8 * f : 8 * f + 8, k * LANES : (k + 1) * LANES]
                        + base
                        + jnp.where(b2, top, low)
                    )
                    t = jnp.tanh(pre)
                    u = 1.0 + t
                    h = pre * u
                    slope[r, part, pl.ds(k * LANES, LANES)] = u + h * (1.0 - t)
                    hidden[k][f] = h
        highs, lows = [], []
        for k in range(NBR):
            high, low = halves(jnp.concatenate(hidden[k], axis=0))
            highs.append(high)
            lows.append(low)
        high = jnp.concatenate(highs, axis=1)
        low = jnp.concatenate(lows, axis=1)
        hs[r, :D] = high
        hs[r, D : 2 * D] = low
        hs[r, 2 * D :] = ones16
        both = mxu(a_hidden[...], jnp.concatenate([high, low, ones16, high], axis=0))
        cb[r] = both[:D]
        db[r] = both[D:]
        gathered = jnp.zeros((D, LANES), F32)
        for k in range(NBR):
            c = both[:D, k * LANES : (k + 1) * LANES]
            variance = jnp.sum(c * c, axis=0, keepdims=True) * (1.0 / D)
            inv = lax.rsqrt(variance + EPS)
            inverse[r, pl.ds(k, 1), :] = inv
            gathered += (inv * valid[r, pl.ds(k, 1), :]) * c
        summed[r] = gathered

    def forward(i, _):
        for u in range(unroll):
            forward_row(unroll * i + u)

    lax.fori_loop(0, rows // unroll, forward, None)

    for ref in (acc_edge, acc_hidden, acc_send, acc_recv, acc_nin, acc_nout, acc_vec, placed):
        ref[...] = jnp.zeros_like(ref)
    pltpu.make_async_copy(cot, cot, cot_sem).wait()
    chunk = 4

    def tile_cols(tile):
        return jnp.concatenate([tile] * chunk, axis=1)

    gain_e, shift_e = tile_cols(columns[1]), tile_cols(columns[2])
    half_bias_n, gain_n, shift_n = (
        tile_cols(columns[3]),
        tile_cols(columns[4]),
        tile_cols(columns[5]),
    )
    ones_node = ones16[:, : chunk * LANES]

    def node(i, _):
        first = i * chunk
        spread = lambda ref, offset: jnp.concatenate(
            [ref[first + offset + j] for j in range(chunk)], axis=1
        )
        st = spread(state, 1)
        total = spread(summed, 0)
        cot_c = spread(cot, 0)
        degree = jnp.concatenate(
            [jnp.sum(valid[first + j], axis=0, keepdims=True) for j in range(chunk)], axis=1
        )
        incoming = gain_e * total + shift_e * degree
        st_high, st_low = halves(st)
        inc_high, inc_low = halves(incoming)
        tops = jnp.concatenate([st_high, inc_high], axis=0)
        ends = jnp.concatenate([st_low, inc_low], axis=0)
        pre = mxu(a_node_in[...], jnp.concatenate([tops, ends, tops], axis=0)) + half_bias_n
        t = jnp.tanh(pre)
        u = 1.0 + t
        h = pre * u
        slope_n = u + h * (1.0 - t)
        h_high, h_low = halves(h)
        h_all = jnp.concatenate([h_high, h_low, ones_node], axis=0)
        c = mxu(a_node_out[...], jnp.concatenate([h_all, h_high], axis=0))
        inv = lax.rsqrt(jnp.sum(c * c, axis=0, keepdims=True) * (1.0 / D) + EPS)
        n = c * inv
        new = st + (gain_n * n + shift_n)
        q = cot_c * gain_n
        q = q - jnp.sum(q, axis=0, keepdims=True) * (1.0 / D)
        grad = inv * (q - n * (jnp.sum(q * n, axis=0, keepdims=True) * (1.0 / D)))
        g_high, g_low = halves(grad)
        acc_nout[...] += outer(jnp.concatenate([g_high, g_low], axis=0), h_all)
        pre_grad = mxu(a_node_out_t[...], jnp.concatenate([g_high, g_low, g_high], axis=0))
        pre_grad = pre_grad * slope_n
        p_high, p_low = halves(pre_grad)
        acc_nin[...] += outer(
            jnp.concatenate([p_high, p_low], axis=0), jnp.concatenate([tops, ends], axis=0)
        )
        back = mxu(a_node_in_t[...], jnp.concatenate([p_high, p_low, p_high], axis=0))
        grad_incoming = back[D : 2 * D]
        for j in range(chunk):
            s = slice(j * LANES, (j + 1) * LANES)
            fresh[first + j] = new[:, s]
            part_nodes[first + j] = cot_c[:, s] + back[:D, s]
            qc_ref[first + j] = back[2 * D : 3 * D, s]
            qo_ref[first + j] = back[3 * D :, s]
            acc_vec[0] += grad_incoming[:, s] * total[:, s]
            acc_vec[1] += grad_incoming[:, s] * degree[:, s]
            acc_vec[2] += pre_grad[:, s]
            acc_vec[3] += cot_c[:, s] * n[:, s]
            acc_vec[4] += cot_c[:, s]
            pltpu.make_async_copy(
                fresh.at[first + j], new_states.at[:, first + j, :], new_sem
            ).start()

    lax.fori_loop(0, rows // chunk, node, None)

    def backward_row(r):
        qc = qc_ref[r]
        qo = qo_ref[r]
        o_highs, o_lows, p_highs, p_lows = [], [], [], []
        grads = []
        received = None
        for k in range(NBR):
            s = pl.ds(k * LANES, LANES)
            c = cb[r, :, s]
            inv = inverse[r, pl.ds(k, 1), :]
            alpha = inv * valid[r, pl.ds(k, 1), :]
            moment = jnp.sum(qc * c, axis=0, keepdims=True) * (1.0 / D)
            beta = alpha * inv * inv * moment
            high, low = halves(alpha * qc - beta * c)
            o_highs.append(high)
            o_lows.append(low)
            grad = (alpha * qo - beta * db[r, :, s]) * slope[r, :, s]
            grads.append(grad)
            received = grad if received is None else received + grad
            high, low = halves(grad)
            p_highs.append(high)
            p_lows.append(low)
        grad_recv[r] = received
        o_high, o_low, p_high, p_low = [
            jnp.concatenate(x, axis=1) for x in (o_highs, o_lows, p_highs, p_lows)
        ]
        acc_hidden[...] += outer(jnp.concatenate([o_high, o_low], axis=0), hs[r])
        both = jnp.concatenate([p_high, p_low], axis=0)
        acc_edge[...] += outer(both, xs[r])
        xb[r] = mxu(a_edge_t[...], jnp.concatenate([both, p_high], axis=0))
        for k in range(NBR):
            pltpu.make_async_copy(
                xb.at[r, :, pl.ds(k * LANES, LANES)], grad_edges.at[:, k, r, :], out_sem
            ).start()
        code = [jnp.broadcast_to(codes[r, pl.ds(k, 1), :], (8, LANES)) for k in range(NBR)]
        for which, (dr, dc) in enumerate(WINDOWS):
            masks = [code[k] == which for k in range(NBR)]
            for f in range(8):
                part = pl.ds(8 * f, 8)
                value = placed[r + 1 + dr, 1 + dc, part, :]
                for k in range(NBR):
                    value += jnp.where(masks[k], grads[k][8 * f : 8 * f + 8], 0.0)
                placed[r + 1 + dr, 1 + dc, part, :] = value

    def backward(i, _):
        for u in range(unroll):
            backward_row(unroll * i + u)

    lax.fori_loop(0, rows // unroll, backward, None)

    def settle(t, cols):
        west_cells, east_cells = cols
        centre = placed[t, 1]
        to_west = placed[t, 0]
        to_east = placed[t, 2]
        own = (
            centre
            + jnp.where(lane == 0, 0.0, pltpu.roll(to_east, 1, 1))
            + jnp.where(lane == LANES - 1, 0.0, pltpu.roll(to_west, LANES - 1, 1))
        )
        mix = pltpu.roll(jnp.where(lane == 0, to_west, to_east), t, 1)
        west_cells = jnp.where(lane == t, mix, west_cells)
        east_cells = jnp.where(lane == lax.rem(t + LANES - 1, LANES), mix, east_cells)
        return own, (west_cells, east_cells)

    def sends(own, there):
        high, low = halves(own)
        there_high, there_low = halves(there)
        both = jnp.concatenate([high, low], axis=0)
        acc_send[...] += outer(both, jnp.concatenate([there_high, there_low], axis=0))
        return mxu(a_send_t[...], jnp.concatenate([both, high], axis=0))

    ones_row = ones16[:, :LANES]

    def finish(i, cols):
        for u in range(2):
            t = 1 + 2 * i + u
            own, cols = settle(t, cols)
            st = state[t]
            st_high, st_low = halves(st)
            high, low = halves(own)
            both = jnp.concatenate([high, low], axis=0)
            st_both = jnp.concatenate([st_high, st_low], axis=0)
            acc_send[...] += outer(both, st_both)
            grad = mxu(a_send_t[...], jnp.concatenate([both, high], axis=0))
            high, low = halves(grad_recv[t - 1])
            both = jnp.concatenate([high, low], axis=0)
            acc_recv[...] += outer(both, jnp.concatenate([st_both, ones_row], axis=0))
            grad += mxu(a_recv_t[...], jnp.concatenate([both, high], axis=0))
            part_nodes[t - 1] += grad
        return cols

    zero = jnp.zeros((D, LANES), F32)
    own, cols = settle(0, (zero, zero))
    row_halo[0] = sends(own, state[0])
    cols = lax.fori_loop(0, rows // 2, finish, cols)
    own, cols = settle(rows + 1, cols)
    row_halo[1] = sends(own, state[rows + 1])
    col_halo[0] = sends(cols[0], west_col[...])
    col_halo[1] = sends(cols[1], east_col[...])

    def folded(acc):
        half = acc[:D, : 2 * D] + acc[D:, : 2 * D]
        return half + pltpu.roll(half, D, 1)

    left = lane < D
    packed[0] = jnp.where(left, folded(acc_edge), folded(acc_send))
    block = jnp.where(left, folded(acc_recv), 0.0)
    ones_sum = lambda ref: jnp.sum(
        jnp.where(lane_ids()[:, :16] == 0, ref[:D, 2 * D :] + ref[D:, 2 * D :], 0.0),
        axis=1,
        keepdims=True,
    )
    lane_sum = lambda i: jnp.sum(acc_vec[i], axis=1, keepdims=True)
    vectors = (
        ones_sum(acc_recv),
        ones_sum(acc_hidden),
        lane_sum(0),
        lane_sum(1),
        lane_sum(2),
        ones_sum(acc_nout),
        lane_sum(3),
        lane_sum(4),
        diverged[:, :1],
    )
    for i, vector in enumerate(vectors):
        block = jnp.where(lane == D + i, vector, block)
    packed[1] = block
    packed[2] = (
        acc_nin[:D, : 2 * D]
        + acc_nin[D:, : 2 * D]
        + acc_nin[:D, 2 * D :]
        + acc_nin[D:, 2 * D :]
    )
    packed[3] = jnp.where(left, folded(acc_hidden), folded(acc_nout))
    pltpu.make_async_copy(fresh, fresh, new_sem).wait()
    pltpu.make_async_copy(xb, xb, out_sem).wait()


def layer_call(counts, place, edges, cotangent, neighbors, edge_mask, halo):
    rows = edges.shape[2]
    wide = NBR * LANES
    tile = (D, LANES)
    shape = lambda *dims: jax.ShapeDtypeStruct(dims, F32)
    vmem = lambda *dims: pltpu.VMEM(dims, F32)
    return pl.pallas_call(
        layer_kernel,
        name="layer",
        out_shape=(
            shape(D, rows, LANES),
            shape(D, NBR, rows, LANES),
            shape(rows, *tile),
            shape(2, *tile),
            shape(2, *tile),
            shape(4, *tile),
        ),
        in_specs=[SMEM, SMEM, HBM, HBM] + [VMEM] * (2 + len(halo)),
        out_specs=[HBM, HBM] + [VMEM] * 4,
        scratch_shapes=[
            vmem(rows, D, wide),
            pltpu.VMEM((rows, 2 * D, wide), BF16),
            pltpu.VMEM((rows, 2 * D + 16, wide), BF16),
            vmem(rows, D, wide),
            vmem(rows, D, wide),
            vmem(rows, D, wide),
            vmem(rows + 2, 3, *tile),
            vmem(rows + 2, *tile),
            pltpu.VMEM((rows, 8, LANES), jnp.int32),
            vmem(rows, 8, LANES),
            vmem(rows, 8, LANES),
            vmem(rows, *tile),
            vmem(rows, *tile),
            vmem(rows, *tile),
            vmem(rows, *tile),
            vmem(rows, *tile),
            vmem(rows + 2, 3, *tile),
            vmem(rows, *tile),
            vmem(2 * D, 2 * D),
            vmem(2 * D, 2 * D + 16),
            vmem(2 * D, 2 * D),
            vmem(2 * D, 2 * D + 16),
            vmem(2 * D, 4 * D),
            vmem(2 * D, 2 * D + 16),
            vmem(5, *tile),
            pltpu.SemaphoreType.DMA((rows,)),
            pltpu.SemaphoreType.DMA,
            pltpu.SemaphoreType.DMA,
            pltpu.SemaphoreType.DMA,
        ],
        compiler_params=pltpu.CompilerParams(vmem_limit_bytes=60 * 2**20),
    )(counts, place, edges, cotangent, neighbors, edge_mask, *halo)


def sum_kernel(
    n_blk,
    n_lon,
    n_rows,
    part,
    row_halo,
    col_halo,
    total,
    row_in,
    col_in,
    scattered,
    across,
    gathered,
    landing,
    rs_send,
    rs_recv,
    x_send,
    x_recv,
    ag_send,
    ag_recv,
    halo_send,
    halo_recv,
):
    blk = lax.axis_index("blk")
    lon = lax.axis_index("lon")
    up = lax.rem(blk + n_blk - 1, n_blk)
    down = lax.rem(blk + 1, n_blk)
    west = lax.rem(lon + n_lon - 1, n_lon)
    east = lax.rem(lon + 1, n_lon)
    around = (
        (up, lon),
        (down, lon),
        (blk, west),
        (blk, east),
        (up, west),
        (up, east),
        (down, west),
        (down, east),
    )
    size = scattered.shape[0]
    n_groups = across.shape[0]
    per = size // n_lon
    me = lax.rem(blk, per) * n_lon + lon
    own_group = blk // per

    def member(index):
        return (own_group * per + index // n_lon, lax.rem(index, n_lon))

    def other(step):
        return lax.rem(me + step, size)

    barrier = pltpu.get_barrier_semaphore()

    def greet(step, _):
        pl.semaphore_signal(
            barrier, inc=1, device_id=member(other(step)), device_id_type=MESH
        )

    lax.fori_loop(1, size, greet, None)
    expected = size - 1
    if n_groups > 1:
        for place in around:
            pl.semaphore_signal(barrier, inc=1, device_id=place, device_id_type=MESH)

        def greet_group(step, _):
            place = (lax.rem(own_group + step, n_groups) * per + lax.rem(blk, per), lon)
            pl.semaphore_signal(barrier, inc=1, device_id=place, device_id_type=MESH)

        lax.fori_loop(1, n_groups, greet_group, None)
        expected += 8 + n_groups - 1
    pl.semaphore_wait(barrier, expected)

    def scatter(step):
        target = other(step)
        return pltpu.make_async_remote_copy(
            src_ref=part.at[target],
            dst_ref=scattered.at[me],
            send_sem=rs_send,
            recv_sem=rs_recv,
            device_id=member(target),
            device_id_type=MESH,
        )

    lax.fori_loop(1, size, lambda step, _: scatter(step).start(), None)
    copies = []
    for slot, (place, source) in enumerate(
        zip(
            around,
            (
                row_halo.at[0],
                row_halo.at[1],
                col_halo.at[0],
                col_halo.at[1],
                col_halo.at[0],
                col_halo.at[1],
                col_halo.at[0],
                col_halo.at[1],
            ),
        )
    ):
        copies.append(
            pltpu.make_async_remote_copy(
                src_ref=source,
                dst_ref=landing.at[slot],
                send_sem=halo_send.at[slot],
                recv_sem=halo_recv.at[slot],
                device_id=place,
                device_id_type=MESH,
            )
        )
        copies[-1].start()
    scattered[me] = part[me]
    rest = pl.ds(0, size - 1)
    pltpu.make_async_copy(scattered.at[rest], scattered.at[rest], rs_recv).wait()
    mine = scattered[0]
    for i in range(1, size):
        mine = mine + scattered[i]
    if n_groups > 1:
        across[own_group] = mine

        def cross(step):
            place = (lax.rem(own_group + step, n_groups) * per + lax.rem(blk, per), lon)
            return pltpu.make_async_remote_copy(
                src_ref=across.at[own_group],
                dst_ref=across.at[own_group],
                send_sem=x_send,
                recv_sem=x_recv,
                device_id=place,
                device_id_type=MESH,
            )

        lax.fori_loop(1, n_groups, lambda step, _: cross(step).start(), None)
        others = pl.ds(0, n_groups - 1)
        pltpu.make_async_copy(across.at[others], across.at[others], x_recv).wait()
        pltpu.make_async_copy(across.at[others], across.at[others], x_send).wait()
        mine = across[0]
        for i in range(1, n_groups):
            mine = mine + across[i]
    gathered[me] = mine

    def gather(step):
        return pltpu.make_async_remote_copy(
            src_ref=gathered.at[me],
            dst_ref=gathered.at[me],
            send_sem=ag_send,
            recv_sem=ag_recv,
            device_id=member(other(step)),
            device_id_type=MESH,
        )

    lax.fori_loop(1, size, lambda step, _: gather(step).start(), None)
    for copy in copies:
        copy.wait()
    row_in[0] = landing[1]
    row_in[1] = landing[0]
    lane = lane_ids()
    corner = lambda slot, at, to: jnp.where(
        lane == to, pltpu.roll(landing[slot], (to - at) % LANES, 1), 0.0
    )
    col_in[0] = (
        pltpu.roll(jnp.where(lane < n_rows, landing[3], 0.0), 1, 1)
        + corner(7, n_rows, 1)
        + corner(5, LANES - 1, n_rows)
    )
    east_in = (
        jnp.where((lane >= 1) & (lane <= n_rows), landing[2], 0.0)
        + corner(6, n_rows + 1, 1)
        + corner(4, 0, n_rows)
    )
    col_in[1] = pltpu.roll(east_in, LANES - 1, 1)
    pltpu.make_async_copy(gathered.at[rest], gathered.at[rest], ag_recv).wait()
    total[...] = gathered[...]
    pltpu.make_async_copy(scattered.at[rest], scattered.at[rest], rs_send).wait()
    pltpu.make_async_copy(gathered.at[rest], gathered.at[rest], ag_send).wait()


def sum_call(n_blk, n_lon, n_rows, part, row_halo, col_halo):
    size = part.shape[0]
    n_groups = n_blk * n_lon // size
    chunk = part.shape[1:]
    tile = (D, LANES)
    return pl.pallas_call(
        functools.partial(sum_kernel, n_blk, n_lon, n_rows),
        name="sums",
        out_shape=(
            jax.ShapeDtypeStruct(part.shape, F32),
            jax.ShapeDtypeStruct((2, *tile), F32),
            jax.ShapeDtypeStruct((2, *tile), F32),
        ),
        in_specs=[VMEM] * 3,
        out_specs=[VMEM] * 3,
        scratch_shapes=[
            pltpu.VMEM(part.shape, F32),
            pltpu.VMEM((n_groups, *chunk), F32),
            pltpu.VMEM(part.shape, F32),
            pltpu.VMEM((8, *tile), F32),
            pltpu.SemaphoreType.DMA,
            pltpu.SemaphoreType.DMA,
            pltpu.SemaphoreType.DMA,
            pltpu.SemaphoreType.DMA,
            pltpu.SemaphoreType.DMA,
            pltpu.SemaphoreType.DMA,
            pltpu.SemaphoreType.DMA((8,)),
            pltpu.SemaphoreType.DMA((8,)),
        ],
        compiler_params=pltpu.CompilerParams(collective_id=1, has_side_effects=True),
    )(part, row_halo, col_halo)


def final_kernel(
    n_lon,
    counts,
    place,
    kl_weight,
    part_nodes,
    mean,
    logstd,
    noise,
    row_in,
    col_in,
    total,
    grad_nodes,
    grad_mean,
    grad_logstd,
    kl_value,
    g_w_ei,
    g_w_eo,
    g_w_ni,
    g_w_no,
    g_vec,
    buf,
    out,
    in_sem,
    out_sem,
):
    rows = mean.shape[1]
    lane = lane_ids()
    n_groups = in_sem.shape[0]
    group = rows // n_groups
    for g in range(n_groups):
        span = pl.ds(g * group, group)
        for r in range(g * group, (g + 1) * group):
            for which, source in enumerate((mean, logstd, noise)):
                pltpu.make_async_copy(
                    source.at[:, r, :], buf.at[r, which], in_sem.at[g]
                ).start()
            pltpu.make_async_copy(part_nodes.at[r], buf.at[r, 3], in_sem.at[g]).start()
    weight = kl_weight[0]
    inside = jnp.where(lane < counts[place[0]], weight, 0.0)
    blocks = [total[i] for i in range(4)]
    g_w_ei[:, : 2 * D] = blocks[0]
    g_w_ei[:, 2 * D :] = blocks[1][:, :D]
    g_w_ni[...] = blocks[2]
    g_w_eo[...] = blocks[3][:, :D]
    g_w_no[...] = pltpu.roll(blocks[3], D, 1)[:, :D]
    for i in range(8):
        g_vec[i] = to_row(blocks[1][:, D + i : D + i + 1])
    n_valid = counts[0]
    for i in range(1, counts.shape[0]):
        n_valid += counts[i]
    scale = (D * rows * n_lon * n_valid).astype(F32)
    diverged = jnp.sum(blocks[1][:, D + 8 : D + 9], axis=0, keepdims=True)
    kl_value[...] = diverged / jnp.full((1, 1), scale)
    west_in = col_in[0]
    east_in = col_in[1]
    for g in range(n_groups):
        span = pl.ds(g * group, group)
        pltpu.make_async_copy(buf.at[span], buf.at[span], in_sem.at[g]).wait()
        for r in range(g * group, (g + 1) * group):
            mix = pltpu.roll(jnp.where(lane == r + 1, west_in, east_in), LANES - 1 - r, 1)
            grad = buf[r, 3] + jnp.where((lane == 0) | (lane == LANES - 1), mix, 0.0)
            if r == 0:
                grad = grad + row_in[0]
            if r == rows - 1:
                grad = grad + row_in[1]
            spread = jnp.exp(buf[r, 1])
            out[r, 0] = grad
            out[r, 1] = grad + inside * buf[r, 0]
            out[r, 2] = grad * spread * buf[r, 2] + inside * (spread * spread - 1.0)
            for which, target in enumerate((grad_nodes, grad_mean, grad_logstd)):
                pltpu.make_async_copy(
                    out.at[r, which], target.at[:, r, :], out_sem
                ).start()
    pltpu.make_async_copy(out, out, out_sem).wait()


def final_call(n_lon, counts, place, kl_weight, part_nodes, mean, logstd, noise, sums):
    rows = mean.shape[1]
    total, row_in, col_in = sums
    shape = lambda *dims: jax.ShapeDtypeStruct(dims, F32)
    whole = shape(D, rows, LANES)
    return pl.pallas_call(
        functools.partial(final_kernel, n_lon),
        name="final",
        out_shape=(
            whole,
            whole,
            whole,
            shape(1, 1),
            shape(D, 3 * D),
            shape(D, D),
            shape(D, 2 * D),
            shape(D, D),
            shape(8, 1, D),
        ),
        in_specs=[SMEM] * 3 + [HBM] * 4 + [VMEM] * 3,
        out_specs=[HBM] * 3 + [VMEM] * 6,
        scratch_shapes=[
            pltpu.VMEM((rows, 4, D, LANES), F32),
            pltpu.VMEM((rows, 3, D, LANES), F32),
            pltpu.SemaphoreType.DMA((4,)),
            pltpu.SemaphoreType.DMA,
        ],
        compiler_params=pltpu.CompilerParams(vmem_limit_bytes=32 * 2**20),
    )(
        counts,
        place,
        kl_weight,
        part_nodes,
        mean,
        logstd,
        noise,
        row_in,
        col_in,
        total.reshape(4, D, LANES),
    )


def shards(
    nodes,
    edges,
    latent_mean,
    latent_logstd,
    latent_noise,
    kl_weight,
    band_counts,
    neighbors,
    edge_mask,
    w_edge_in,
    b_edge_in,
    w_edge_out,
    b_edge_out,
    edge_gain,
    edge_shift,
    w_node_in,
    b_node_in,
    w_node_out,
    b_node_out,
    node_gain,
    node_shift,
    cotangent,
):
    n_blk = lax.axis_size("blk")
    n_lon = lax.axis_size("lon")
    blk = lax.axis_index("blk").astype(jnp.int32)
    place = jnp.stack([blk, lax.rem(blk + n_blk - 1, n_blk), lax.rem(blk + 1, n_blk)])
    vectors = jnp.stack(
        [
            b_edge_in,
            b_edge_out,
            edge_gain,
            edge_shift,
            b_node_in,
            b_node_out,
            node_gain,
            node_shift,
        ]
    ).reshape(8, 1, D)
    halo = halo_call(
        n_blk,
        n_lon,
        band_counts,
        nodes,
        latent_mean,
        latent_logstd,
        latent_noise,
        w_edge_in,
        w_edge_out,
        w_node_in,
        w_node_out,
        vectors,
    )
    new_states, grad_edges, part_nodes, row_halo, col_halo, packed = layer_call(
        band_counts, place, edges, cotangent, neighbors, edge_mask, halo
    )
    size = min(32, n_blk * n_lon)
    sums = sum_call(
        n_blk, n_lon, nodes.shape[1], packed.reshape(size, 4 * D // size, LANES), row_halo, col_halo
    )
    grad_nodes, grad_mean, grad_logstd, kl_value, g_w_ei, g_w_eo, g_w_ni, g_w_no, g_vec = (
        final_call(
            n_lon,
            band_counts,
            place,
            kl_weight,
            part_nodes,
            latent_mean,
            latent_logstd,
            latent_noise,
            sums,
        )
    )
    g_vec = [g_vec[i, 0] for i in range(8)]
    return (
        new_states,
        kl_value.reshape(1),
        grad_nodes,
        grad_edges,
        grad_mean,
        grad_logstd,
        g_w_ei,
        g_vec[0],
        g_w_eo,
        g_vec[1],
        g_vec[2],
        g_vec[3],
        g_w_ni,
        g_vec[4],
        g_w_no,
        g_vec[5],
        g_vec[6],
        g_vec[7],
    )


def solution(mesh):
    node = P(None, "blk", "lon")
    slot = P(None, None, "blk", "lon")
    return jax.shard_map(
        shards,
        mesh=mesh,
        in_specs=(
            (node, slot, node, node, node, P(), P(), node, node) + (P(),) * 12 + (node,)
        ),
        out_specs=(node, P(), node, slot, node, node) + (P(),) * 12,
        check_vma=False,
    )
```

profile of v0, /device:TPU:0, one launch (start us, length us, event | category | flops | bytes accessed | tf_op | source)
XLA Modules:
  0.0 116.5 jit_solution(17059751707668083363)
XLA Ops:
  1.9 0.8 stack.51
  2.7 1.2 %copy-done = f32[64,32,128]{2,1,0:T(8,128)S(1)} copy-done((f32[64,32,128]{2,1,0:T(8,128)S(1)}, f32[64,32,128]{2,1,0:T(8,128)}, u32[]{:S(2)}) %copy-start) | copy-done | bytes 1048600
  3.9 1.2 %copy-done.2 = f32[64,32,128]{2,1,0:T(8,128)S(1)} copy-done((f32[64,32,128]{2,1,0:T(8,128)S(1)}, f32[64,32,128]{2,1,0:T(8,128)}, u32[]{:S(2)}) %copy-start.2) | copy-done | bytes 1048600
  5.1 1.2 %copy-done.4 = f32[64,32,128]{2,1,0:T(8,128)S(1)} copy-done((f32[64,32,128]{2,1,0:T(8,128)S(1)}, f32[64,32,128]{2,1,0:T(8,128)}, u32[]{:S(2)}) %copy-start.4) | copy-done | bytes 1048600
  6.4 1.2 %copy-done.7 = f32[64,32,128]{2,1,0:T(8,128)S(1)} copy-done((f32[64,32,128]{2,1,0:T(8,128)S(1)}, f32[64,32,128]{2,1,0:T(8,128)}, u32[]{:S(2)}) %copy-start.7) | copy-done | bytes 1048600
  7.6 0.8 copy-done.12
  8.4 0.8 copy-done.18
  9.2 0.8 copy-done.19
  9.9 0.8 copy-done.20
  10.7 0.7 copy-done.31
  11.4 15.2 %state_halo.1 = (f32[34,64,128]{2,1,0:T(8,128)S(1)}, f32[64,128]{1,0:T(8,128)S(1)}, f32[64,128]{1,0:T(8,128)S(1)}, f32[64,128]{1,0:T(8,128)S(1)}, bf16[64,192]{1...) custom-call(s32[8]{0:T(128)S(1)} %copy-done.31, ...), custom_call_target="tpu_custom_call" | custom-call | tf_op jit(solution)/shard_map/state_halo/pallas_call | solution.py:253
  26.6 1.0 copy-done.6
  27.6 0.7 copy-done.9
  28.3 0.7 copy-done.10
  29.0 0.6 copy-done.13
  29.6 0.6 copy-done.14
  30.8 0.6 copy-done.21
  31.4 0.6 copy-done.22
  32.1 0.6 copy-done.23
  32.7 0.6 copy-done.24
  33.3 0.6 copy-done.25
  33.9 0.6 copy-done.26
  34.5 0.6 copy-done.27
  35.1 0.6 copy-done.28
  35.7 0.6 copy-done.29
  36.3 49.5 %layer.1 = (f32[64,32,128]{2,1,0:T(8,128)}, f32[64,6,32,128]{3,2,1,0:T(8,128)}, f32[32,64,128]{2,1,0:T(8,128)}, f32[2,64,128]{2,1,0:T(8,128)}, f32[2,64,128]{2,1,0:T(8,128)}, /*index=5*/f32[4,64,128]{2,1,0:T(8,128)}) custom-call(s32[8]{0:T(128)} %counts.5, s32[3]{0:T(128)} %pad_add_fusion.place, f32[64,6,32,128]{3,2,1,0:T(8,128)} %edges.1, ...), custom_call_target="tpu_custom_call" | custom-call | tf_op jit(solution)/shard_map/layer/pallas_call | solution.py:688
  85.8 18.5 %sums.1 = (f32[32,8,128]{2,1,0:T(8,128)}, f32[2,64,128]{2,1,0:T(8,128)}, f32[2,64,128]{2,1,0:T(8,128)}) custom-call(f32[32,8,128]{2,1,0:T(8,128)} %bitcast.33, f32[2,64,128]{2,1,0:T(8,128)} %get-tuple-element.69.row_halo, f32[2,64,128]{2,1,0:T(8,128)} %get-tuple-element.70.col_halo), custom_call_target="tpu_custom_call" | custom-call | tf_op jit(solution)/shard_map/sums/pallas_call | solution.py:917
  104.4 1.2 %copy-done.8 = f32[32,64,128]{2,1,0:T(8,128)S(1)} copy-done((f32[32,64,128]{2,1,0:T(8,128)S(1)}, f32[32,64,128]{2,1,0:T(8,128)}, u32[]{:S(2)}) %copy-start.8) | copy-done | bytes 1048600
  105.6 0.9 copy-done.11
  106.5 0.8 copy-done.15
  107.3 0.8 copy-done.16
  108.2 7.8 %final.1 = (f32[64,32,128]{2,1,0:T(8,128)}, f32[64,32,128]{2,1,0:T(8,128)}, f32[64,32,128]{2,1,0:T(8,128)}, f32[1,1]{1,0:T(1,128)}, f32[64,192]{1,0:T(8,128)}, /...) custom-call(s32[8]{0:T(128)S(1)} %copy-done.32, s32[3]{0:T(128)S(1)} %copy-done.30, ...), custom_call_target="tpu_custom_call" | custom-call | tf_op jit(solution)/shard_map/final/pallas_call | solution.py:1027
  (41 shorter events, 1.8 us)
Async XLA Ops:
  2.7 1.2 %copy-start = (f32[64,32,128]{2,1,0:T(8,128)S(1)}, f32[64,32,128]{2,1,0:T(8,128)}, u32[]{:S(2)}) copy-start(f32[64,32,128]{2,1,0:T(8,128)} %mean.3) | copy-start | bytes 3145732
  3.9 1.2 %copy-start.2 = (f32[64,32,128]{2,1,0:T(8,128)S(1)}, f32[64,32,128]{2,1,0:T(8,128)}, u32[]{:S(2)}) copy-start(f32[64,32,128]{2,1,0:T(8,128)} %logstd.3) | copy-start | bytes 3145732
  5.1 1.2 %copy-start.4 = (f32[64,32,128]{2,1,0:T(8,128)S(1)}, f32[64,32,128]{2,1,0:T(8,128)}, u32[]{:S(2)}) copy-start(f32[64,32,128]{2,1,0:T(8,128)} %noise.3) | copy-start | bytes 3145732
  6.4 1.2 %copy-start.7 = (f32[64,32,128]{2,1,0:T(8,128)S(1)}, f32[64,32,128]{2,1,0:T(8,128)}, u32[]{:S(2)}) copy-start(f32[64,32,128]{2,1,0:T(8,128)} %nodes.1) | copy-start | bytes 3145732
  7.6 0.8 copy-start.12
  8.4 0.8 copy-start.18
  9.2 0.8 copy-start.19
  9.9 0.8 copy-start.20
  10.7 0.7 copy-start.31
  11.4 93.0 %copy-start.1 = (f32[64,32,128]{2,1,0:T(8,128)S(1)}, f32[64,32,128]{2,1,0:T(8,128)}, u32[]{:S(2)}) copy-start(f32[64,32,128]{2,1,0:T(8,128)} %mean.3) | copy-start | bytes 3145732
  11.4 93.0 %copy-start.3 = (f32[64,32,128]{2,1,0:T(8,128)S(1)}, f32[64,32,128]{2,1,0:T(8,128)}, u32[]{:S(2)}) copy-start(f32[64,32,128]{2,1,0:T(8,128)} %logstd.3) | copy-start | bytes 3145732
  11.4 93.0 %copy-start.5 = (f32[64,32,128]{2,1,0:T(8,128)S(1)}, f32[64,32,128]{2,1,0:T(8,128)}, u32[]{:S(2)}) copy-start(f32[64,32,128]{2,1,0:T(8,128)} %noise.3) | copy-start | bytes 3145732
  11.4 93.0 %copy-start.30 = (s32[3]{0:T(128)S(1)}, s32[3]{0:T(128)}, u32[]{:S(2)}) copy-start(s32[3]{0:T(128)} %pad_add_fusion.place) | copy-start | bytes 40
  11.4 93.0 %copy-start.32 = (s32[8]{0:T(128)S(1)}, s32[8]{0:T(128)}, u32[]{:S(2)}) copy-start(s32[8]{0:T(128)} %counts.5) | copy-start | bytes 100
  26.6 1.0 copy-start.6
  27.6 0.7 copy-start.9
  28.3 0.7 copy-start.10
  29.0 0.6 copy-start.13
  29.6 0.6 copy-start.14
  30.8 0.6 copy-start.21
  31.4 0.6 copy-start.22
  32.0 0.6 copy-start.23
  32.7 0.6 copy-start.24
  33.3 0.6 copy-start.25
  33.9 0.6 copy-start.26
  34.5 0.6 copy-start.27
  35.1 0.6 copy-start.28
  35.7 0.6 copy-start.29
  104.4 1.2 %copy-start.8 = (f32[32,64,128]{2,1,0:T(8,128)S(1)}, f32[32,64,128]{2,1,0:T(8,128)}, u32[]{:S(2)}) copy-start(f32[32,64,128]{2,1,0:T(8,128)} %get-tuple-element.67.part_nodes) | copy-start | bytes 3145732
  105.6 0.9 copy-start.11
  106.5 0.8 copy-start.15
  107.3 0.8 copy-start.16
  (1 other events, 0.6 us)
where the time goes:
time: 117 us; the launch traced here: 116 us
  Pallas kernels  91 us (78%)
  local copies, waits for them, and re-layouts  23.5 us (20%)
  between operations  1.44 us (1%)
    pallas_call x1, Pallas kernels, layer_call(): pl.pallas_call(layer_kernel, name='layer', out_shape=(shape(D, rows, LANE...  49.5 us
    unnamed x66, local copies, waits for them, and re-layouts  22.2 us
    pallas_call x1, Pallas kernels, sum_call(): pl.pallas_call(functools.partial(sum_kernel, n_blk, n_lon, n_rows), name=...  18.5 us
    pallas_call x1, Pallas kernels, halo_call(): pl.pallas_call(functools.partial(halo_kernel, n_blk, n_lon), name='state_...  15.2 us
    pallas_call x1, Pallas kernels, final_call(): pl.pallas_call(functools.partial(final_kernel, n_lon), name='final', out_...  7.77 us

commit v1 on v0

v1 whole, which is shorter than its diff:
```python
import functools

import jax
import jax.numpy as jnp
from jax import lax
from jax.experimental import pallas as pl
from jax.experimental.pallas import tpu as pltpu
from jax.sharding import PartitionSpec as P

F32 = jnp.float32
BF16 = jnp.bfloat16
MESH = pl.DeviceIdType.MESH
D = 64
LANES = 128
NBR = 6
EPS = 1e-05
HBM = pl.BlockSpec(memory_space=pltpu.HBM)
VMEM = pl.BlockSpec(memory_space=pltpu.VMEM)
ROOM = 62 * 2**20
SMEM = pl.BlockSpec(memory_space=pltpu.SMEM)

WINDOWS = ((-1, -1), (-1, 0), (-1, 1), (0, -1), (0, 1), (1, -1), (1, 0), (1, 1))


def halves(value):
    high = value.astype(BF16)
    return high, (value - high.astype(F32)).astype(BF16)


def weight_pack(weight, bias=None):
    high, low = halves(weight)
    if bias is None:
        return jnp.concatenate([high, high, low], axis=1)
    bias_high, bias_low = halves(bias)
    place = lax.broadcasted_iota(jnp.int32, (weight.shape[0], 16), 1)
    wide = jnp.where(
        place == 0, bias_high.astype(F32), jnp.where(place == 1, bias_low.astype(F32), 0.0)
    )
    return jnp.concatenate([high, high, wide.astype(BF16), low], axis=1)


def mxu(left, right):
    return jnp.dot(left, right, preferred_element_type=F32)


def outer(left, right):
    return lax.dot_general(
        left, right, (((1,), (1,)), ((), ())), preferred_element_type=F32
    )


def exact(left, right, dims):
    return lax.dot_general(
        left,
        right,
        (dims, ((), ())),
        precision=lax.Precision.HIGHEST,
        preferred_element_type=F32,
    )


def eye():
    return lax.broadcasted_iota(jnp.int32, (D, D), 0) == lax.broadcasted_iota(
        jnp.int32, (D, D), 1
    )


def to_column(row):
    return jnp.sum(jnp.where(eye(), row, 0.0), axis=1, keepdims=True)


def to_row(column):
    return jnp.sum(jnp.where(eye(), column, 0.0), axis=0, keepdims=True)


def waits(ref, sem):
    pltpu.make_async_copy(ref, ref, sem).wait()


def in_turn(*routines):
    waiting = list(routines)
    while waiting:
        for routine in list(waiting):
            if next(routine, routine) is routine:
                waiting.remove(routine)


def lane_ids(rows=D):
    return lax.broadcasted_iota(jnp.int32, (rows, LANES), 1)


P_HIDDEN, P_EDGE_T, P_SEND_T, P_RECV_T = (0, 128), (128, 192), (192, 256), (256, 320)
P_NODE_IN, P_NODE_OUT, P_NODE_OUT_T, P_NODE_IN_T = (320, 384), (384, 448), (448, 512), (512, 768)
P_ROWS, P_LANES = 768, 384
C_GAIN_E, C_SHIFT_E, C_BIAS_N, C_GAIN_N, C_SHIFT_N, C_VALID, C_DIVERGED, C_COUNT = range(8)


def packed_rows(ref, rows, lanes=3 * D):
    return ref[rows[0] : rows[1], :lanes]


def neighbours(n_blk, n_lon):
    blk = lax.axis_index("blk")
    lon = lax.axis_index("lon")
    up = lax.rem(blk + n_blk - 1, n_blk)
    down = lax.rem(blk + 1, n_blk)
    west = lax.rem(lon + n_lon - 1, n_lon)
    east = lax.rem(lon + 1, n_lon)
    around = (
        (up, lon),
        (down, lon),
        (blk, west),
        (blk, east),
        (up, west),
        (up, east),
        (down, west),
        (down, east),
    )
    return blk, lon, around


def start_kernel(
    n_blk,
    n_lon,
    counts,
    nodes,
    mean,
    logstd,
    noise,
    edges,
    neighbors,
    edge_mask,
    w_ei,
    w_eo,
    w_ni,
    w_no,
    *rest,
):
    vectors = rest[:8]
    (
        state_out,
        cols_out,
        windows_out,
        from_edge_out,
        split_out,
        codes_out,
        valid_out,
        pack_out,
        columns_out,
        buf,
        state,
        windows,
        xb,
        from_edge,
        split,
        receiver,
        nb,
        mk,
        codes,
        valid,
        v_ei,
        v_eo,
        v_ni,
        v_no,
        v_vec,
        pack,
        columns,
        cols,
        tiles,
        landing,
        in_sem,
        edge_sem,
        slot_sem,
        weight_sem,
        send_sem,
        recv_sem,
        out_sem,
    ) = rest[8:]
    rows = nodes.shape[1]
    blk, lon, around = neighbours(n_blk, n_lon)
    barrier = pltpu.get_barrier_semaphore()
    for place in around:
        pl.semaphore_signal(barrier, inc=1, device_id=place, device_id_type=MESH)

    n_groups = in_sem.shape[0]
    group = rows // n_groups

    def load_rows(g):
        def load(i, _):
            r = g * group + i
            for which, source in enumerate((nodes, mean, logstd, noise)):
                pltpu.make_async_copy(
                    source.at[:, r, :], buf.at[r, which], in_sem.at[g]
                ).start()

        lax.fori_loop(0, group, load, None)

    weights = [(w_ei, v_ei), (w_eo, v_eo), (w_ni, v_ni), (w_no, v_no)]
    weights += [(vectors[i], v_vec.at[i]) for i in range(8)]
    for source, target in weights:
        pltpu.make_async_copy(source, target, weight_sem).start()
    for g in range(n_groups):
        load_rows(g)

    def load_edges(r):
        for k in range(NBR):
            pltpu.make_async_copy(
                edges.at[:, k, r, :],
                xb.at[r, :, pl.ds(k * LANES, LANES)],
                edge_sem.at[r],
            ).start()

    def load_slots(r, _):
        pltpu.make_async_copy(
            neighbors.at[:, r, :], nb.at[r, pl.ds(0, NBR), :], slot_sem
        ).start()
        pltpu.make_async_copy(
            edge_mask.at[:, r, :], mk.at[r, pl.ds(0, NBR), :], slot_sem
        ).start()

    ahead = 8
    for r in range(ahead):
        load_edges(r)
    lax.fori_loop(0, rows, load_slots, None)

    for _, target in weights:
        waits(target, weight_sem)
    b_ei, b_eo, gain_e, shift_e, b_ni, b_no, gain_n, shift_n = [
        to_column(v_vec[i]) for i in range(8)
    ]
    lane = lane_ids()
    count = counts[blk]
    inside = lane < count
    n_valid = counts[0]
    for i in range(1, counts.shape[0]):
        n_valid += counts[i]
    for i, column in (
        (C_GAIN_E, gain_e),
        (C_SHIFT_E, shift_e),
        (C_BIAS_N, 0.5 * b_ni),
        (C_GAIN_N, gain_n),
        (C_SHIFT_N, shift_n),
        (C_VALID, jnp.where(inside, 1.0, 0.0)),
        (C_COUNT, jnp.full((D, LANES), (D * rows * n_lon * n_valid).astype(F32))),
    ):
        columns[i] = jnp.broadcast_to(column, (D, LANES))
    w_in = v_ei[...]
    w_e, w_s, w_r = w_in[:, :D], w_in[:, D : 2 * D], w_in[:, 2 * D :]
    a_edge = weight_pack(0.5 * w_e)
    a_state = jnp.concatenate([weight_pack(0.5 * w_s), weight_pack(0.5 * w_r)], axis=0)
    w_o = v_eo[...]
    w_oc = w_o - jnp.mean(w_o, axis=0, keepdims=True)
    b_oc = b_eo - jnp.mean(b_eo, axis=0, keepdims=True)
    back = 0.5 * exact(w_o, w_oc, ((0,), (0,)))
    b_back = 0.5 * exact(w_o, b_oc, ((0,), (0,)))
    w_n = v_ni[...]
    w_nt = w_n.T
    w_out = v_no[...]
    scaled = gain_e * w_nt[D:]
    scaled = scaled - jnp.mean(scaled, axis=0, keepdims=True)

    def put(place, *parts):
        value = jnp.concatenate(parts, axis=0) if len(parts) > 1 else parts[0]
        pack[place[0] : place[1], : value.shape[1]] = value

    put(P_HIDDEN, weight_pack(w_oc, b_oc), weight_pack(back, b_back))
    put(P_EDGE_T, weight_pack(w_e.T))
    put(P_SEND_T, weight_pack(w_s.T))
    put(P_RECV_T, weight_pack(w_r.T))
    put(P_NODE_IN, weight_pack(0.5 * w_n))
    put(
        P_NODE_OUT,
        weight_pack(
            w_out - jnp.mean(w_out, axis=0, keepdims=True),
            b_no - jnp.mean(b_no, axis=0, keepdims=True),
        ),
    )
    put(P_NODE_OUT_T, weight_pack(0.5 * w_out.T))
    put(
        P_NODE_IN_T,
        weight_pack(w_nt),
        weight_pack(scaled),
        weight_pack(0.5 * exact(w_o, scaled, ((0,), (0,)))),
    )
    pltpu.make_async_copy(pack, pack_out, out_sem).start()

    total = jnp.zeros((D, LANES), F32)
    west_tile = jnp.zeros((D, LANES), F32)
    east_tile = jnp.zeros((D, LANES), F32)
    half_bias = 0.5 * b_ei

    def project(t, value):
        high, low = halves(value)
        both = mxu(a_state, jnp.concatenate([high, low, high], axis=0))
        send = both[:D]
        windows[t, 1] = send
        windows[t, 0] = jnp.where(lane == 0, 0.0, pltpu.roll(send, 1, 1))
        windows[t, 2] = jnp.where(lane == LANES - 1, 0.0, pltpu.roll(send, LANES - 1, 1))
        return both[D:] + half_bias

    for g in range(n_groups):
        waits(buf.at[pl.ds(g * group, group)], in_sem.at[g])

        def state_row(i, carry, g=g):
            total, west_tile, east_tile = carry
            r = g * group + i
            mean_r = buf[r, 1]
            logstd_r = buf[r, 2]
            spread = jnp.exp(logstd_r)
            value = buf[r, 0] + mean_r + spread * buf[r, 3]
            state[r + 1] = value
            term = mean_r * mean_r + spread * spread - 1.0 - 2.0 * logstd_r
            total += jnp.where(inside, term, 0.0)
            moved = pltpu.roll(value, r + 1, 1)
            west_tile = jnp.where(lane == r + 1, moved, west_tile)
            east_tile = jnp.where(lane == r, moved, east_tile)
            receiver[r] = project(r + 1, value)
            return total, west_tile, east_tile

        def state_rows(i, carry):
            return state_row(2 * i + 1, state_row(2 * i, carry))

        total, west_tile, east_tile = lax.fori_loop(
            0, group // 2, state_rows, (total, west_tile, east_tile)
        )
    tiles[0] = state[1]
    tiles[1] = state[rows]
    tiles[2] = west_tile
    tiles[3] = east_tile
    columns[C_DIVERGED] = jnp.broadcast_to(
        0.5 * jnp.sum(total, axis=1, keepdims=True), (D, LANES)
    )
    pltpu.make_async_copy(columns, columns_out, out_sem).start()

    waits(nb.at[:, pl.ds(0, NBR), :], slot_sem)
    waits(mk.at[:, pl.ds(0, NBR), :], slot_sem)
    before = counts[lax.rem(blk + n_blk - 1, n_blk)]
    after = counts[lax.rem(blk + 1, n_blk)]
    lane8 = lane_ids(8)
    used = lax.broadcasted_iota(jnp.int32, (8, LANES), 0) < NBR

    def slots(r, _):
        above = jnp.where(r == 0, before, count)
        below = jnp.where(r == rows - 1, after, count)
        delta = nb[r] - (r * (LANES + 2) + lane8)
        first = delta < LANES + 2
        middle = delta < 2 * (LANES + 2)
        step = jnp.where(
            first, delta, jnp.where(middle, delta - (LANES + 2), delta - 2 * (LANES + 2))
        )
        code = jnp.where(first, step, jnp.where(middle, 3 + (step >> 1), 5 + step))
        owner = lane8 + step - 1
        owner = jnp.where(owner < 0, LANES - 1, jnp.where(owner >= LANES, 0, owner))
        limit = jnp.where(first, above, jnp.where(middle, count, below))
        codes[r] = jnp.where(used, code, 0)
        valid[r] = jnp.where(
            used & (lane8 < count) & (owner < limit), mk[r].astype(F32), 0.0
        )

    lax.fori_loop(0, rows, slots, None)
    pltpu.make_async_copy(codes, codes_out, out_sem).start()
    pltpu.make_async_copy(valid, valid_out, out_sem).start()

    def edge_row(r):
        waits(xb.at[r], edge_sem.at[r])
        for k in range(NBR):
            s = pl.ds(k * LANES, LANES)
            high, low = halves(xb[r, :, s])
            split[r, :D, s] = high
            split[r, D:, s] = low
        own = receiver[r]
        for pair in range(NBR // 2):
            s = pl.ds(pair * 2 * LANES, 2 * LANES)
            high = split[r, :D, s]
            out = mxu(a_edge, jnp.concatenate([high, split[r, D:, s], high], axis=0))
            from_edge[r, :, s] = out + jnp.concatenate([own, own], axis=1)
        pltpu.make_async_copy(split.at[r], split_out.at[r], out_sem).start()
        pltpu.make_async_copy(from_edge.at[r], from_edge_out.at[r], out_sem).start()

    def edge_rows(i, _):
        for u in range(2):
            load_edges(2 * i + u + ahead)
            edge_row(2 * i + u)

    def last_rows(i, _):
        for u in range(2):
            edge_row(2 * i + u)

    pause = (rows - ahead) // 2
    lax.fori_loop(0, pause, edge_rows, None)

    pl.semaphore_wait(barrier, 8)
    copies = []
    for slot, (place, tile) in enumerate(zip(around, (0, 1, 2, 3, 0, 0, 1, 1))):
        copies.append(
            pltpu.make_async_remote_copy(
                src_ref=tiles.at[tile],
                dst_ref=landing.at[slot],
                send_sem=send_sem.at[slot],
                recv_sem=recv_sem.at[slot],
                device_id=place,
                device_id_type=MESH,
            )
        )
        copies[-1].start()
    lax.fori_loop(pause, rows // 2, last_rows, None)

    for copy in copies:
        copy.wait()
    state[rows + 1] = landing[0]
    state[0] = landing[1]
    corner = lambda slot, at, to: jnp.where(
        lane == to, pltpu.roll(landing[slot], (to - at) % LANES, 1), 0.0
    )
    cols[1] = (
        pltpu.roll(jnp.where((lane >= 1) & (lane <= rows), landing[2], 0.0), LANES - 1, 1)
        + corner(4, 0, rows)
        + corner(6, 0, LANES - 1)
    )
    cols[0] = (
        pltpu.roll(jnp.where(lane < rows, landing[3], 0.0), 1, 1)
        + corner(5, LANES - 1, rows + 1)
        + corner(7, LANES - 1, 0)
    )
    pltpu.make_async_copy(state, state_out, out_sem).start()
    pltpu.make_async_copy(cols, cols_out, out_sem).start()
    project(0, state[0])
    project(rows + 1, state[rows + 1])
    sides = []
    for i in range(2):
        high, low = halves(cols[i])
        sides.append(mxu(a_state[:D], jnp.concatenate([high, low, high], axis=0)))

    def fix(t, _):
        mix = pltpu.roll(
            jnp.where(lane == t, sides[0], sides[1]), lax.rem(LANES - t, LANES), 1
        )
        windows[t, 0] += jnp.where(lane == 0, mix, 0.0)
        windows[t, 2] += jnp.where(lane == LANES - 1, mix, 0.0)
        pltpu.make_async_copy(windows.at[t], windows_out.at[t], out_sem).start()

    lax.fori_loop(0, (rows + 2) // 2, lambda i, _: (fix(2 * i, _), fix(2 * i + 1, _))[0], None)
    for ref in (pack, columns, codes, valid, split, from_edge, state, cols, windows):
        waits(ref, out_sem)


def start_call(n_blk, n_lon, counts, nodes, mean, logstd, noise, edges, neighbors, mask, weights):
    rows = nodes.shape[1]
    wide = NBR * LANES
    tile = (D, LANES)
    shapes = (
        ((rows + 2, *tile), F32),
        ((2, *tile), F32),
        ((rows + 2, 3, *tile), F32),
        ((rows, D, wide), F32),
        ((rows, 2 * D, wide), BF16),
        ((rows, 8, LANES), jnp.int32),
        ((rows, 8, LANES), F32),
        ((P_ROWS, P_LANES), BF16),
        ((8, *tile), F32),
    )
    vmem = lambda *dims: pltpu.VMEM(dims, F32)
    return pl.pallas_call(
        functools.partial(start_kernel, n_blk, n_lon),
        name="start",
        out_shape=[jax.ShapeDtypeStruct(*shape) for shape in shapes],
        in_specs=[SMEM] + [HBM] * (7 + len(weights)),
        out_specs=[HBM] * len(shapes),
        scratch_shapes=[
            vmem(rows, 4, *tile),
            vmem(rows + 2, *tile),
            vmem(rows + 2, 3, *tile),
            vmem(rows, D, wide),
            vmem(rows, D, wide),
            pltpu.VMEM((rows, 2 * D, wide), BF16),
            vmem(rows, *tile),
            pltpu.VMEM((rows, 8, LANES), jnp.int32),
            pltpu.VMEM((rows, 8, LANES), jnp.int32),
            pltpu.VMEM((rows, 8, LANES), jnp.int32),
            vmem(rows, 8, LANES),
            vmem(D, 3 * D),
            vmem(D, D),
            vmem(D, 2 * D),
            vmem(D, D),
            vmem(8, 1, D),
            pltpu.VMEM((P_ROWS, P_LANES), BF16),
            vmem(8, *tile),
            vmem(2, *tile),
            vmem(4, *tile),
            vmem(8, *tile),
            pltpu.SemaphoreType.DMA((4,)),
            pltpu.SemaphoreType.DMA((rows,)),
            pltpu.SemaphoreType.DMA,
            pltpu.SemaphoreType.DMA,
            pltpu.SemaphoreType.DMA((8,)),
            pltpu.SemaphoreType.DMA((8,)),
            pltpu.SemaphoreType.DMA,
        ],
        compiler_params=pltpu.CompilerParams(
            collective_id=0, has_side_effects=True, vmem_limit_bytes=ROOM
        ),
    )(counts, nodes, mean, logstd, noise, edges, neighbors, mask, *weights)


def layer_kernel(
    cotangent,
    windows_in,
    from_edge_in,
    split_in,
    codes_in,
    valid_in,
    pack_in,
    columns_in,
    state_in,
    new_states,
    grad_edges,
    part_out,
    recv_out,
    placed_out,
    acc_out,
    slope,
    xs,
    hs,
    cb,
    db,
    windows,
    codes,
    valid,
    pack,
    columns,
    state,
    inverse,
    summed,
    qc_ref,
    qo_ref,
    cot,
    fresh,
    part,
    placed,
    grad_recv,
    gather_grads,
    acc_edge,
    acc_hidden,
    acc_nin,
    acc_nout,
    acc_vec,
    acc,
    row_sem,
    in_sem,
    split_sem,
    out_sem,
):
    rows = cotangent.shape[1]
    wide = NBR * LANES
    two = 2 * LANES
    lane = lane_ids()

    for source, target in (
        (codes_in, codes),
        (valid_in, valid),
        (pack_in, pack),
        (columns_in, columns),
    ):
        pltpu.make_async_copy(source, target, in_sem.at[0]).start()
    n_groups = row_sem.shape[0]
    group = rows // n_groups
    spans = []
    for g in range(n_groups):
        span = pl.ds(g * group, group)
        first = 0 if g == 0 else g * group + 2
        last = (g + 1) * group + 2
        spans.append((span, pl.ds(first, last - first)))
        pltpu.make_async_copy(
            windows_in.at[spans[g][1]], windows.at[spans[g][1]], row_sem.at[g]
        ).start()
        pltpu.make_async_copy(from_edge_in.at[span], slope.at[span], row_sem.at[g]).start()
    pltpu.make_async_copy(state_in, state, in_sem.at[1]).start()

    def load_cot(r, _):
        pltpu.make_async_copy(cotangent.at[:, r, :], cot.at[r], in_sem.at[1]).start()

    lax.fori_loop(0, rows, load_cot, None)
    pltpu.make_async_copy(split_in, xs, split_sem).start()

    ones16 = jnp.where(
        lax.broadcasted_iota(jnp.int32, (16, wide), 0) < 2, 1.0, 0.0
    ).astype(BF16)
    ones_two = ones16[:, :two]
    for ref in (codes, valid, pack, columns):
        waits(ref, in_sem.at[0])

    def hidden_unit(r, pair):
        slots = (2 * pair, 2 * pair + 1)
        hidden = {k: [None] * 8 for k in slots}
        masks = {}
        for k in slots:
            code = jnp.broadcast_to(codes[r, pl.ds(k, 1), :], (8, LANES))
            masks[k] = ((code & 1) != 0, (code & 2) != 0, (code & 4) != 0)
        for f in range(8):
            rows_f = pl.ds(8 * f, 8)
            w = [windows[r + 1 + dr, 1 + dc, rows_f, :] for dr, dc in WINDOWS]
            for k in slots:
                s = pl.ds(k * LANES, LANES)
                b0, b1, b2 = masks[k]
                low = jnp.where(b1, jnp.where(b0, w[3], w[2]), jnp.where(b0, w[1], w[0]))
                top = jnp.where(b1, jnp.where(b0, w[7], w[6]), jnp.where(b0, w[5], w[4]))
                pre = slope[r, rows_f, s] + jnp.where(b2, top, low)
                t = jnp.tanh(pre)
                u = 1.0 + t
                h = pre * u
                slope[r, rows_f, s] = u + h * (1.0 - t)
                hidden[k][f] = h
        s = pl.ds(pair * two, two)
        high, low = halves(
            jnp.concatenate([jnp.concatenate(hidden[k], axis=0) for k in slots], axis=1)
        )
        hs[r, :D, s] = high
        hs[r, D : 2 * D, s] = low
        hs[r, 2 * D :, s] = ones_two
        return mxu(
            packed_rows(pack, P_HIDDEN, 3 * D + 16),
            jnp.concatenate([high, low, ones_two, high], axis=0),
        )

    def norm_unit(r, pair, both, total):
        s = pl.ds(pair * two, two)
        cb[r, :, s] = both[:D]
        db[r, :, s] = both[D:]
        for j in range(2):
            k = 2 * pair + j
            c = both[:D, j * LANES : (j + 1) * LANES]
            variance = jnp.sum(c * c, axis=0, keepdims=True) * (1.0 / D)
            inv = lax.rsqrt(variance + EPS)
            inverse[r, pl.ds(k, 1), :] = inv
            total = total + (inv * valid[r, pl.ds(k, 1), :]) * c
        if pair == NBR // 2 - 1:
            summed[r] = total
            total = jnp.zeros((D, LANES), F32)
        return total

    def forward(i, _, unroll=2):
        units = [(unroll * i + u, pair) for u in range(unroll) for pair in range(NBR // 2)]
        total = jnp.zeros((D, LANES), F32)
        pending = None
        for unit in units:
            both = hidden_unit(*unit)
            if pending is not None:
                total = norm_unit(*pending, total)
            pending = (*unit, both)
        norm_unit(*pending, total)

    for g in range(n_groups):
        waits(slope.at[spans[g][0]], row_sem.at[g])
        waits(windows.at[spans[g][1]], row_sem.at[g])
        lax.fori_loop(g * group // 2, (g + 1) * group // 2, forward, None)

    for ref in (acc_edge, acc_hidden, acc_nin, acc_nout, acc_vec, placed):
        ref[...] = jnp.zeros_like(ref)
    waits(cot, in_sem.at[1])
    waits(state, in_sem.at[1])
    chunk = 4

    def node_chunk(first):
        tile_cols = lambda i: jnp.concatenate([columns[i]] * chunk, axis=1)
        spread = lambda ref, offset: jnp.concatenate(
            [ref[first + offset + j] for j in range(chunk)], axis=1
        )
        st = spread(state, 1)
        total = spread(summed, 0)
        degree = jnp.concatenate(
            [jnp.sum(valid[first + j], axis=0, keepdims=True) for j in range(chunk)], axis=1
        )
        incoming = tile_cols(C_GAIN_E) * total + tile_cols(C_SHIFT_E) * degree
        st_high, st_low = halves(st)
        inc_high, inc_low = halves(incoming)
        tops = jnp.concatenate([st_high, inc_high], axis=0)
        ends = jnp.concatenate([st_low, inc_low], axis=0)
        pre = mxu(
            packed_rows(pack, P_NODE_IN, 6 * D), jnp.concatenate([tops, ends, tops], axis=0)
        ) + tile_cols(C_BIAS_N)
        yield
        t = jnp.tanh(pre)
        u = 1.0 + t
        h = pre * u
        slope_n = u + h * (1.0 - t)
        h_high, h_low = halves(h)
        h_all = jnp.concatenate([h_high, h_low, ones16[:, : chunk * LANES]], axis=0)
        c = mxu(
            packed_rows(pack, P_NODE_OUT, 3 * D + 16),
            jnp.concatenate([h_all, h_high], axis=0),
        )
        yield
        cot_c = spread(cot, 0)
        inv = lax.rsqrt(jnp.sum(c * c, axis=0, keepdims=True) * (1.0 / D) + EPS)
        n = c * inv
        new = st + (tile_cols(C_GAIN_N) * n + tile_cols(C_SHIFT_N))
        q = cot_c * tile_cols(C_GAIN_N)
        q = q - jnp.sum(q, axis=0, keepdims=True) * (1.0 / D)
        grad = inv * (q - n * (jnp.sum(q * n, axis=0, keepdims=True) * (1.0 / D)))
        g_high, g_low = halves(grad)
        pre_grad = mxu(
            packed_rows(pack, P_NODE_OUT_T), jnp.concatenate([g_high, g_low, g_high], axis=0)
        )
        acc_nout[...] += outer(jnp.concatenate([g_high, g_low], axis=0), h_all)
        for j in range(chunk):
            s = slice(j * LANES, (j + 1) * LANES)
            fresh[first + j] = new[:, s]
            acc_vec[3] += cot_c[:, s] * n[:, s]
            acc_vec[4] += cot_c[:, s]
            pltpu.make_async_copy(
                fresh.at[first + j], new_states.at[:, first + j, :], out_sem
            ).start()
        yield
        pre_grad = pre_grad * slope_n
        p_high, p_low = halves(pre_grad)
        back = mxu(
            packed_rows(pack, P_NODE_IN_T), jnp.concatenate([p_high, p_low, p_high], axis=0)
        )
        acc_nin[...] += outer(
            jnp.concatenate([p_high, p_low], axis=0), jnp.concatenate([tops, ends], axis=0)
        )
        yield
        grad_incoming = back[D : 2 * D]
        for j in range(chunk):
            s = slice(j * LANES, (j + 1) * LANES)
            part[first + j] = cot_c[:, s] + back[:D, s]
            qc_ref[first + j] = back[2 * D : 3 * D, s]
            qo_ref[first + j] = back[3 * D :, s]
            acc_vec[0] += grad_incoming[:, s] * total[:, s]
            acc_vec[1] += grad_incoming[:, s] * degree[:, s]
            acc_vec[2] += pre_grad[:, s]

    def node(i, _):
        in_turn(node_chunk(2 * chunk * i), node_chunk(2 * chunk * i + chunk))

    lax.fori_loop(0, rows // (2 * chunk), node, None)
    pltpu.make_async_copy(part, part_out, out_sem).start()

    waits(xs, split_sem)

    def grad_unit(r, pair, u, received):
        qc = qc_ref[r]
        qo = qo_ref[r]
        hidden_grads, grads = [], []
        for k in (2 * pair, 2 * pair + 1):
            s = pl.ds(k * LANES, LANES)
            c = cb[r, :, s]
            inv = inverse[r, pl.ds(k, 1), :]
            alpha = inv * valid[r, pl.ds(k, 1), :]
            moment = jnp.sum(qc * c, axis=0, keepdims=True) * (1.0 / D)
            beta = alpha * inv * inv * moment
            hidden_grads.append(alpha * qc - beta * c)
            grad = (alpha * qo - beta * db[r, :, s]) * slope[r, :, s]
            grads.append(grad)
            received = grad if received is None else received + grad
        high, low = halves(jnp.concatenate(hidden_grads, axis=1))
        s = pl.ds(pair * two, two)
        gather_grads[u, :D, s] = high
        gather_grads[u, D : 2 * D, s] = low
        high, low = halves(jnp.concatenate(grads, axis=1))
        gather_grads[u, 2 * D : 3 * D, s] = high
        gather_grads[u, 3 * D :, s] = low
        ge = mxu(
            packed_rows(pack, P_EDGE_T), jnp.concatenate([high, low, high], axis=0)
        )
        return grads, received, ge

    def place_unit(r, pair, grads, ge):
        cb[r, :, pl.ds(pair * two, two)] = ge
        code = [
            jnp.broadcast_to(codes[r, pl.ds(k, 1), :], (8, LANES))
            for k in (2 * pair, 2 * pair + 1)
        ]
        for which, (dr, dc) in enumerate(WINDOWS):
            masks = [c == which for c in code]
            for f in range(8):
                rows_f = pl.ds(8 * f, 8)
                value = placed[r + 1 + dr, 1 + dc, rows_f, :]
                for j in range(2):
                    value += jnp.where(masks[j], grads[j][8 * f : 8 * f + 8], 0.0)
                placed[r + 1 + dr, 1 + dc, rows_f, :] = value

    def products(r, u):
        acc_hidden[...] += outer(gather_grads[u, : 2 * D], hs[r])
        acc_edge[...] += outer(gather_grads[u, 2 * D :], xs[r])

    def backward(i, _, unroll=2):
        pending = None
        for u in range(unroll):
            r = unroll * i + u
            received = None
            for pair in range(NBR // 2):
                grads, received, ge = grad_unit(r, pair, u, received)
                if pending is not None:
                    place_unit(*pending)
                pending = (r, pair, grads, ge)
                if pair == 0 and u > 0:
                    products(r - 1, u - 1)
            grad_recv[r] = received
        place_unit(*pending)
        products(unroll * i + unroll - 1, unroll - 1)
        for u in range(unroll):
            r = unroll * i + u
            pltpu.make_async_copy(grad_recv.at[r], recv_out.at[r], out_sem).start()
            pltpu.make_async_copy(placed.at[r], placed_out.at[r], out_sem).start()
            for k in range(NBR):
                pltpu.make_async_copy(
                    cb.at[r, :, pl.ds(k * LANES, LANES)], grad_edges.at[:, k, r, :], out_sem
                ).start()

    lax.fori_loop(0, rows // 2, backward, None)
    tail = pl.ds(rows, 2)
    pltpu.make_async_copy(placed.at[tail], placed_out.at[tail], out_sem).start()

    def folded(ref):
        half = ref[:D, : 2 * D] + ref[D:, : 2 * D]
        return half + pltpu.roll(half, D, 1)

    left = lane < D
    acc[0] = folded(acc_edge)
    acc[2] = (
        acc_nin[:D, : 2 * D]
        + acc_nin[D:, : 2 * D]
        + acc_nin[:D, 2 * D :]
        + acc_nin[D:, 2 * D :]
    )
    acc[3] = jnp.where(left, folded(acc_hidden), folded(acc_nout))
    ones_sum = lambda ref: jnp.sum(
        jnp.where(lane[:, :16] == 0, ref[:D, 2 * D :] + ref[D:, 2 * D :], 0.0),
        axis=1,
        keepdims=True,
    )
    lane_sum = lambda i: jnp.sum(acc_vec[i], axis=1, keepdims=True)
    block = jnp.zeros((D, LANES), F32)
    for i, vector in (
        (1, ones_sum(acc_hidden)),
        (2, lane_sum(0)),
        (3, lane_sum(1)),
        (4, lane_sum(2)),
        (5, ones_sum(acc_nout)),
        (6, lane_sum(3)),
        (7, lane_sum(4)),
        (8, columns[C_DIVERGED]),
    ):
        block = jnp.where(lane == D + i, vector, block)
    acc[1] = block
    pltpu.make_async_copy(acc, acc_out, out_sem).start()
    for ref in (fresh, part, grad_recv, placed, cb, acc):
        waits(ref, out_sem)


def layer_call(cotangent, windows, from_edge, split, codes, valid, pack, columns, state):
    rows = cotangent.shape[1]
    wide = NBR * LANES
    tile = (D, LANES)
    shape = lambda *dims: jax.ShapeDtypeStruct(dims, F32)
    vmem = lambda *dims: pltpu.VMEM(dims, F32)
    return pl.pallas_call(
        layer_kernel,
        name="layer",
        out_shape=(
            shape(D, rows, LANES),
            shape(D, NBR, rows, LANES),
            shape(rows, *tile),
            shape(rows, *tile),
            shape(rows + 2, 3, *tile),
            shape(4, *tile),
        ),
        in_specs=[HBM] * 9,
        out_specs=[HBM] * 6,
        scratch_shapes=[
            vmem(rows, D, wide),
            pltpu.VMEM((rows, 2 * D, wide), BF16),
            pltpu.VMEM((rows, 2 * D + 16, wide), BF16),
            vmem(rows, D, wide),
            vmem(rows, D, wide),
            vmem(rows + 2, 3, *tile),
            pltpu.VMEM((rows, 8, LANES), jnp.int32),
            vmem(rows, 8, LANES),
            pltpu.VMEM((P_ROWS, P_LANES), BF16),
            vmem(8, *tile),
            vmem(rows + 2, *tile),
            vmem(rows, 8, LANES),
            vmem(rows, *tile),
            vmem(rows, *tile),
            vmem(rows, *tile),
            vmem(rows, *tile),
            vmem(rows, *tile),
            vmem(rows, *tile),
            vmem(rows + 2, 3, *tile),
            vmem(rows, *tile),
            pltpu.VMEM((2, 4 * D, wide), BF16),
            vmem(2 * D, 2 * D),
            vmem(2 * D, 2 * D + 16),
            vmem(2 * D, 4 * D),
            vmem(2 * D, 2 * D + 16),
            vmem(5, *tile),
            vmem(4, *tile),
            pltpu.SemaphoreType.DMA((4,)),
            pltpu.SemaphoreType.DMA((2,)),
            pltpu.SemaphoreType.DMA,
            pltpu.SemaphoreType.DMA,
        ],
        compiler_params=pltpu.CompilerParams(vmem_limit_bytes=ROOM),
    )(cotangent, windows, from_edge, split, codes, valid, pack, columns, state)


def sum_kernel(
    n_blk,
    n_lon,
    acc_in,
    placed_in,
    recv_in,
    part_in,
    state_in,
    cols_in,
    pack_in,
    part_out,
    total_out,
    halo_out,
    acc,
    placed,
    grad_recv,
    part,
    state,
    cols,
    pack,
    own,
    halo,
    acc_send,
    acc_recv,
    packed,
    scattered,
    across,
    gathered,
    landing,
    halo_in,
    in_sem,
    row_sem,
    rs_send,
    rs_recv,
    x_send,
    x_recv,
    ag_send,
    ag_recv,
    halo_send,
    halo_recv,
    out_sem,
):
    rows = recv_in.shape[0]
    blk, lon, around = neighbours(n_blk, n_lon)
    size = scattered.shape[0]
    n_groups = across.shape[0]
    per = size // n_lon
    me = lax.rem(blk, per) * n_lon + lon
    own_group = blk // per
    lane = lane_ids()

    def member(index):
        return (own_group * per + index // n_lon, lax.rem(index, n_lon))

    def other(step):
        return lax.rem(me + step, size)

    def peer(step):
        return (lax.rem(own_group + step, n_groups) * per + lax.rem(blk, per), lon)

    half = rows // 2
    for h in range(2):
        span = pl.ds(h * half, half)
        span3 = pl.ds(0, half + 1) if h == 0 else pl.ds(half + 1, half + 1)
        for source, target in (
            (placed_in.at[span3], placed.at[span3]),
            (state_in.at[span3], state.at[span3]),
            (recv_in.at[span], grad_recv.at[span]),
        ):
            pltpu.make_async_copy(source, target, row_sem.at[h]).start()
    small = (
        (pack_in.at[pl.ds(P_SEND_T[0], 2 * D)], pack),
        (cols_in, cols),
        (acc_in, acc),
        (part_in, part),
    )
    for i, (source, target) in enumerate(small):
        pltpu.make_async_copy(source, target, in_sem.at[i]).start()

    barrier = pltpu.get_barrier_semaphore()

    def greet(step, _):
        pl.semaphore_signal(
            barrier, inc=1, device_id=member(other(step)), device_id_type=MESH
        )

    lax.fori_loop(1, size, greet, None)
    expected = size - 1
    if n_groups > 1:
        for place in around:
            pl.semaphore_signal(barrier, inc=1, device_id=place, device_id_type=MESH)

        def greet_group(step, _):
            pl.semaphore_signal(barrier, inc=1, device_id=peer(step), device_id_type=MESH)

        lax.fori_loop(1, n_groups, greet_group, None)
        expected += 8 + n_groups - 1

    acc_send[...] = jnp.zeros_like(acc_send)
    acc_recv[...] = jnp.zeros_like(acc_recv)

    def settle(t, cells):
        west_cells, east_cells = cells
        to_west = placed[t, 0]
        to_east = placed[t, 2]
        value = (
            placed[t, 1]
            + jnp.where(lane == 0, 0.0, pltpu.roll(to_east, 1, 1))
            + jnp.where(lane == LANES - 1, 0.0, pltpu.roll(to_west, LANES - 1, 1))
        )
        own[t] = value
        mix = pltpu.roll(jnp.where(lane == 0, to_west, to_east), t, 1)
        west_cells = jnp.where(lane == t, mix, west_cells)
        east_cells = jnp.where(lane == lax.rem(t + LANES - 1, LANES), mix, east_cells)
        return value, (west_cells, east_cells)

    def both_halves(value):
        return jnp.concatenate(halves(value), axis=0)

    ones_row = jnp.where(
        lax.broadcasted_iota(jnp.int32, (16, 4 * LANES), 0) < 1, 1.0, 0.0
    ).astype(BF16)

    def collect(i, cells):
        values, there, received = [], [], []
        for u in range(4):
            t = 1 + 4 * i + u
            value, cells = settle(t, cells)
            values.append(value)
            there.append(state[t])
            received.append(grad_recv[t - 1])
        wide = lambda parts: both_halves(jnp.concatenate(parts, axis=1))
        there = wide(there)
        acc_send[...] += outer(wide(values), there)
        acc_recv[...] += outer(wide(received), jnp.concatenate([there, ones_row], axis=0))
        return cells

    zero = jnp.zeros((D, LANES), F32)
    for h in range(2):
        span = pl.ds(h * half, half)
        waits(placed.at[pl.ds(h * (half + 1), half + 1)], row_sem.at[h])
        waits(state.at[pl.ds(h * (half + 1), half + 1)], row_sem.at[h])
        waits(grad_recv.at[span], row_sem.at[h])
        if h == 0:
            _, cells = settle(0, (zero, zero))
        cells = lax.fori_loop(h * half // 4, (h + 1) * half // 4, collect, cells)
    _, cells = settle(rows + 1, cells)
    waits(cols, in_sem.at[1])
    edge_values = jnp.concatenate([own[0], own[rows + 1], cells[0], cells[1]], axis=1)
    edge_states = jnp.concatenate([state[0], state[rows + 1], cols[0], cols[1]], axis=1)
    acc_send[...] += outer(both_halves(edge_values), both_halves(edge_states))

    def folded(ref):
        part_sum = ref[:D, : 2 * D] + ref[D:, : 2 * D]
        return part_sum + pltpu.roll(part_sum, D, 1)

    left = lane < D
    waits(acc, in_sem.at[2])
    ones_sum = jnp.sum(
        jnp.where(lane[:, :16] == 0, acc_recv[:D, 2 * D :] + acc_recv[D:, 2 * D :], 0.0),
        axis=1,
        keepdims=True,
    )
    chunk = packed.shape[1]
    blocks = (
        jnp.where(left, acc[0], folded(acc_send)),
        jnp.where(left, folded(acc_recv), jnp.where(lane == D, ones_sum, acc[1])),
        acc[2],
        acc[3],
    )
    per_block = D // chunk
    for i, block in enumerate(blocks):
        for j in range(per_block):
            packed[i * per_block + j] = block[j * chunk : (j + 1) * chunk]
    pl.semaphore_wait(barrier, expected)

    def scatter(step, _):
        target = other(step)
        pltpu.make_async_remote_copy(
            src_ref=packed.at[target],
            dst_ref=scattered.at[me],
            send_sem=rs_send,
            recv_sem=rs_recv,
            device_id=member(target),
            device_id_type=MESH,
        ).start()

    lax.fori_loop(1, size, scatter, None)
    scattered[me] = packed[me]

    waits(pack, in_sem.at[0])
    a_send = pack[:D, : 3 * D]
    a_recv = pack[D : 2 * D, : 3 * D]
    high, low = halves(edge_values)
    edge_grads = mxu(a_send, jnp.concatenate([high, low, high], axis=0))
    for i in range(4):
        halo[i] = edge_grads[:, i * LANES : (i + 1) * LANES]
    copies = []
    for slot, (place, source) in enumerate(zip(around, (0, 1, 2, 3, 2, 3, 2, 3))):
        copies.append(
            pltpu.make_async_remote_copy(
                src_ref=halo.at[source],
                dst_ref=landing.at[slot],
                send_sem=halo_send.at[slot],
                recv_sem=halo_recv.at[slot],
                device_id=place,
                device_id_type=MESH,
            )
        )
        copies[-1].start()
    waits(part, in_sem.at[3])

    def finish(i, _):
        for u in range(2):
            first = 4 * i + 2 * u
            grads = None
            for weights, ref, offset in ((a_send, own, 1), (a_recv, grad_recv, 0)):
                high, low = halves(
                    jnp.concatenate([ref[first + offset], ref[first + offset + 1]], axis=1)
                )
                product = mxu(weights, jnp.concatenate([high, low, high], axis=0))
                grads = product if grads is None else grads + product
            for j in range(2):
                part[first + j] += grads[:, j * LANES : (j + 1) * LANES]

    lax.fori_loop(0, rows // 4, finish, None)
    pltpu.make_async_copy(part, part_out, out_sem).start()

    others = pl.ds(0, size - 1)
    waits(scattered.at[others], rs_recv)
    mine = scattered[0]
    for i in range(1, size):
        mine = mine + scattered[i]
    if n_groups > 1:
        across[own_group] = mine

        def cross(step, _):
            pltpu.make_async_remote_copy(
                src_ref=across.at[own_group],
                dst_ref=across.at[own_group],
                send_sem=x_send,
                recv_sem=x_recv,
                device_id=peer(step),
                device_id_type=MESH,
            ).start()

        lax.fori_loop(1, n_groups, cross, None)
        rest = pl.ds(0, n_groups - 1)
        waits(across.at[rest], x_recv)
        waits(across.at[rest], x_send)
        mine = across[0]
        for i in range(1, n_groups):
            mine = mine + across[i]
    gathered[me] = mine

    def gather(step, _):
        pltpu.make_async_remote_copy(
            src_ref=gathered.at[me],
            dst_ref=gathered.at[me],
            send_sem=ag_send,
            recv_sem=ag_recv,
            device_id=member(other(step)),
            device_id_type=MESH,
        ).start()

    lax.fori_loop(1, size, gather, None)
    for copy in copies:
        copy.wait()
    halo_in[0] = landing[1]
    halo_in[1] = landing[0]
    corner = lambda slot, at, to: jnp.where(
        lane == to, pltpu.roll(landing[slot], (to - at) % LANES, 1), 0.0
    )
    halo_in[2] = (
        pltpu.roll(jnp.where(lane < rows, landing[3], 0.0), 1, 1)
        + corner(7, rows, 1)
        + corner(5, LANES - 1, rows)
    )
    east_in = (
        jnp.where((lane >= 1) & (lane <= rows), landing[2], 0.0)
        + corner(6, rows + 1, 1)
        + corner(4, 0, rows)
    )
    halo_in[3] = pltpu.roll(east_in, LANES - 1, 1)
    pltpu.make_async_copy(halo_in, halo_out, out_sem).start()
    waits(gathered.at[others], ag_recv)
    pltpu.make_async_copy(gathered, total_out, out_sem).start()
    waits(scattered.at[others], rs_send)
    waits(gathered.at[others], ag_send)
    for ref in (part, halo_in, gathered):
        waits(ref, out_sem)


def sum_call(n_blk, n_lon, acc, placed, recv, part, state, cols, pack):
    rows = recv.shape[0]
    size = min(32, n_blk * n_lon)
    n_groups = n_blk * n_lon // size
    chunk = (4 * D // size, LANES)
    tile = (D, LANES)
    shape = lambda *dims: jax.ShapeDtypeStruct(dims, F32)
    vmem = lambda *dims: pltpu.VMEM(dims, F32)
    dma = pltpu.SemaphoreType.DMA
    return pl.pallas_call(
        functools.partial(sum_kernel, n_blk, n_lon),
        name="sums",
        out_shape=(shape(rows, *tile), shape(size, *chunk), shape(4, *tile)),
        in_specs=[HBM] * 7,
        out_specs=[HBM] * 3,
        scratch_shapes=[
            vmem(4, *tile),
            vmem(rows + 2, 3, *tile),
            vmem(rows, *tile),
            vmem(rows, *tile),
            vmem(rows + 2, *tile),
            vmem(2, *tile),
            pltpu.VMEM((2 * D, P_LANES), BF16),
            vmem(rows + 2, *tile),
            vmem(4, *tile),
            vmem(2 * D, 2 * D),
            vmem(2 * D, 2 * D + 16),
            vmem(size, *chunk),
            vmem(size, *chunk),
            vmem(n_groups, *chunk),
            vmem(size, *chunk),
            vmem(8, *tile),
            vmem(4, *tile),
            dma((4,)),
            dma((2,)),
            dma,
            dma,
            dma,
            dma,
            dma,
            dma,
            dma((8,)),
            dma((8,)),
            dma,
        ],
        compiler_params=pltpu.CompilerParams(
            collective_id=1, has_side_effects=True, vmem_limit_bytes=ROOM
        ),
    )(acc, placed, recv, part, state, cols, pack)


def final_kernel(
    kl_weight,
    part_nodes,
    mean,
    logstd,
    noise,
    total_in,
    halo_in,
    columns_in,
    grad_nodes,
    grad_mean,
    grad_logstd,
    kl_value,
    g_w_ei,
    g_w_eo,
    g_w_ni,
    g_w_no,
    *rest,
):
    g_vec = rest[:8]
    buf, out, total, halo, columns, in_sem, small_sem, out_sem = rest[8:]
    rows = mean.shape[1]
    lane = lane_ids()
    for i, (source, target) in enumerate(
        ((total_in, total), (halo_in, halo), (columns_in, columns))
    ):
        pltpu.make_async_copy(source, target, small_sem.at[i]).start()
    n_groups = in_sem.shape[0]
    group = rows // n_groups
    for g in range(n_groups):

        def load(i, _, g=g):
            r = g * group + i
            for which, source in enumerate((mean, logstd, noise)):
                pltpu.make_async_copy(
                    source.at[:, r, :], buf.at[r, which], in_sem.at[g]
                ).start()
            pltpu.make_async_copy(part_nodes.at[r], buf.at[r, 3], in_sem.at[g]).start()

        lax.fori_loop(0, group, load, None)
    waits(halo, small_sem.at[1])
    waits(columns, small_sem.at[2])
    inside = kl_weight[0] * columns[C_VALID]
    west_in = halo[2]
    east_in = halo[3]
    for g in range(n_groups):
        span = pl.ds(g * group, group)
        waits(buf.at[span], in_sem.at[g])

        def finish(i, _, g=g):
            for u in range(2):
                r = g * group + 2 * i + u
                mix = pltpu.roll(
                    jnp.where(lane == r + 1, west_in, east_in), LANES - 1 - r, 1
                )
                grad = buf[r, 3] + jnp.where((lane == 0) | (lane == LANES - 1), mix, 0.0)
                grad = grad + jnp.where(r == 0, 1.0, 0.0) * halo[0]
                grad = grad + jnp.where(r == rows - 1, 1.0, 0.0) * halo[1]
                spread = jnp.exp(buf[r, 1])
                out[r, 0] = grad
                out[r, 1] = grad + inside * buf[r, 0]
                out[r, 2] = grad * spread * buf[r, 2] + inside * (spread * spread - 1.0)
                for which, target in enumerate((grad_nodes, grad_mean, grad_logstd)):
                    pltpu.make_async_copy(
                        out.at[r, which], target.at[:, r, :], out_sem
                    ).start()

        lax.fori_loop(0, group // 2, finish, None)
    waits(total, small_sem.at[0])
    chunk = total.shape[1]
    per_block = D // chunk
    blocks = [
        jnp.concatenate([total[i * per_block + j] for j in range(per_block)], axis=0)
        for i in range(4)
    ]
    g_w_ei[:, : 2 * D] = blocks[0]
    g_w_ei[:, 2 * D :] = blocks[1][:, :D]
    g_w_ni[...] = blocks[2]
    g_w_eo[...] = blocks[3][:, :D]
    g_w_no[...] = pltpu.roll(blocks[3], D, 1)[:, :D]
    for i in range(8):
        g_vec[i][...] = to_row(blocks[1][:, D + i : D + i + 1])
    diverged = jnp.sum(blocks[1][:, D + 8 : D + 9], axis=0, keepdims=True)
    kl_value[...] = diverged / columns[C_COUNT][:1, :1]
    waits(out, out_sem)


def final_call(kl_weight, part_nodes, mean, logstd, noise, total, halo, columns):
    rows = mean.shape[1]
    tile = (D, LANES)
    shape = lambda *dims: jax.ShapeDtypeStruct(dims, F32)
    whole = shape(D, rows, LANES)
    return pl.pallas_call(
        final_kernel,
        name="final",
        out_shape=(
            whole,
            whole,
            whole,
            shape(1, 1),
            shape(D, 3 * D),
            shape(D, D),
            shape(D, 2 * D),
            shape(D, D),
        )
        + (shape(1, D),) * 8,
        in_specs=[SMEM] + [HBM] * 7,
        out_specs=[HBM] * 3 + [VMEM] * 13,
        scratch_shapes=[
            pltpu.VMEM((rows, 4, *tile), F32),
            pltpu.VMEM((rows, 3, *tile), F32),
            pltpu.VMEM(total.shape, F32),
            pltpu.VMEM((4, *tile), F32),
            pltpu.VMEM((8, *tile), F32),
            pltpu.SemaphoreType.DMA((4,)),
            pltpu.SemaphoreType.DMA((3,)),
            pltpu.SemaphoreType.DMA,
        ],
        compiler_params=pltpu.CompilerParams(vmem_limit_bytes=ROOM),
    )(kl_weight, part_nodes, mean, logstd, noise, total, halo, columns)


def shards(
    nodes,
    edges,
    latent_mean,
    latent_logstd,
    latent_noise,
    kl_weight,
    band_counts,
    neighbors,
    edge_mask,
    w_edge_in,
    b_edge_in,
    w_edge_out,
    b_edge_out,
    edge_gain,
    edge_shift,
    w_node_in,
    b_node_in,
    w_node_out,
    b_node_out,
    node_gain,
    node_shift,
    cotangent,
):
    n_blk = lax.axis_size("blk")
    n_lon = lax.axis_size("lon")
    vectors = (
        b_edge_in,
        b_edge_out,
        edge_gain,
        edge_shift,
        b_node_in,
        b_node_out,
        node_gain,
        node_shift,
    )
    weights = (w_edge_in, w_edge_out, w_node_in, w_node_out)
    weights += tuple(vector.reshape(1, D) for vector in vectors)
    state, cols, windows, from_edge, split, codes, valid, pack, columns = start_call(
        n_blk,
        n_lon,
        band_counts,
        nodes,
        latent_mean,
        latent_logstd,
        latent_noise,
        edges,
        neighbors,
        edge_mask,
        weights,
    )
    new_states, grad_edges, part, recv, placed, acc = layer_call(
        cotangent, windows, from_edge, split, codes, valid, pack, columns, state
    )
    part, total, halo = sum_call(n_blk, n_lon, acc, placed, recv, part, state, cols, pack)
    grad_nodes, grad_mean, grad_logstd, kl_value, g_w_ei, g_w_eo, g_w_ni, g_w_no, *g_vec = (
        final_call(
            kl_weight,
            part,
            latent_mean,
            latent_logstd,
            latent_noise,
            total,
            halo,
            columns,
        )
    )
    g_vec = [vector.reshape(D) for vector in g_vec]
    return (
        new_states,
        kl_value.reshape(1),
        grad_nodes,
        grad_edges,
        grad_mean,
        grad_logstd,
        g_w_ei,
        g_vec[0],
        g_w_eo,
        g_vec[1],
        g_vec[2],
        g_vec[3],
        g_w_ni,
        g_vec[4],
        g_w_no,
        g_vec[5],
        g_vec[6],
        g_vec[7],
    )


def solution(mesh):
    node = P(None, "blk", "lon")
    slot = P(None, None, "blk", "lon")
    return jax.shard_map(
        shards,
        mesh=mesh,
        in_specs=(
            (node, slot, node, node, node, P(), P(), node, node) + (P(),) * 12 + (node,)
        ),
        out_specs=(node, P(), node, slot, node, node) + (P(),) * 12,
        check_vma=False,
    )
```

time: 117 us -> 78.5 us (0.67)
  local copies, waits for them, and re-layouts: 23.5 us -> 0 us
  Pallas kernels: 91 us -> 77 us
    unnamed x66 -> x0, local copies, waits for them, and re-layouts: 22.2 us -> none
    pallas_call x1, Pallas kernels: 49.5 us -> 28.7 us  [layer_call(): pl.pallas_call(layer_kernel, name='layer', out_shape=(shape(D, rows, LANE...]
    pallas_call x3, Pallas kernels: 41.5 us -> 48.3 us  [the longest x1 24.4 us: start_call(): pl.pallas_call(functools.partial(start_kernel, n_blk, n_lon), name='start...]
where the time goes in v1:
time: 78.5 us; the launch traced here: 78.3 us
  Pallas kernels  77 us (98%)
  between operations  1.33 us (2%)
    pallas_call x1, Pallas kernels, layer_call(): pl.pallas_call(layer_kernel, name='layer', out_shape=(shape(D, rows, LANE...  28.7 us
    pallas_call x1, Pallas kernels, start_call(): pl.pallas_call(functools.partial(start_kernel, n_blk, n_lon), name='start...  24.4 us
    pallas_call x1, Pallas kernels, sum_call(): pl.pallas_call(functools.partial(sum_kernel, n_blk, n_lon), name='sums',...  18.7 us
    pallas_call x1, Pallas kernels, final_call(): pl.pallas_call(final_kernel, name='final', out_shape=(whole, whole, whole...  5.16 us

profile of v1, /device:TPU:0, one launch (start us, length us, event | category | flops | bytes accessed | tf_op | source)
XLA Modules:
  0.0 78.3 jit_solution(12248004591631113314)
XLA Ops:
  0.7 24.4 %start.1 = (f32[34,64,128]{2,1,0:T(8,128)}, f32[2,64,128]{2,1,0:T(8,128)}, f32[34,3,64,128]{3,2,1,0:T(8,128)}, f32[32,64,768]{2,1,0:T(8,128)}, bf16[32,128,768]{...) custom-call(s32[8]{0:T(128)} %counts.1, ...), custom_call_target="tpu_custom_call" | custom-call | tf_op jit(solution)/shard_map/start/pallas_call | solution.py:463
  25.0 28.7 %layer.1 = (f32[64,32,128]{2,1,0:T(8,128)}, f32[64,6,32,128]{3,2,1,0:T(8,128)}, f32[32,64,128]{2,1,0:T(8,128)}, f32[32,64,128]{2,1,0:T(8,128)}, f32[34,3,64,128]{3,2,1,0:T(8,128)}, /*index=5*/f32[4,64,128]{2,1,0:T(8,128)}) custom-call(f32[64,32,128]{2,1,0:T(8,128)} %cotangent.1, f32[34,3,64,128]{3,2,1,0:T(8,128)} %get-tuple-element.52.windows_in, ...), custom_call_target="tpu_custom_call" | custom-call | tf_op jit(solution)/shard_map/layer/pallas_call | solution.py:858
  53.7 18.7 %sums.1 = (f32[32,64,128]{2,1,0:T(8,128)}, f32[32,8,128]{2,1,0:T(8,128)}, f32[4,64,128]{2,1,0:T(8,128)}) custom-call(f32[4,64,128]{2,1,0:T(8,128)} %get-tuple-element.61.acc_in, f32[34,3,64,128]{3,2,1,0:T(8,128)} %get-tuple-element.62.placed_in, f32[32,64,128]{2,1,0:T(8,128)} %get-tuple-element.63.recv_in, f32[32,64,128]{2,1,0:T(8,128)} %get-tuple-element.64.part_in, ...), custom_call_target="tpu_custom_call" | custom-call | tf_op jit(solution)/shard_map/sums/pallas_call | solution.py:1210
  73.1 5.2 %final.1 = (f32[64,32,128]{2,1,0:T(8,128)}, f32[64,32,128]{2,1,0:T(8,128)}, f32[64,32,128]{2,1,0:T(8,128)}, f32[1,1]{1,0:T(1,128)}, f32[64,192]{1,0:T(8,128)}, /...) custom-call(f32[1]{0:T(128)S(6)} %copy.40.kl_weight, ...), custom_call_target="tpu_custom_call" | custom-call | tf_op jit(solution)/shard_map/final/pallas_call | solution.py:1344

commit v2 on v1

v2 whole, which is shorter than its diff:
```python
import functools

import jax
import jax.numpy as jnp
from jax import lax
from jax.experimental import pallas as pl
from jax.experimental.pallas import tpu as pltpu
from jax.sharding import PartitionSpec as P

F32 = jnp.float32
BF16 = jnp.bfloat16
MESH = pl.DeviceIdType.MESH
D = 64
LANES = 128
NBR = 6
EPS = 1e-05
HBM = pl.BlockSpec(memory_space=pltpu.HBM)
VMEM = pl.BlockSpec(memory_space=pltpu.VMEM)
ROOM = 62 * 2**20
SMEM = pl.BlockSpec(memory_space=pltpu.SMEM)

WINDOWS = ((-1, -1), (-1, 0), (-1, 1), (0, -1), (0, 1), (1, -1), (1, 0), (1, 1))


def halves(value):
    high = value.astype(BF16)
    return high, (value - high.astype(F32)).astype(BF16)


def weight_pack(weight, *biases):
    high, low = halves(weight)
    if not biases:
        return jnp.concatenate([high, high, low], axis=1)
    place = lax.broadcasted_iota(jnp.int32, (weight.shape[0], 16), 1)
    wide = jnp.zeros((weight.shape[0], 16), F32)
    for i, bias in enumerate(biases):
        for j, part in enumerate(halves(bias)):
            wide = jnp.where(place == 2 * i + j, part.astype(F32), wide)
    return jnp.concatenate([high, high, wide.astype(BF16), low], axis=1)


def mxu(left, right):
    return jnp.dot(left, right, preferred_element_type=F32)


def outer(left, right):
    return lax.dot_general(
        left, right, (((1,), (1,)), ((), ())), preferred_element_type=F32
    )


def exact(left, right, dims):
    return lax.dot_general(
        left,
        right,
        (dims, ((), ())),
        precision=lax.Precision.HIGHEST,
        preferred_element_type=F32,
    )


def eye():
    return lax.broadcasted_iota(jnp.int32, (D, D), 0) == lax.broadcasted_iota(
        jnp.int32, (D, D), 1
    )


def to_column(row):
    return jnp.sum(jnp.where(eye(), row, 0.0), axis=1, keepdims=True)


def to_row(column):
    return jnp.sum(jnp.where(eye(), column, 0.0), axis=0, keepdims=True)


def waits(ref, sem):
    pltpu.make_async_copy(ref, ref, sem).wait()


def in_turn(*routines):
    waiting = list(routines)
    while waiting:
        for routine in list(waiting):
            if next(routine, routine) is routine:
                waiting.remove(routine)


def lane_ids(rows=D):
    return lax.broadcasted_iota(jnp.int32, (rows, LANES), 1)


P_HIDDEN, P_EDGE, P_EDGE_T, P_NODE_OUT = (0, 128), (128, 192), (192, 256), (256, 320)
P_NODE_OUT_T, P_NODE_IN_T, P_SEND_T, P_RECV_T = (320, 384), (384, 576), (576, 640), (640, 704)
P_NODE_IN, P_NODE_IN_END = (704, 768), (768, 832)
P_ROWS, P_LANES = 832, 256
C_GAIN_N, C_SHIFT_N, C_VALID, C_DIVERGED, C_COUNT, C_WEIGHT_N, C_ROWS = range(7)
C_TILES = 7


def packed_rows(ref, rows, lanes=3 * D):
    return ref[rows[0] : rows[1], :lanes]


def neighbours(n_blk, n_lon):
    blk = lax.axis_index("blk")
    lon = lax.axis_index("lon")
    up = lax.rem(blk + n_blk - 1, n_blk)
    down = lax.rem(blk + 1, n_blk)
    west = lax.rem(lon + n_lon - 1, n_lon)
    east = lax.rem(lon + 1, n_lon)
    around = (
        (up, lon),
        (down, lon),
        (blk, west),
        (blk, east),
        (up, west),
        (up, east),
        (down, west),
        (down, east),
    )
    return blk, lon, around


def start_kernel(
    n_blk,
    n_lon,
    counts,
    nodes,
    mean,
    logstd,
    noise,
    neighbors,
    edge_mask,
    w_ei,
    w_eo,
    w_ni,
    w_no,
    *rest,
):
    vectors = rest[:8]
    (
        state_out,
        cols_out,
        project_out,
        receive_out,
        sides_out,
        codes_out,
        valid_out,
        pack_out,
        columns_out,
        buf,
        state,
        projected,
        receiver,
        sides,
        nb,
        mk,
        codes,
        valid,
        v_ei,
        v_eo,
        v_ni,
        v_no,
        v_vec,
        pack,
        columns,
        cols,
        tiles,
        landing,
        in_sem,
        slot_sem,
        weight_sem,
        send_sem,
        recv_sem,
        out_sem,
    ) = rest[8:]
    rows = nodes.shape[1]
    blk, lon, around = neighbours(n_blk, n_lon)
    barrier = pltpu.get_barrier_semaphore()
    for place in around:
        pl.semaphore_signal(barrier, inc=1, device_id=place, device_id_type=MESH)

    n_groups = in_sem.shape[0]
    group = rows // n_groups

    def load_row(g, i):
        r = g * group + i
        for which, source in enumerate((nodes, mean, logstd, noise)):
            pltpu.make_async_copy(source.at[:, r, :], buf.at[r, which], in_sem.at[g]).start()

    for g in range(2):
        for i in range(group):
            load_row(g, i)
    weights = [(w_ei, v_ei), (w_eo, v_eo), (w_ni, v_ni), (w_no, v_no)]
    weights += [(vectors[i], v_vec.at[i]) for i in range(8)]
    lane = lane_ids()
    count = counts[blk]
    inside = lane < count

    def state_row(r, carry):
        total, west_tile, east_tile = carry
        mean_r = buf[r, 1]
        logstd_r = buf[r, 2]
        spread = jnp.exp(logstd_r)
        value = buf[r, 0] + mean_r + spread * buf[r, 3]
        state[r + 1] = value
        total += jnp.where(inside, mean_r * mean_r + spread * spread - 2.0 * logstd_r, 0.0)
        moved = pltpu.roll(value, r + 1, 1)
        west_tile = jnp.where(lane == r + 1, moved, west_tile)
        east_tile = jnp.where(lane == r, moved, east_tile)
        return total, west_tile, east_tile

    carry = (jnp.zeros((D, LANES), F32),) * 3
    for g in range(n_groups):
        if g == 2:
            for source, target in weights:
                pltpu.make_async_copy(source, target, weight_sem).start()
        waits(buf.at[pl.ds(g * group, group)], in_sem.at[g])

        def state_rows(i, carry, g=g):
            for u in range(2):
                if g + 2 < n_groups:
                    load_row(g + 2, 2 * i + u)
                carry = state_row(g * group + 2 * i + u, carry)
            return carry

        carry = lax.fori_loop(0, group // 2, state_rows, carry)
    total, west_tile, east_tile = carry
    tiles[0] = state[1]
    tiles[1] = state[rows]
    tiles[2] = west_tile
    tiles[3] = east_tile

    pl.semaphore_wait(barrier, 8)
    copies = []
    for slot, (place, tile) in enumerate(zip(around, (0, 1, 2, 3, 0, 0, 1, 1))):
        copies.append(
            pltpu.make_async_remote_copy(
                src_ref=tiles.at[tile],
                dst_ref=landing.at[slot],
                send_sem=send_sem.at[slot],
                recv_sem=recv_sem.at[slot],
                device_id=place,
                device_id_type=MESH,
            )
        )
        copies[-1].start()

    pltpu.make_async_copy(neighbors, nb, slot_sem).start()
    pltpu.make_async_copy(edge_mask, mk, slot_sem).start()
    inner = pl.ds(1, rows)
    pltpu.make_async_copy(state.at[inner], state_out.at[inner], out_sem).start()

    for _, target in weights:
        waits(target, weight_sem)
    b_ei, b_eo, gain_e, shift_e, b_ni, b_no, gain_n, shift_n = [
        to_column(v_vec[i]) for i in range(8)
    ]
    n_valid = counts[0]
    for i in range(1, counts.shape[0]):
        n_valid += counts[i]
    for i, column in (
        (C_GAIN_N, gain_n),
        (C_SHIFT_N, shift_n),
        (C_VALID, jnp.where(inside, 1.0, 0.0)),
        (C_COUNT, jnp.full((D, LANES), (D * rows * n_lon * n_valid).astype(F32))),
        (
            C_DIVERGED,
            0.5 * jnp.sum(total - rows * jnp.where(inside, 1.0, 0.0), axis=1, keepdims=True),
        ),
    ):
        columns[i] = jnp.broadcast_to(column, (D, LANES))
    w_in = v_ei[...]
    w_e, w_s, w_r = w_in[:, :D], w_in[:, D : 2 * D], w_in[:, 2 * D :]
    a_state = jnp.concatenate([weight_pack(0.5 * w_s), weight_pack(0.5 * w_r)], axis=0)
    w_o = v_eo[...]
    w_oc = w_o - jnp.mean(w_o, axis=0, keepdims=True)
    b_oc = b_eo - jnp.mean(b_eo, axis=0, keepdims=True)
    back = 0.5 * exact(w_o, w_oc, ((0,), (0,)))
    b_back = 0.5 * exact(w_o, b_oc, ((0,), (0,)))
    w_n = v_ni[...]
    w_nt = w_n.T
    gain_row, shift_row = v_vec[2], v_vec[3]
    one_row = jnp.ones_like(gain_row)
    scale_row = jnp.concatenate([one_row, gain_row], axis=1)
    add_row = jnp.concatenate([0.0 * one_row, shift_row], axis=1)
    columns[C_WEIGHT_N] = w_n
    row_id = lax.broadcasted_iota(jnp.int32, (D, LANES), 0)
    columns[C_ROWS] = jnp.where(row_id == 0, scale_row, jnp.where(row_id == 1, add_row, 0.0))
    w_shift = jnp.sum(w_n * add_row, axis=1, keepdims=True)
    w_out = v_no[...]
    scaled = gain_e * w_nt[D:]
    scaled = scaled - jnp.mean(scaled, axis=0, keepdims=True)

    def put(place, *parts):
        value = jnp.concatenate(parts, axis=0) if len(parts) > 1 else parts[0]
        pack[place[0] : place[1], : value.shape[1]] = value

    put(P_EDGE, weight_pack(0.5 * w_e))
    put(P_HIDDEN, weight_pack(w_oc, b_oc), weight_pack(back, b_back))
    put(P_EDGE_T, weight_pack(w_e.T))
    put(P_SEND_T, weight_pack(w_s.T))
    put(P_RECV_T, weight_pack(w_r.T))
    node_in = weight_pack(0.5 * w_n * scale_row, 0.5 * b_ni, 0.5 * w_shift)
    put(P_NODE_IN, node_in[:, :P_LANES])
    put(P_NODE_IN_END, node_in[:, P_LANES:])
    put(
        P_NODE_OUT,
        weight_pack(
            w_out - jnp.mean(w_out, axis=0, keepdims=True),
            b_no - jnp.mean(b_no, axis=0, keepdims=True),
        ),
    )
    put(P_NODE_OUT_T, weight_pack(0.5 * w_out.T))
    put(
        P_NODE_IN_T,
        weight_pack(w_nt[:D]),
        weight_pack(scaled),
        weight_pack(0.5 * exact(w_o, scaled, ((0,), (0,)))),
    )
    pltpu.make_async_copy(pack, pack_out, out_sem).start()
    pltpu.make_async_copy(columns, columns_out, out_sem).start()

    waits(nb, slot_sem)
    waits(mk, slot_sem)
    before = counts[lax.rem(blk + n_blk - 1, n_blk)]
    after = counts[lax.rem(blk + 1, n_blk)]
    row_id = lax.broadcasted_iota(jnp.int32, (rows, LANES), 0)
    col_id = lax.broadcasted_iota(jnp.int32, (rows, LANES), 1)
    above = jnp.where(row_id == 0, before, count)
    below = jnp.where(row_id == rows - 1, after, count)
    for k in range(NBR):
        delta = nb[k] - (row_id * (LANES + 2) + col_id)
        first = delta < LANES + 2
        middle = delta < 2 * (LANES + 2)
        step = jnp.where(
            first, delta, jnp.where(middle, delta - (LANES + 2), delta - 2 * (LANES + 2))
        )
        codes[k] = jnp.where(first, step, jnp.where(middle, 3 + (step >> 1), 5 + step))
        owner = col_id + step - 1
        owner = jnp.where(owner < 0, LANES - 1, jnp.where(owner >= LANES, 0, owner))
        limit = jnp.where(first, above, jnp.where(middle, count, below))
        valid[k] = jnp.where((col_id < count) & (owner < limit), mk[k].astype(F32), 0.0)
    for k in range(NBR, 8):
        codes[k] = jnp.zeros((rows, LANES), jnp.int32)
        valid[k] = jnp.zeros((rows, LANES), F32)
    for k in range(8):
        pltpu.make_async_copy(codes.at[k], codes_out.at[:, k, :], out_sem).start()
        pltpu.make_async_copy(valid.at[k], valid_out.at[:, k, :], out_sem).start()

    half_bias = 0.5 * b_ei

    def project(i, _):
        high, low = halves(
            jnp.concatenate([state[1 + 4 * i + u] for u in range(4)], axis=1)
        )
        both = mxu(a_state, jnp.concatenate([high, low, high], axis=0))
        for u in range(4):
            s = slice(u * LANES, (u + 1) * LANES)
            projected[1 + 4 * i + u] = both[:D, s]
            receiver[4 * i + u] = both[D:, s] + half_bias

    lax.fori_loop(0, rows // 4, project, None)
    pltpu.make_async_copy(projected.at[inner], project_out.at[inner], out_sem).start()
    pltpu.make_async_copy(receiver, receive_out, out_sem).start()

    for copy in copies:
        copy.wait()
    state[rows + 1] = landing[0]
    state[0] = landing[1]
    corner = lambda slot, at, to: jnp.where(
        lane == to, pltpu.roll(landing[slot], (to - at) % LANES, 1), 0.0
    )
    cols[1] = (
        pltpu.roll(jnp.where((lane >= 1) & (lane <= rows), landing[2], 0.0), LANES - 1, 1)
        + corner(4, 0, rows)
        + corner(6, 0, LANES - 1)
    )
    cols[0] = (
        pltpu.roll(jnp.where(lane < rows, landing[3], 0.0), 1, 1)
        + corner(5, LANES - 1, rows + 1)
        + corner(7, LANES - 1, 0)
    )
    high, low = halves(
        jnp.concatenate([landing[1], landing[0], cols[0], cols[1]], axis=1)
    )
    rim = mxu(a_state[:D], jnp.concatenate([high, low, high], axis=0))
    projected[0] = rim[:, :LANES]
    projected[rows + 1] = rim[:, LANES : 2 * LANES]
    sides[0] = rim[:, 2 * LANES : 3 * LANES]
    sides[1] = rim[:, 3 * LANES :]
    for t in (0, rows + 1):
        pltpu.make_async_copy(projected.at[t], project_out.at[t], out_sem).start()
        pltpu.make_async_copy(state.at[t], state_out.at[t], out_sem).start()
    pltpu.make_async_copy(sides, sides_out, out_sem).start()
    pltpu.make_async_copy(cols, cols_out, out_sem).start()
    for ref in (pack, columns, codes, valid, receiver, state, projected, cols, sides):
        waits(ref, out_sem)


def start_call(n_blk, n_lon, counts, nodes, mean, logstd, noise, neighbors, mask, weights):
    rows = nodes.shape[1]
    tile = (D, LANES)
    shapes = (
        ((rows + 2, *tile), F32),
        ((2, *tile), F32),
        ((rows + 2, *tile), F32),
        ((rows, *tile), F32),
        ((2, *tile), F32),
        ((rows, 8, LANES), jnp.int32),
        ((rows, 8, LANES), F32),
        ((P_ROWS, P_LANES), BF16),
        ((C_TILES, *tile), F32),
    )
    vmem = lambda *dims: pltpu.VMEM(dims, F32)
    ints = lambda *dims: pltpu.VMEM(dims, jnp.int32)
    dma = pltpu.SemaphoreType.DMA
    return pl.pallas_call(
        functools.partial(start_kernel, n_blk, n_lon),
        name="start",
        out_shape=[jax.ShapeDtypeStruct(*shape) for shape in shapes],
        in_specs=[SMEM] + [HBM] * (6 + len(weights)),
        out_specs=[HBM] * len(shapes),
        scratch_shapes=[
            vmem(rows, 4, *tile),
            vmem(rows + 2, *tile),
            vmem(rows + 2, *tile),
            vmem(rows, *tile),
            vmem(2, *tile),
            ints(NBR, rows, LANES),
            ints(NBR, rows, LANES),
            ints(8, rows, LANES),
            vmem(8, rows, LANES),
            vmem(D, 3 * D),
            vmem(D, D),
            vmem(D, 2 * D),
            vmem(D, D),
            vmem(8, 1, D),
            pltpu.VMEM((P_ROWS, P_LANES), BF16),
            vmem(C_TILES, *tile),
            vmem(2, *tile),
            vmem(4, *tile),
            vmem(8, *tile),
            dma((4,)),
            dma,
            dma,
            dma((8,)),
            dma((8,)),
            dma,
        ],
        compiler_params=pltpu.CompilerParams(
            collective_id=0, has_side_effects=True, vmem_limit_bytes=ROOM
        ),
    )(counts, nodes, mean, logstd, noise, neighbors, mask, *weights)


def layer_kernel(
    edges,
    cotangent,
    project_in,
    receive_in,
    sides_in,
    codes_in,
    valid_in,
    pack_in,
    columns_in,
    state_in,
    new_states,
    grad_edges,
    part_out,
    recv_out,
    placed_out,
    acc_out,
    slope,
    xs,
    hs,
    cb,
    db,
    staged,
    windows,
    projected,
    receiver,
    sides,
    codes,
    valid,
    pack,
    columns,
    state,
    inverse,
    summed,
    qc_ref,
    qo_ref,
    cot,
    fresh,
    part,
    placed,
    grad_recv,
    gather_grads,
    acc_edge,
    acc_hidden,
    acc_nin,
    acc_nout,
    acc_vec,
    acc,
    row_sem,
    edge_sem,
    in_sem,
    out_sem,
):
    rows = cotangent.shape[1]
    wide = NBR * LANES
    two = 2 * LANES
    lane = lane_ids()

    halfway = 14
    ahead = 8

    def load_edges(r):
        for k in range(NBR):
            pltpu.make_async_copy(
                edges.at[:, k, r, :],
                staged.at[r, :, pl.ds(k * LANES, LANES)],
                edge_sem.at[r],
            ).start()

    first_weights = pl.ds(P_HIDDEN[0], P_EDGE[1])
    first_small = (
        (sides_in, sides),
        (pack_in.at[first_weights], pack.at[first_weights]),
        (codes_in, codes),
        (valid_in, valid),
    )
    parts = []
    for g, (first, last) in enumerate(((0, halfway), (halfway, rows + 2))):
        send, receive = pl.ds(first, last - first), pl.ds(first, min(last, rows) - first)
        part_g = ((project_in, projected, send), (receive_in, receiver, receive))
        for source, target, span in part_g:
            pltpu.make_async_copy(source.at[span], target.at[span], row_sem.at[g]).start()
        parts.append([target.at[span] for _, target, span in part_g])
        if g == 0:
            for source, target in first_small[:2]:
                pltpu.make_async_copy(source, target, in_sem.at[0]).start()
            for r in range(4):
                load_edges(r)
            for source, target in first_small[2:]:
                pltpu.make_async_copy(source, target, in_sem.at[0]).start()
    for r in range(4, ahead + 2):
        load_edges(r)

    def load_rest():
        rest = pl.ds(P_EDGE[1], P_ROWS - P_EDGE[1])
        pltpu.make_async_copy(pack_in.at[rest], pack.at[rest], in_sem.at[1]).start()
        pltpu.make_async_copy(columns_in, columns, in_sem.at[1]).start()
        pltpu.make_async_copy(state_in, state, in_sem.at[1]).start()

        def load_cot(r, _):
            pltpu.make_async_copy(cotangent.at[:, r, :], cot.at[r], in_sem.at[1]).start()

        lax.fori_loop(0, rows, load_cot, None)
        return (cot, state, columns, pack.at[rest])

    ones16 = jnp.where(
        lax.broadcasted_iota(jnp.int32, (16, wide), 0) < 2, 1.0, 0.0
    ).astype(BF16)
    ones_two = ones16[:, :two]
    for _, target in first_small:
        waits(target, in_sem.at[0])

    def shift(t):
        centre = projected[t]
        mix = pltpu.roll(
            jnp.where(lane == t, sides[0], sides[1]), lax.rem(LANES - t, LANES), 1
        )
        windows[t, 1] = centre
        windows[t, 0] = jnp.where(lane == 0, mix, pltpu.roll(centre, 1, 1))
        windows[t, 2] = jnp.where(lane == LANES - 1, mix, pltpu.roll(centre, LANES - 1, 1))

    def shifts(i, _):
        shift(2 * i)
        shift(2 * i + 1)

    def edge_product(r, pair):
        own = receiver[r]
        s = pl.ds(pair * two, two)
        high, low = halves(staged[r, :, s])
        xs[r, :D, s] = high
        xs[r, D:, s] = low
        out = mxu(packed_rows(pack, P_EDGE), jnp.concatenate([high, low, high], axis=0))
        slope[r, :, s] = out + jnp.concatenate([own, own], axis=1)

    def hidden_values(r, pair):
        slots = (2 * pair, 2 * pair + 1)
        hidden = {k: [None] * 8 for k in slots}
        masks = {}
        for k in slots:
            code = jnp.broadcast_to(codes[r, pl.ds(k, 1), :], (8, LANES))
            masks[k] = ((code & 1) != 0, (code & 2) != 0, (code & 4) != 0)
        for f in range(8):
            rows_f = pl.ds(8 * f, 8)
            w = [windows[r + 1 + dr, 1 + dc, rows_f, :] for dr, dc in WINDOWS]
            for k in slots:
                s = pl.ds(k * LANES, LANES)
                b0, b1, b2 = masks[k]
                low = jnp.where(b1, jnp.where(b0, w[3], w[2]), jnp.where(b0, w[1], w[0]))
                top = jnp.where(b1, jnp.where(b0, w[7], w[6]), jnp.where(b0, w[5], w[4]))
                pre = slope[r, rows_f, s] + jnp.where(b2, top, low)
                t = jnp.tanh(pre)
                u = 1.0 + t
                h = pre * u
                slope[r, rows_f, s] = u + h * (1.0 - t)
                hidden[k][f] = h
        s = pl.ds(pair * two, two)
        high, low = halves(
            jnp.concatenate([jnp.concatenate(hidden[k], axis=0) for k in slots], axis=1)
        )
        hs[r, :D, s] = high
        hs[r, D : 2 * D, s] = low
        hs[r, 2 * D :, s] = ones_two

    def hidden_product(r, pair):
        s = pl.ds(pair * two, two)
        both = mxu(
            packed_rows(pack, P_HIDDEN, 3 * D + 16),
            jnp.concatenate([hs[r, :, s], hs[r, :D, s]], axis=0),
        )
        cb[r, :, s] = both[:D]
        db[r, :, s] = both[D:]
        return r, pair, both[:D]

    def norm(r, pair, pair_c, total):
        for j in range(2):
            k = 2 * pair + j
            c = pair_c[:, j * LANES : (j + 1) * LANES]
            variance = jnp.sum(c * c, axis=0, keepdims=True) * (1.0 / D)
            inv = lax.rsqrt(variance + EPS)
            inverse[r, pl.ds(k, 1), :] = inv
            term = (inv * valid[r, pl.ds(k, 1), :]) * c
            total = term if total is None else total + term
        if pair == NBR // 2 - 1:
            summed[r] = total
            total = None
        return total

    def forward(i, _, first=0, last=2, more=True):
        if first == 0:
            for r in (2 * i, 2 * i + 1):
                if more:
                    load_edges(r + 2 + ahead)
                waits(staged.at[r + 2], edge_sem.at[r + 2])
        units = [(2 * i + u, pair) for u in range(2) for pair in range(NBR // 2)]
        products = []
        total = None
        if last >= 2:
            products.append(hidden_product(units[0][0] - 2, units[0][1]))
        for i_unit, (r, pair) in enumerate(units):
            if last >= 2 and i_unit + 1 < len(units):
                ahead_r, ahead_pair = units[i_unit + 1]
                products.append(hidden_product(ahead_r - 2, ahead_pair))
            if first <= 1 <= last:
                if pair == 0:
                    placed[r + 2] = jnp.zeros((3, D, LANES), F32)
                hidden_values(r, pair)
            if last >= 2:
                total = norm(*products[i_unit], total)
            if first == 0:
                edge_product(r + 2, pair)

    for ref in parts[0]:
        waits(ref, row_sem.at[0])
    lax.fori_loop(0, halfway // 2, shifts, None)
    for r in range(2):
        placed[r] = jnp.zeros((3, D, LANES), F32)
        waits(staged.at[r], edge_sem.at[r])
        for pair in range(NBR // 2):
            edge_product(r, pair)
    forward(0, None, last=1)
    for ref in parts[1]:
        waits(ref, row_sem.at[1])
    lax.fori_loop(halfway // 2, rows // 2 + 1, shifts, None)
    node_inputs = load_rest()
    forward(1, None)
    turns = rows // 2
    full = turns - 1 - ahead // 2
    lax.fori_loop(2, full, forward, None)
    lax.fori_loop(full, turns - 1, functools.partial(forward, more=False), None)
    forward(turns - 1, None, first=1)
    forward(turns, None, first=2)

    for ref in (acc_edge, acc_hidden, acc_nin, acc_nout, acc_vec):
        ref[...] = jnp.zeros_like(ref)
    for ref in node_inputs:
        waits(ref, in_sem.at[1])
    chunk = 4
    span = chunk * LANES

    def node_chunk(first):
        tile_cols = lambda i: jnp.concatenate([columns[i]] * chunk, axis=1)
        spread = lambda ref, offset: jnp.concatenate(
            [ref[first + offset + j] for j in range(chunk)], axis=1
        )
        degree = jnp.concatenate(
            [jnp.sum(valid[first + j], axis=0, keepdims=True) for j in range(chunk)], axis=1
        )
        st_high, st_low = halves(spread(state, 1))
        sum_high, sum_low = halves(spread(summed, 0))
        place = lax.broadcasted_iota(jnp.int32, (16, span), 0)
        extra = jnp.where(place < 2, 1.0, jnp.where(place < 4, degree, 0.0)).astype(BF16)
        tops = jnp.concatenate([st_high, sum_high], axis=0)
        ends = jnp.concatenate([st_low, sum_low], axis=0)
        pre = mxu(
            jnp.concatenate(
                [
                    packed_rows(pack, P_NODE_IN, P_LANES),
                    packed_rows(pack, P_NODE_IN_END, 6 * D + 16 - P_LANES),
                ],
                axis=1,
            ),
            jnp.concatenate([tops, ends, extra, tops], axis=0),
        )
        yield
        t = jnp.tanh(pre)
        u = 1.0 + t
        h = pre * u
        slope_n = u + h * (1.0 - t)
        h_high, h_low = halves(h)
        h_all = jnp.concatenate([h_high, h_low, ones16[:, :span]], axis=0)
        c = mxu(
            packed_rows(pack, P_NODE_OUT, 3 * D + 16),
            jnp.concatenate([h_all, h_high], axis=0),
        )
        yield
        cot_c = spread(cot, 0)
        inv = lax.rsqrt(jnp.sum(c * c, axis=0, keepdims=True) * (1.0 / D) + EPS)
        n = c * inv
        new = spread(state, 1) + (tile_cols(C_GAIN_N) * n + tile_cols(C_SHIFT_N))
        q = cot_c * tile_cols(C_GAIN_N)
        q = q - jnp.sum(q, axis=0, keepdims=True) * (1.0 / D)
        grad = inv * (q - n * (jnp.sum(q * n, axis=0, keepdims=True) * (1.0 / D)))
        g_high, g_low = halves(grad)
        pre_grad = mxu(
            packed_rows(pack, P_NODE_OUT_T), jnp.concatenate([g_high, g_low, g_high], axis=0)
        )
        for j in range(chunk):
            s = slice(j * LANES, (j + 1) * LANES)
            fresh[first + j] = new[:, s]
            acc_vec[0] += cot_c[:, s] * n[:, s]
            acc_vec[1] += cot_c[:, s]
        yield
        acc_nout[...] += outer(jnp.concatenate([g_high, g_low], axis=0), h_all)
        pre_grad = pre_grad * slope_n
        p_high, p_low = halves(pre_grad)
        back = mxu(
            packed_rows(pack, P_NODE_IN_T), jnp.concatenate([p_high, p_low, p_high], axis=0)
        )
        for j in range(chunk):
            s = slice(j * LANES, (j + 1) * LANES)
            acc_vec[2] += pre_grad[:, s]
            acc_vec[3] += pre_grad[:, s] * degree[:, s]
        yield
        acc_nin[...] += outer(
            jnp.concatenate([p_high, p_low], axis=0), jnp.concatenate([tops, ends], axis=0)
        )
        for j in range(chunk):
            s = slice(j * LANES, (j + 1) * LANES)
            part[first + j] = cot[first + j] + back[:D, s]
            qc_ref[first + j] = back[D : 2 * D, s]
            qo_ref[first + j] = back[2 * D :, s]

    in_flight = []
    for first in range(0, rows + 4 * chunk, chunk):
        if first < rows:
            in_flight.append(node_chunk(first))
        for routine in list(in_flight):
            if next(routine, routine) is routine:
                in_flight.remove(routine)

    def send_new(r, _):
        pltpu.make_async_copy(fresh.at[r], new_states.at[:, r, :], out_sem).start()

    lax.fori_loop(0, rows, send_new, None)
    pltpu.make_async_copy(part, part_out, out_sem).start()

    def grad_unit(r, pair, u, received):
        qc = qc_ref[r]
        qo = qo_ref[r]
        hidden_grads, grads = [], []
        for k in (2 * pair, 2 * pair + 1):
            s = pl.ds(k * LANES, LANES)
            c = cb[r, :, s]
            inv = inverse[r, pl.ds(k, 1), :]
            alpha = inv * valid[r, pl.ds(k, 1), :]
            moment = jnp.sum(qc * c, axis=0, keepdims=True) * (1.0 / D)
            beta = alpha * inv * inv * moment
            hidden_grads.append(alpha * qc - beta * c)
            grad = (alpha * qo - beta * db[r, :, s]) * slope[r, :, s]
            grads.append(grad)
            received = grad if received is None else received + grad
        high, low = halves(jnp.concatenate(hidden_grads, axis=1))
        s = pl.ds(pair * two, two)
        gather_grads[u, :D, s] = high
        gather_grads[u, D : 2 * D, s] = low
        high, low = halves(jnp.concatenate(grads, axis=1))
        gather_grads[u, 2 * D : 3 * D, s] = high
        gather_grads[u, 3 * D :, s] = low
        ge = mxu(
            packed_rows(pack, P_EDGE_T), jnp.concatenate([high, low, high], axis=0)
        )
        return grads, received, ge

    def place_unit(r, pair, grads):
        code = [
            jnp.broadcast_to(codes[r, pl.ds(k, 1), :], (8, LANES))
            for k in (2 * pair, 2 * pair + 1)
        ]
        for which, (dr, dc) in enumerate(WINDOWS):
            masks = [c == which for c in code]
            for f in range(8):
                rows_f = pl.ds(8 * f, 8)
                value = placed[r + 1 + dr, 1 + dc, rows_f, :]
                for j in range(2):
                    value += jnp.where(masks[j], grads[j][8 * f : 8 * f + 8], 0.0)
                placed[r + 1 + dr, 1 + dc, rows_f, :] = value

    def store_unit(r, pair, ge):
        staged[r, :, pl.ds(pair * two, two)] = ge

    def products(r, u):
        r = jnp.maximum(r, 0)
        acc_hidden[...] += outer(gather_grads[u, : 2 * D], hs[r])
        acc_edge[...] += outer(gather_grads[u, 2 * D :], xs[r])

    def send_rows(i, unroll=2):
        for u in range(unroll):
            r = unroll * i + u
            pltpu.make_async_copy(grad_recv.at[r], recv_out.at[r], out_sem).start()
            pltpu.make_async_copy(placed.at[r], placed_out.at[r], out_sem).start()
            for k in range(NBR):
                pltpu.make_async_copy(
                    staged.at[r, :, pl.ds(k * LANES, LANES)],
                    grad_edges.at[:, k, r, :],
                    out_sem,
                ).start()

    def backward(i, _, unroll=2):
        if not isinstance(i, int):
            send_rows(i - 1)
        pending = None
        for u in range(unroll):
            r = unroll * i + u
            products(r - unroll, u)
            received = None
            for pair in range(NBR // 2):
                grads, received, ge = grad_unit(r, pair, u, received)
                place_unit(r, pair, grads)
                if pending is not None:
                    store_unit(*pending)
                pending = (r, pair, ge)
            grad_recv[r] = received
        store_unit(*pending)

    gather_grads[...] = jnp.zeros_like(gather_grads)
    backward(0, None)
    lax.fori_loop(1, rows // 2, backward, None)
    products(rows - 2, 0)
    products(rows - 1, 1)
    send_rows(rows // 2 - 1)
    tail = pl.ds(rows, 2)
    pltpu.make_async_copy(placed.at[tail], placed_out.at[tail], out_sem).start()

    def folded(ref):
        half = ref[:D, : 2 * D] + ref[D:, : 2 * D]
        return half + pltpu.roll(half, D, 1)

    left = lane < D
    acc[0] = folded(acc_edge)
    plain = (
        acc_nin[:D, : 2 * D]
        + acc_nin[D:, : 2 * D]
        + acc_nin[:D, 2 * D :]
        + acc_nin[D:, 2 * D :]
    )
    pick = lambda ref, start, i: jnp.sum(
        jnp.where(lane[:, :16] == i, ref[:D, start:] + ref[D:, start:], 0.0),
        axis=1,
        keepdims=True,
    )
    lane_sum = lambda i: jnp.sum(acc_vec[i], axis=1, keepdims=True)
    by_degree = lane_sum(3)
    acc[2] = plain * columns[C_ROWS, 0:1, :] + by_degree * columns[C_ROWS, 1:2, :]
    acc[3] = jnp.where(left, folded(acc_hidden), folded(acc_nout))
    weight_n = columns[C_WEIGHT_N]
    gain_row = jnp.sum(weight_n * plain, axis=0, keepdims=True)[:, D:]
    shift_row = jnp.sum(weight_n * by_degree, axis=0, keepdims=True)[:, D:]
    block = jnp.zeros((D, LANES), F32)
    for i, vector in (
        (1, pick(acc_hidden, 2 * D, 0)),
        (2, to_column(gain_row)),
        (3, to_column(shift_row)),
        (4, lane_sum(2)),
        (5, pick(acc_nout, 2 * D, 0)),
        (6, lane_sum(0)),
        (7, lane_sum(1)),
        (8, columns[C_DIVERGED]),
    ):
        block = jnp.where(lane == D + i, vector, block)
    acc[1] = block
    pltpu.make_async_copy(acc, acc_out, out_sem).start()
    for ref in (fresh, part, grad_recv, placed, staged, acc):
        waits(ref, out_sem)


def layer_call(edges, cotangent, projected, receiver, sides, codes, valid, pack, columns, state):
    rows = cotangent.shape[1]
    wide = NBR * LANES
    tile = (D, LANES)
    shape = lambda *dims: jax.ShapeDtypeStruct(dims, F32)
    vmem = lambda *dims: pltpu.VMEM(dims, F32)
    return pl.pallas_call(
        layer_kernel,
        name="layer",
        out_shape=(
            shape(D, rows, LANES),
            shape(D, NBR, rows, LANES),
            shape(rows, *tile),
            shape(rows, *tile),
            shape(rows + 2, 3, *tile),
            shape(4, *tile),
        ),
        in_specs=[HBM] * 10,
        out_specs=[HBM] * 6,
        scratch_shapes=[
            vmem(rows, D, wide),
            pltpu.VMEM((rows, 2 * D, wide), BF16),
            pltpu.VMEM((rows, 2 * D + 16, wide), BF16),
            vmem(rows, D, wide),
            vmem(rows, D, wide),
            vmem(rows, D, wide),
            vmem(rows + 2, 3, *tile),
            vmem(rows + 2, *tile),
            vmem(rows, *tile),
            vmem(2, *tile),
            pltpu.VMEM((rows, 8, LANES), jnp.int32),
            vmem(rows, 8, LANES),
            pltpu.VMEM((P_ROWS, P_LANES), BF16),
            vmem(C_TILES, *tile),
            vmem(rows + 2, *tile),
            vmem(rows, 8, LANES),
            vmem(rows, *tile),
            vmem(rows, *tile),
            vmem(rows, *tile),
            vmem(rows, *tile),
            vmem(rows, *tile),
            vmem(rows, *tile),
            vmem(rows + 2, 3, *tile),
            vmem(rows, *tile),
            pltpu.VMEM((2, 4 * D, wide), BF16),
            vmem(2 * D, 2 * D),
            vmem(2 * D, 2 * D + 16),
            vmem(2 * D, 4 * D),
            vmem(2 * D, 2 * D + 16),
            vmem(4, *tile),
            vmem(4, *tile),
            pltpu.SemaphoreType.DMA((2,)),
            pltpu.SemaphoreType.DMA((rows,)),
            pltpu.SemaphoreType.DMA((2,)),
            pltpu.SemaphoreType.DMA,
        ],
        compiler_params=pltpu.CompilerParams(vmem_limit_bytes=ROOM),
    )(edges, cotangent, projected, receiver, sides, codes, valid, pack, columns, state)


def sum_kernel(
    n_blk,
    n_lon,
    acc_in,
    placed_in,
    recv_in,
    part_in,
    state_in,
    cols_in,
    pack_in,
    part_out,
    total_out,
    acc,
    placed,
    grad_recv,
    part,
    state,
    cols,
    pack,
    own,
    halo,
    acc_send,
    acc_recv,
    packed,
    scattered,
    across,
    gathered,
    landing,
    halo_in,
    in_sem,
    row_sem,
    rs_send,
    rs_recv,
    x_send,
    x_recv,
    ag_send,
    ag_recv,
    halo_send,
    halo_recv,
    out_sem,
):
    rows = recv_in.shape[0]
    blk, lon, around = neighbours(n_blk, n_lon)
    size = scattered.shape[0]
    n_groups = across.shape[0]
    per = size // n_lon
    me = lax.rem(blk, per) * n_lon + lon
    own_group = blk // per
    lane = lane_ids()

    def member(index):
        return (own_group * per + index // n_lon, lax.rem(index, n_lon))

    def other(step):
        return lax.rem(me + step, size)

    def peer(step):
        return (lax.rem(own_group + step, n_groups) * per + lax.rem(blk, per), lon)

    half = rows // 2
    for h in range(2):
        span = pl.ds(h * half, half)
        span3 = pl.ds(0, half + 1) if h == 0 else pl.ds(half + 1, half + 1)
        for source, target in (
            (placed_in.at[span3], placed.at[span3]),
            (state_in.at[span3], state.at[span3]),
            (recv_in.at[span], grad_recv.at[span]),
        ):
            pltpu.make_async_copy(source, target, row_sem.at[h]).start()
    small = (
        (pack_in.at[pl.ds(P_SEND_T[0], 2 * D)], pack),
        (cols_in, cols),
        (acc_in, acc),
        (part_in, part),
    )
    for i, (source, target) in enumerate(small):
        pltpu.make_async_copy(source, target, in_sem.at[i]).start()

    barrier = pltpu.get_barrier_semaphore()

    def greet(step, _):
        pl.semaphore_signal(
            barrier, inc=1, device_id=member(other(step)), device_id_type=MESH
        )

    lax.fori_loop(1, size, greet, None)
    expected = size - 1
    if n_groups > 1:
        for place in around:
            pl.semaphore_signal(barrier, inc=1, device_id=place, device_id_type=MESH)

        def greet_group(step, _):
            pl.semaphore_signal(barrier, inc=1, device_id=peer(step), device_id_type=MESH)

        lax.fori_loop(1, n_groups, greet_group, None)
        expected += 8 + n_groups - 1

    acc_send[...] = jnp.zeros_like(acc_send)
    acc_recv[...] = jnp.zeros_like(acc_recv)

    def settle(t, cells):
        west_cells, east_cells = cells
        to_west = placed[t, 0]
        to_east = placed[t, 2]
        value = (
            placed[t, 1]
            + jnp.where(lane == 0, 0.0, pltpu.roll(to_east, 1, 1))
            + jnp.where(lane == LANES - 1, 0.0, pltpu.roll(to_west, LANES - 1, 1))
        )
        own[t] = value
        mix = pltpu.roll(jnp.where(lane == 0, to_west, to_east), t, 1)
        west_cells = jnp.where(lane == t, mix, west_cells)
        east_cells = jnp.where(lane == lax.rem(t + LANES - 1, LANES), mix, east_cells)
        return value, (west_cells, east_cells)

    def both_halves(value):
        return jnp.concatenate(halves(value), axis=0)

    ones_row = jnp.where(
        lax.broadcasted_iota(jnp.int32, (16, 4 * LANES), 0) < 1, 1.0, 0.0
    ).astype(BF16)

    def collect(i, cells):
        values, there, received = [], [], []
        for u in range(4):
            t = 1 + 4 * i + u
            value, cells = settle(t, cells)
            values.append(value)
            there.append(state[t])
            received.append(grad_recv[t - 1])
        wide = lambda parts: both_halves(jnp.concatenate(parts, axis=1))
        there = wide(there)
        acc_send[...] += outer(wide(values), there)
        acc_recv[...] += outer(wide(received), jnp.concatenate([there, ones_row], axis=0))
        return cells

    zero = jnp.zeros((D, LANES), F32)
    for h in range(2):
        span = pl.ds(h * half, half)
        waits(placed.at[pl.ds(h * (half + 1), half + 1)], row_sem.at[h])
        waits(state.at[pl.ds(h * (half + 1), half + 1)], row_sem.at[h])
        waits(grad_recv.at[span], row_sem.at[h])
        if h == 0:
            _, cells = settle(0, (zero, zero))
        cells = lax.fori_loop(h * half // 4, (h + 1) * half // 4, collect, cells)
    _, cells = settle(rows + 1, cells)
    waits(cols, in_sem.at[1])
    edge_values = jnp.concatenate([own[0], own[rows + 1], cells[0], cells[1]], axis=1)
    edge_states = jnp.concatenate([state[0], state[rows + 1], cols[0], cols[1]], axis=1)
    acc_send[...] += outer(both_halves(edge_values), both_halves(edge_states))

    def folded(ref):
        part_sum = ref[:D, : 2 * D] + ref[D:, : 2 * D]
        return part_sum + pltpu.roll(part_sum, D, 1)

    left = lane < D
    waits(acc, in_sem.at[2])
    ones_sum = jnp.sum(
        jnp.where(lane[:, :16] == 0, acc_recv[:D, 2 * D :] + acc_recv[D:, 2 * D :], 0.0),
        axis=1,
        keepdims=True,
    )
    chunk = packed.shape[1]
    blocks = (
        jnp.where(left, acc[0], folded(acc_send)),
        jnp.where(left, folded(acc_recv), jnp.where(lane == D, ones_sum, acc[1])),
        acc[2],
        acc[3],
    )
    per_block = D // chunk
    for i, block in enumerate(blocks):
        for j in range(per_block):
            packed[i * per_block + j] = block[j * chunk : (j + 1) * chunk]
    pl.semaphore_wait(barrier, expected)

    def scatter(step, _):
        target = other(step)
        pltpu.make_async_remote_copy(
            src_ref=packed.at[target],
            dst_ref=scattered.at[me],
            send_sem=rs_send,
            recv_sem=rs_recv,
            device_id=member(target),
            device_id_type=MESH,
        ).start()

    lax.fori_loop(1, size, scatter, None)
    scattered[me] = packed[me]

    waits(pack, in_sem.at[0])
    a_send = pack[:D, : 3 * D]
    a_recv = pack[D : 2 * D, : 3 * D]
    high, low = halves(edge_values)
    edge_grads = mxu(a_send, jnp.concatenate([high, low, high], axis=0))
    for i in range(4):
        halo[i] = edge_grads[:, i * LANES : (i + 1) * LANES]
    copies = []
    for slot, (place, source) in enumerate(zip(around, (0, 1, 2, 3, 2, 3, 2, 3))):
        copies.append(
            pltpu.make_async_remote_copy(
                src_ref=halo.at[source],
                dst_ref=landing.at[slot],
                send_sem=halo_send.at[slot],
                recv_sem=halo_recv.at[slot],
                device_id=place,
                device_id_type=MESH,
            )
        )
        copies[-1].start()
    waits(part, in_sem.at[3])

    def finish(i, _):
        for u in range(2):
            first = 4 * i + 2 * u
            grads = None
            for weights, ref, offset in ((a_send, own, 1), (a_recv, grad_recv, 0)):
                high, low = halves(
                    jnp.concatenate([ref[first + offset], ref[first + offset + 1]], axis=1)
                )
                product = mxu(weights, jnp.concatenate([high, low, high], axis=0))
                grads = product if grads is None else grads + product
            for j in range(2):
                part[first + j] += grads[:, j * LANES : (j + 1) * LANES]

    lax.fori_loop(0, rows // 4, finish, None)

    others = pl.ds(0, size - 1)
    waits(scattered.at[others], rs_recv)
    mine = scattered[0]
    for i in range(1, size):
        mine = mine + scattered[i]
    if n_groups > 1:
        across[own_group] = mine

        def cross(step, _):
            pltpu.make_async_remote_copy(
                src_ref=across.at[own_group],
                dst_ref=across.at[own_group],
                send_sem=x_send,
                recv_sem=x_recv,
                device_id=peer(step),
                device_id_type=MESH,
            ).start()

        lax.fori_loop(1, n_groups, cross, None)
        rest = pl.ds(0, n_groups - 1)
        waits(across.at[rest], x_recv)
        waits(across.at[rest], x_send)
        mine = across[0]
        for i in range(1, n_groups):
            mine = mine + across[i]
    gathered[me] = mine

    def gather(step, _):
        pltpu.make_async_remote_copy(
            src_ref=gathered.at[me],
            dst_ref=gathered.at[me],
            send_sem=ag_send,
            recv_sem=ag_recv,
            device_id=member(other(step)),
            device_id_type=MESH,
        ).start()

    lax.fori_loop(1, size, gather, None)
    for copy in copies:
        copy.wait()
    halo_in[0] = landing[1]
    halo_in[1] = landing[0]
    corner = lambda slot, at, to: jnp.where(
        lane == to, pltpu.roll(landing[slot], (to - at) % LANES, 1), 0.0
    )
    halo_in[2] = (
        pltpu.roll(jnp.where(lane < rows, landing[3], 0.0), 1, 1)
        + corner(7, rows, 1)
        + corner(5, LANES - 1, rows)
    )
    east_in = (
        jnp.where((lane >= 1) & (lane <= rows), landing[2], 0.0)
        + corner(6, rows + 1, 1)
        + corner(4, 0, rows)
    )
    west_in = halo_in[2]
    east_in = pltpu.roll(east_in, LANES - 1, 1)
    rim = (lane == 0) | (lane == LANES - 1)
    part[0] += halo_in[0]
    part[rows - 1] += halo_in[1]

    def add_columns(i, _):
        for u in range(4):
            r = 4 * i + u
            mix = pltpu.roll(
                jnp.where(lane == r + 1, west_in, east_in), LANES - 1 - r, 1
            )
            part[r] += jnp.where(rim, mix, 0.0)
        for u in range(4):
            r = 4 * i + u
            pltpu.make_async_copy(part.at[r], part_out.at[:, r, :], out_sem).start()

    lax.fori_loop(0, rows // 4, add_columns, None)
    waits(gathered.at[others], ag_recv)
    pltpu.make_async_copy(gathered, total_out, out_sem).start()
    waits(scattered.at[others], rs_send)
    waits(gathered.at[others], ag_send)
    for ref in (part, gathered):
        waits(ref, out_sem)


def sum_call(n_blk, n_lon, acc, placed, recv, part, state, cols, pack):
    rows = recv.shape[0]
    size = min(32, n_blk * n_lon)
    n_groups = n_blk * n_lon // size
    chunk = (4 * D // size, LANES)
    tile = (D, LANES)
    shape = lambda *dims: jax.ShapeDtypeStruct(dims, F32)
    vmem = lambda *dims: pltpu.VMEM(dims, F32)
    dma = pltpu.SemaphoreType.DMA
    return pl.pallas_call(
        functools.partial(sum_kernel, n_blk, n_lon),
        name="sums",
        out_shape=(shape(D, rows, LANES), shape(size, *chunk)),
        in_specs=[HBM] * 7,
        out_specs=[HBM] * 2,
        scratch_shapes=[
            vmem(4, *tile),
            vmem(rows + 2, 3, *tile),
            vmem(rows, *tile),
            vmem(rows, *tile),
            vmem(rows + 2, *tile),
            vmem(2, *tile),
            pltpu.VMEM((2 * D, P_LANES), BF16),
            vmem(rows + 2, *tile),
            vmem(4, *tile),
            vmem(2 * D, 2 * D),
            vmem(2 * D, 2 * D + 16),
            vmem(size, *chunk),
            vmem(size, *chunk),
            vmem(n_groups, *chunk),
            vmem(size, *chunk),
            vmem(8, *tile),
            vmem(3, *tile),
            dma((4,)),
            dma((2,)),
            dma,
            dma,
            dma,
            dma,
            dma,
            dma,
            dma((8,)),
            dma((8,)),
            dma,
        ],
        compiler_params=pltpu.CompilerParams(
            collective_id=1, has_side_effects=True, vmem_limit_bytes=ROOM
        ),
    )(acc, placed, recv, part, state, cols, pack)


def final_kernel(
    kl_weight,
    part_nodes,
    mean,
    logstd,
    noise,
    total_in,
    columns_in,
    *rest,
):
    grad_nodes, grad_mean, grad_logstd = rest[:3]
    small_outs = rest[3:16]
    grad, mean_v, logstd_v, noise_v, total, columns = rest[16:22]
    smalls = rest[22:35]
    in_sem, small_sem, out_sem = rest[35:]
    n_chunks = in_sem.shape[0]
    depth = D // n_chunks
    for i, (source, target) in enumerate(((columns_in, columns), (total_in, total))):
        pltpu.make_async_copy(source, target, small_sem.at[i]).start()
    spans = [pl.ds(i * depth, depth) for i in range(n_chunks)]
    pairs = ((part_nodes, grad), (mean, mean_v), (logstd, logstd_v), (noise, noise_v))
    for i, span in enumerate(spans):
        for source, target in pairs:
            pltpu.make_async_copy(source.at[span], target.at[span], in_sem.at[i]).start()

    waits(columns, small_sem.at[0])
    waits(total, small_sem.at[1])
    kl_value, g_w_ei, g_w_eo, g_w_ni, g_w_no = smalls[:5]
    chunk = total.shape[1]
    per_block = D // chunk
    blocks = [
        jnp.concatenate([total[i * per_block + j] for j in range(per_block)], axis=0)
        for i in range(4)
    ]
    g_w_ei[:, : 2 * D] = blocks[0]
    g_w_ei[:, 2 * D :] = blocks[1][:, :D]
    g_w_ni[...] = blocks[2]
    g_w_eo[...] = blocks[3][:, :D]
    g_w_no[...] = pltpu.roll(blocks[3], D, 1)[:, :D]
    for i in range(8):
        smalls[5 + i][...] = to_row(blocks[1][:, D + i : D + i + 1])
    diverged = jnp.sum(blocks[1][:, D + 8 : D + 9], axis=0, keepdims=True)
    kl_value[...] = diverged / columns[C_COUNT, 0:1, 0:1]
    for source, target in zip(smalls, small_outs):
        pltpu.make_async_copy(source, target, out_sem).start()

    inside = (kl_weight[0] * columns[C_VALID, 0:1, :]).reshape(1, 1, LANES)
    for i, span in enumerate(spans):
        for _, target in pairs:
            waits(target.at[span], in_sem.at[i])
        pltpu.make_async_copy(grad.at[span], grad_nodes.at[span], out_sem).start()
        for f in range(i * depth, (i + 1) * depth):
            one = pl.ds(f, 1)
            g = grad[one]
            spread = jnp.exp(logstd_v[one])
            mean_v[one] = g + inside * mean_v[one]
            logstd_v[one] = g * spread * noise_v[one] + inside * (spread * spread - 1.0)
        pltpu.make_async_copy(mean_v.at[span], grad_mean.at[span], out_sem).start()
        pltpu.make_async_copy(logstd_v.at[span], grad_logstd.at[span], out_sem).start()
    for ref in (grad, mean_v, logstd_v, *smalls):
        waits(ref, out_sem)


def final_call(kl_weight, part_nodes, mean, logstd, noise, total, columns):
    shape = lambda *dims: jax.ShapeDtypeStruct(dims, F32)
    vmem = lambda *dims: pltpu.VMEM(dims, F32)
    whole = mean.shape
    small = ((1, 1), (D, 3 * D), (D, D), (D, 2 * D), (D, D)) + ((1, D),) * 8
    return pl.pallas_call(
        final_kernel,
        name="final",
        out_shape=[shape(*dims) for dims in (whole,) * 3 + small],
        in_specs=[SMEM] + [HBM] * 6,
        out_specs=[HBM] * 16,
        scratch_shapes=[vmem(*whole) for _ in range(4)]
        + [vmem(*total.shape), vmem(C_TILES, D, LANES)]
        + [vmem(*dims) for dims in small]
        + [
            pltpu.SemaphoreType.DMA((8,)),
            pltpu.SemaphoreType.DMA((2,)),
            pltpu.SemaphoreType.DMA,
        ],
        compiler_params=pltpu.CompilerParams(vmem_limit_bytes=ROOM),
    )(kl_weight, part_nodes, mean, logstd, noise, total, columns)


def shards(
    nodes,
    edges,
    latent_mean,
    latent_logstd,
    latent_noise,
    kl_weight,
    band_counts,
    neighbors,
    edge_mask,
    w_edge_in,
    b_edge_in,
    w_edge_out,
    b_edge_out,
    edge_gain,
    edge_shift,
    w_node_in,
    b_node_in,
    w_node_out,
    b_node_out,
    node_gain,
    node_shift,
    cotangent,
):
    n_blk = lax.axis_size("blk")
    n_lon = lax.axis_size("lon")
    vectors = (
        b_edge_in,
        b_edge_out,
        edge_gain,
        edge_shift,
        b_node_in,
        b_node_out,
        node_gain,
        node_shift,
    )
    weights = (w_edge_in, w_edge_out, w_node_in, w_node_out)
    weights += tuple(vector.reshape(1, D) for vector in vectors)
    state, cols, projected, receiver, sides, codes, valid, pack, columns = start_call(
        n_blk,
        n_lon,
        band_counts,
        nodes,
        latent_mean,
        latent_logstd,
        latent_noise,
        neighbors,
        edge_mask,
        weights,
    )
    new_states, grad_edges, part, recv, placed, acc = layer_call(
        edges, cotangent, projected, receiver, sides, codes, valid, pack, columns, state
    )
    part, total = sum_call(n_blk, n_lon, acc, placed, recv, part, state, cols, pack)
    grad_nodes, grad_mean, grad_logstd, kl_value, g_w_ei, g_w_eo, g_w_ni, g_w_no, *g_vec = (
        final_call(
            kl_weight,
            part,
            latent_mean,
            latent_logstd,
            latent_noise,
            total,
            columns,
        )
    )
    g_vec = [vector.reshape(D) for vector in g_vec]
    return (
        new_states,
        kl_value.reshape(1),
        grad_nodes,
        grad_edges,
        grad_mean,
        grad_logstd,
        g_w_ei,
        g_vec[0],
        g_w_eo,
        g_vec[1],
        g_vec[2],
        g_vec[3],
        g_w_ni,
        g_vec[4],
        g_w_no,
        g_vec[5],
        g_vec[6],
        g_vec[7],
    )


def solution(mesh):
    node = P(None, "blk", "lon")
    slot = P(None, None, "blk", "lon")
    return jax.shard_map(
        shards,
        mesh=mesh,
        in_specs=(
            (node, slot, node, node, node, P(), P(), node, node) + (P(),) * 12 + (node,)
        ),
        out_specs=(node, P(), node, slot, node, node) + (P(),) * 12,
        check_vma=False,
    )
```

time: 78.5 us -> 70.8 us (0.902)
  Pallas kernels: 77 us -> 69.1 us
    pallas_call x1, Pallas kernels: 24.4 us -> 14.3 us  [start_call(): pl.pallas_call(functools.partial(start_kernel, n_blk, n_lon), name='start...]
    pallas_call x1, Pallas kernels: 28.7 us -> 31.8 us  [layer_call(): pl.pallas_call(layer_kernel, name='layer', out_shape=(shape(D, rows, LANE...]
    pallas_call x1, Pallas kernels: 5.16 us -> 4.31 us  [final_call(): pl.pallas_call(final_kernel, name='final', out_shape=[shape(*dims) for di...]
where the time goes in v2:
time: 70.8 us; the launch traced here: 70.4 us
  Pallas kernels  69.1 us (98%)
  between operations  1.33 us (2%)
    pallas_call x1, Pallas kernels, layer_call(): pl.pallas_call(layer_kernel, name='layer', out_shape=(shape(D, rows, LANE...  31.8 us
    pallas_call x1, Pallas kernels, sum_call(): pl.pallas_call(functools.partial(sum_kernel, n_blk, n_lon), name='sums',...  18.7 us
    pallas_call x1, Pallas kernels, start_call(): pl.pallas_call(functools.partial(start_kernel, n_blk, n_lon), name='start...  14.3 us
    pallas_call x1, Pallas kernels, final_call(): pl.pallas_call(final_kernel, name='final', out_shape=[shape(*dims) for di...  4.31 us

profile of v2, /device:TPU:0, one launch (start us, length us, event | category | flops | bytes accessed | tf_op | source)
XLA Modules:
  0.0 70.4 jit_solution(2316396064686568267)
XLA Ops:
  0.7 14.3 %start.1 = (f32[34,64,128]{2,1,0:T(8,128)}, f32[2,64,128]{2,1,0:T(8,128)}, f32[34,64,128]{2,1,0:T(8,128)}, f32[32,64,128]{2,1,0:T(8,128)}, f32[2,64,128]{2,1,0:T...) custom-call(s32[8]{0:T(128)} %counts.1, ...), custom_call_target="tpu_custom_call" | custom-call | tf_op jit(solution)/shard_map/start/pallas_call | solution.py:418
  15.0 31.8 %layer.1 = (f32[64,32,128]{2,1,0:T(8,128)}, f32[64,6,32,128]{3,2,1,0:T(8,128)}, f32[32,64,128]{2,1,0:T(8,128)}, f32[32,64,128]{2,1,0:T(8,128)}, f32[34,3,64,128]{3,2,1,0:T(8,128)}, /*index=5*/f32[4,64,128]{2,1,0:T(8,128)}) custom-call(f32[64,6,32,128]{3,2,1,0:T(8,128)} %edges.1, f32[64,32,128]{2,1,0:T(8,128)} %cotangent.1, ...), custom_call_target="tpu_custom_call" | custom-call | tf_op jit(solution)/shard_map/layer/pallas_call | solution.py:918
  46.7 18.7 %sums.1 = (f32[64,32,128]{2,1,0:T(8,128)}, f32[32,8,128]{2,1,0:T(8,128)}) custom-call(f32[4,64,128]{2,1,0:T(8,128)} %get-tuple-element.60.acc_in, f32[34,3,64,128]{3,2,1,0:T(8,128)} %get-tuple-element.61.placed_in, f32[32,64,128]{2,1,0:T(8,128)} %get-tuple-element.62.recv_in, f32[32,64,128]{2,1,0:T(8,128)} %get-tuple-element.63.part_in, ...), custom_call_target="tpu_custom_call" | custom-call | tf_op jit(solution)/shard_map/sums/pallas_call | solution.py:1288
  66.1 4.3 %final.1 = (f32[64,32,128]{2,1,0:T(8,128)}, f32[64,32,128]{2,1,0:T(8,128)}, f32[64,32,128]{2,1,0:T(8,128)}, f32[1,1]{1,0:T(1,128)}, f32[64,192]{1,0:T(8,128)}, /...) custom-call(f32[1]{0:T(128)S(6)} %copy.40.kl_weight, ...), custom_call_target="tpu_custom_call" | custom-call | tf_op jit(solution)/shard_map/final/pallas_call | solution.py:1398

commit v3 on v2

--- a/solution.py
+++ b/solution.py
@@ -99,6 +99,56 @@
 
 def packed_rows(ref, rows, lanes=3 * D):
     return ref[rows[0] : rows[1], :lanes]
+
+
+def row_of(ref, row, step, count=D):
+    flat = ref.reshape(count * step, LANES)
+    return flat, pl.ds(row, count, stride=step)
+
+
+def read_row(ref, row, step=8):
+    flat, place = row_of(ref, row, step)
+    return flat[place, :]
+
+
+def write_row(ref, row, value, step=8):
+    flat, place = row_of(ref, row, step)
+    flat[place, :] = value
+
+
+def pack_column(tile):
+    return jnp.where(lane_ids(D // 2) < D, tile[: D // 2], pltpu.roll(tile[D // 2 :], D, 1))
+
+
+def unpack_column(tile):
+    return jnp.concatenate([tile, pltpu.roll(tile, D, 1)], axis=0)
+
+
+def corner_rows(columns):
+    rows = [to_row(column) for column in columns]
+    wide = jnp.concatenate(rows + [jnp.zeros((4, D), F32)], axis=0)
+    return jnp.concatenate([wide, jnp.zeros((8, D), F32)], axis=1)
+
+
+def corner_at(ref, row, lane):
+    return jnp.where(lane_ids() == lane, to_column(ref[row : row + 1, :D]), 0.0)
+
+
+def rim_copies(around, rows, columns, corners, rows_in, columns_in, corners_in, send, recv):
+    pairs = [(rows.at[0], rows_in.at[0]), (rows.at[1], rows_in.at[1])]
+    pairs += [(columns.at[0], columns_in.at[0]), (columns.at[1], columns_in.at[1])]
+    pairs += [(corners, corners_in.at[i]) for i in range(4)]
+    return [
+        pltpu.make_async_remote_copy(
+            src_ref=source,
+            dst_ref=target,
+            send_sem=send.at[slot],
+            recv_sem=recv.at[slot],
+            device_id=place,
+            device_id_type=MESH,
+        )
+        for slot, (place, (source, target)) in enumerate(zip(around, pairs))
+    ]
 
 
 def neighbours(n_blk, n_lon):
@@ -125,6 +175,7 @@
     n_blk,
     n_lon,
     counts,
+    kl_weight,
     nodes,
     mean,
     logstd,
@@ -165,8 +216,12 @@
         pack,
         columns,
         cols,
-        tiles,
-        landing,
+        edge_rows,
+        edge_cols,
+        edge_corners,
+        rows_in,
+        cols_in,
+        corners_in,
         in_sem,
         slot_sem,
         weight_sem,
@@ -182,27 +237,25 @@
 
     n_groups = in_sem.shape[0]
     group = rows // n_groups
-
-    def load_row(g, i):
-        r = g * group + i
+    for g in range(n_groups):
         for which, source in enumerate((nodes, mean, logstd, noise)):
-            pltpu.make_async_copy(source.at[:, r, :], buf.at[r, which], in_sem.at[g]).start()
-
-    for g in range(2):
-        for i in range(group):
-            load_row(g, i)
+            pltpu.make_async_copy(
+                source.at[:, pl.ds(g * group, group), :], buf.at[g, which], in_sem.at[g]
+            ).start()
     weights = [(w_ei, v_ei), (w_eo, v_eo), (w_ni, v_ni), (w_no, v_no)]
     weights += [(vectors[i], v_vec.at[i]) for i in range(8)]
     lane = lane_ids()
     count = counts[blk]
     inside = lane < count
 
-    def state_row(r, carry):
+    def state_row(g, j, carry):
         total, west_tile, east_tile = carry
-        mean_r = buf[r, 1]
-        logstd_r = buf[r, 2]
+        r = g * group + j
+        node_r, mean_r, logstd_r, noise_r = [
+            read_row(buf.at[g, which], j, group) for which in range(4)
+        ]
         spread = jnp.exp(logstd_r)
-        value = buf[r, 0] + mean_r + spread * buf[r, 3]
+        value = node_r + mean_r + spread * noise_r
         state[r + 1] = value
         total += jnp.where(inside, mean_r * mean_r + spread * spread - 2.0 * logstd_r, 0.0)
         moved = pltpu.roll(value, r + 1, 1)
@@ -211,41 +264,43 @@
         return total, west_tile, east_tile
 
     carry = (jnp.zeros((D, LANES), F32),) * 3
-    for g in range(n_groups):
-        if g == 2:
-            for source, target in weights:
-                pltpu.make_async_copy(source, target, weight_sem).start()
-        waits(buf.at[pl.ds(g * group, group)], in_sem.at[g])
-
-        def state_rows(i, carry, g=g):
-            for u in range(2):
-                if g + 2 < n_groups:
-                    load_row(g + 2, 2 * i + u)
-                carry = state_row(g * group + 2 * i + u, carry)
-            return carry
-
-        carry = lax.fori_loop(0, group // 2, state_rows, carry)
+    for source, target in weights:
+        pltpu.make_async_copy(source, target, weight_sem).start()
+
+    def state_group(g, carry):
+        waits(buf.at[g], in_sem.at[g])
+        for j in range(0, group, 2):
+            carry = state_row(g, j + 1, state_row(g, j, carry))
+        return carry
+
+    carry = lax.fori_loop(0, n_groups, state_group, carry)
     total, west_tile, east_tile = carry
-    tiles[0] = state[1]
-    tiles[1] = state[rows]
-    tiles[2] = west_tile
-    tiles[3] = east_tile
+    edge_rows[0] = state[1]
+    edge_rows[1] = state[rows]
+    edge_cols[0] = pack_column(west_tile)
+    edge_cols[1] = pack_column(east_tile)
+    edge_corners[...] = corner_rows(
+        [
+            state[row][:, lane0 : lane0 + 1]
+            for row in (1, rows)
+            for lane0 in (0, LANES - 1)
+        ]
+    )
 
     pl.semaphore_wait(barrier, 8)
-    copies = []
-    for slot, (place, tile) in enumerate(zip(around, (0, 1, 2, 3, 0, 0, 1, 1))):
-        copies.append(
-            pltpu.make_async_remote_copy(
-                src_ref=tiles.at[tile],
-                dst_ref=landing.at[slot],
-                send_sem=send_sem.at[slot],
-                recv_sem=recv_sem.at[slot],
-                device_id=place,
-                device_id_type=MESH,
-            )
-        )
-        copies[-1].start()
-
+    copies = rim_copies(
+        around,
+        edge_rows,
+        edge_cols,
+        edge_corners,
+        rows_in,
+        cols_in,
+        corners_in,
+        send_sem,
+        recv_sem,
+    )
+    for copy in copies:
+        copy.start()
     pltpu.make_async_copy(neighbors, nb, slot_sem).start()
     pltpu.make_async_copy(edge_mask, mk, slot_sem).start()
     inner = pl.ds(1, rows)
@@ -262,7 +317,7 @@
     for i, column in (
         (C_GAIN_N, gain_n),
         (C_SHIFT_N, shift_n),
-        (C_VALID, jnp.where(inside, 1.0, 0.0)),
+        (C_VALID, jnp.where(inside, kl_weight[0], 0.0)),
         (C_COUNT, jnp.full((D, LANES), (D * rows * n_lon * n_valid).astype(F32))),
         (
             C_DIVERGED,
@@ -366,23 +421,22 @@
 
     for copy in copies:
         copy.wait()
-    state[rows + 1] = landing[0]
-    state[0] = landing[1]
-    corner = lambda slot, at, to: jnp.where(
-        lane == to, pltpu.roll(landing[slot], (to - at) % LANES, 1), 0.0
-    )
+    state[rows + 1] = rows_in[0]
+    state[0] = rows_in[1]
+    from_east = unpack_column(cols_in[0])
+    from_west = unpack_column(cols_in[1])
     cols[1] = (
-        pltpu.roll(jnp.where((lane >= 1) & (lane <= rows), landing[2], 0.0), LANES - 1, 1)
-        + corner(4, 0, rows)
-        + corner(6, 0, LANES - 1)
+        pltpu.roll(jnp.where((lane >= 1) & (lane <= rows), from_east, 0.0), LANES - 1, 1)
+        + corner_at(corners_in.at[0], 0, rows)
+        + corner_at(corners_in.at[2], 2, LANES - 1)
     )
     cols[0] = (
-        pltpu.roll(jnp.where(lane < rows, landing[3], 0.0), 1, 1)
-        + corner(5, LANES - 1, rows + 1)
-        + corner(7, LANES - 1, 0)
+        pltpu.roll(jnp.where(lane < rows, from_west, 0.0), 1, 1)
+        + corner_at(corners_in.at[1], 1, rows + 1)
+        + corner_at(corners_in.at[3], 3, 0)
     )
     high, low = halves(
-        jnp.concatenate([landing[1], landing[0], cols[0], cols[1]], axis=1)
+        jnp.concatenate([rows_in[1], rows_in[0], cols[0], cols[1]], axis=1)
     )
     rim = mxu(a_state[:D], jnp.concatenate([high, low, high], axis=0))
     projected[0] = rim[:, :LANES]
@@ -398,7 +452,7 @@
         waits(ref, out_sem)
 
 
-def start_call(n_blk, n_lon, counts, nodes, mean, logstd, noise, neighbors, mask, weights):
+def start_call(n_blk, n_lon, counts, kl_weight, nodes, mean, logstd, noise, neighbors, mask, weights):
     rows = nodes.shape[1]
     tile = (D, LANES)
     shapes = (
@@ -419,10 +473,10 @@
         functools.partial(start_kernel, n_blk, n_lon),
         name="start",
         out_shape=[jax.ShapeDtypeStruct(*shape) for shape in shapes],
-        in_specs=[SMEM] + [HBM] * (6 + len(weights)),
+        in_specs=[SMEM, SMEM] + [HBM] * (6 + len(weights)),
         out_specs=[HBM] * len(shapes),
         scratch_shapes=[
-            vmem(rows, 4, *tile),
+            vmem(rows // 8, 4, D, 8, LANES),
             vmem(rows + 2, *tile),
             vmem(rows + 2, *tile),
             vmem(rows, *tile),
@@ -439,9 +493,13 @@
             pltpu.VMEM((P_ROWS, P_LANES), BF16),
             vmem(C_TILES, *tile),
             vmem(2, *tile),
-            vmem(4, *tile),
-            vmem(8, *tile),
-            dma((4,)),
+            vmem(2, *tile),
+            vmem(2, D // 2, LANES),
+            vmem(8, LANES),
+            vmem(2, *tile),
+            vmem(2, D // 2, LANES),
+            vmem(4, 8, LANES),
+            dma((rows // 8,)),
             dma,
             dma,
             dma((8,)),
@@ -451,7 +509,7 @@
         compiler_params=pltpu.CompilerParams(
             collective_id=0, has_side_effects=True, vmem_limit_bytes=ROOM
         ),
-    )(counts, nodes, mean, logstd, noise, neighbors, mask, *weights)
+    )(counts, kl_weight, nodes, mean, logstd, noise, neighbors, mask, *weights)
 
 
 def layer_kernel(
@@ -469,7 +527,8 @@
     grad_edges,
     part_out,
     recv_out,
-    placed_out,
+    own_out,
+    cells_out,
     acc_out,
     slope,
     xs,
@@ -494,6 +553,7 @@
     fresh,
     part,
     placed,
+    cells,
     grad_recv,
     gather_grads,
     acc_edge,
@@ -544,7 +604,7 @@
                 load_edges(r)
             for source, target in first_small[2:]:
                 pltpu.make_async_copy(source, target, in_sem.at[0]).start()
-    for r in range(4, ahead + 2):
+    for r in range(4, ahead + 4):
         load_edges(r)
 
     def load_rest():
@@ -553,10 +613,10 @@
         pltpu.make_async_copy(columns_in, columns, in_sem.at[1]).start()
         pltpu.make_async_copy(state_in, state, in_sem.at[1]).start()
 
-        def load_cot(r, _):
-            pltpu.make_async_copy(cotangent.at[:, r, :], cot.at[r], in_sem.at[1]).start()
-
-        lax.fori_loop(0, rows, load_cot, None)
+        for g in range(rows // 8):
+            pltpu.make_async_copy(
+                cotangent.at[:, pl.ds(8 * g, 8), :], cot.at[g], in_sem.at[1]
+            ).start()
         return (cot, state, columns, pack.at[rest])
 
     ones16 = jnp.where(
@@ -574,10 +634,6 @@
         windows[t, 1] = centre
         windows[t, 0] = jnp.where(lane == 0, mix, pltpu.roll(centre, 1, 1))
         windows[t, 2] = jnp.where(lane == LANES - 1, mix, pltpu.roll(centre, LANES - 1, 1))
-
-    def shifts(i, _):
-        shift(2 * i)
-        shift(2 * i + 1)
 
     def edge_product(r, pair):
         own = receiver[r]
@@ -642,20 +698,23 @@
         return total
 
     def forward(i, _, first=0, last=2, more=True):
+        turn = [4 * i + u for u in range(4)]
         if first == 0:
-            for r in (2 * i, 2 * i + 1):
+            for r in turn:
                 if more:
-                    load_edges(r + 2 + ahead)
-                waits(staged.at[r + 2], edge_sem.at[r + 2])
-        units = [(2 * i + u, pair) for u in range(2) for pair in range(NBR // 2)]
+                    load_edges(r + 4 + ahead)
+                waits(staged.at[r + 4], edge_sem.at[r + 4])
+            for r in turn:
+                shift(r + 6)
+        units = [(r, pair) for r in turn for pair in range(NBR // 2)]
         products = []
         total = None
         if last >= 2:
-            products.append(hidden_product(units[0][0] - 2, units[0][1]))
+            products.append(hidden_product(units[0][0] - 4, units[0][1]))
         for i_unit, (r, pair) in enumerate(units):
             if last >= 2 and i_unit + 1 < len(units):
                 ahead_r, ahead_pair = units[i_unit + 1]
-                products.append(hidden_product(ahead_r - 2, ahead_pair))
+                products.append(hidden_product(ahead_r - 4, ahead_pair))
             if first <= 1 <= last:
                 if pair == 0:
                     placed[r + 2] = jnp.zeros((3, D, LANES), F32)
@@ -663,25 +722,25 @@
             if last >= 2:
                 total = norm(*products[i_unit], total)
             if first == 0:
-                edge_product(r + 2, pair)
+                edge_product(r + 4, pair)
 
     for ref in parts[0]:
         waits(ref, row_sem.at[0])
-    lax.fori_loop(0, halfway // 2, shifts, None)
+    for t in range(6):
+        shift(t)
     for r in range(2):
         placed[r] = jnp.zeros((3, D, LANES), F32)
+    for r in range(4):
         waits(staged.at[r], edge_sem.at[r])
         for pair in range(NBR // 2):
             edge_product(r, pair)
-    forward(0, None, last=1)
     for ref in parts[1]:
         waits(ref, row_sem.at[1])
-    lax.fori_loop(halfway // 2, rows // 2 + 1, shifts, None)
     node_inputs = load_rest()
-    forward(1, None)
-    turns = rows // 2
-    full = turns - 1 - ahead // 2
-    lax.fori_loop(2, full, forward, None)
+    forward(0, None, last=1)
+    turns = rows // 4
+    full = turns - 1 - ahead // 4
+    lax.fori_loop(1, full, forward, None)
     lax.fori_loop(full, turns - 1, functools.partial(forward, more=False), None)
     forward(turns - 1, None, first=1)
     forward(turns, None, first=2)
@@ -729,7 +788,9 @@
             jnp.concatenate([h_all, h_high], axis=0),
         )
         yield
-        cot_c = spread(cot, 0)
+        cot_c = jnp.concatenate(
+            [read_row(cot.at[(first + j) // 8], (first + j) % 8) for j in range(chunk)], axis=1
+        )
         inv = lax.rsqrt(jnp.sum(c * c, axis=0, keepdims=True) * (1.0 / D) + EPS)
         n = c * inv
         new = spread(state, 1) + (tile_cols(C_GAIN_N) * n + tile_cols(C_SHIFT_N))
@@ -742,7 +803,7 @@
         )
         for j in range(chunk):
             s = slice(j * LANES, (j + 1) * LANES)
-            fresh[first + j] = new[:, s]
+            write_row(fresh.at[(first + j) // 8], (first + j) % 8, new[:, s])
             acc_vec[0] += cot_c[:, s] * n[:, s]
             acc_vec[1] += cot_c[:, s]
         yield
@@ -762,7 +823,7 @@
         )
         for j in range(chunk):
             s = slice(j * LANES, (j + 1) * LANES)
-            part[first + j] = cot[first + j] + back[:D, s]
+            part[first + j] = cot_c[:, s] + back[:D, s]
             qc_ref[first + j] = back[D : 2 * D, s]
             qo_ref[first + j] = back[2 * D :, s]
 
@@ -774,10 +835,10 @@
             if next(routine, routine) is routine:
                 in_flight.remove(routine)
 
-    def send_new(r, _):
-        pltpu.make_async_copy(fresh.at[r], new_states.at[:, r, :], out_sem).start()
-
-    lax.fori_loop(0, rows, send_new, None)
+    for g in range(rows // 8):
+        pltpu.make_async_copy(
+            fresh.at[g], new_states.at[:, pl.ds(8 * g, 8), :], out_sem
+        ).start()
     pltpu.make_async_copy(part, part_out, out_sem).start()
 
     def grad_unit(r, pair, u, received):
@@ -829,11 +890,25 @@
         acc_hidden[...] += outer(gather_grads[u, : 2 * D], hs[r])
         acc_edge[...] += outer(gather_grads[u, 2 * D :], xs[r])
 
-    def send_rows(i, unroll=2):
+    own = projected
+
+    def settle(t):
+        to_west = placed[t, 0]
+        to_east = placed[t, 2]
+        own[t] = (
+            placed[t, 1]
+            + jnp.where(lane == 0, 0.0, pltpu.roll(to_east, 1, 1))
+            + jnp.where(lane == LANES - 1, 0.0, pltpu.roll(to_west, LANES - 1, 1))
+        )
+        mix = pltpu.roll(jnp.where(lane == 0, to_west, to_east), t, 1)
+        cells[0] = jnp.where(lane == t, mix, cells[0])
+        cells[1] = jnp.where(lane == lax.rem(t + LANES - 1, LANES), mix, cells[1])
+
+    def send_rows(i, unroll=4):
+        span = pl.ds(unroll * i, unroll)
+        pltpu.make_async_copy(grad_recv.at[span], recv_out.at[span], out_sem).start()
         for u in range(unroll):
             r = unroll * i + u
-            pltpu.make_async_copy(grad_recv.at[r], recv_out.at[r], out_sem).start()
-            pltpu.make_async_copy(placed.at[r], placed_out.at[r], out_sem).start()
             for k in range(NBR):
                 pltpu.make_async_copy(
                     staged.at[r, :, pl.ds(k * LANES, LANES)],
@@ -841,9 +916,11 @@
                     out_sem,
                 ).start()
 
-    def backward(i, _, unroll=2):
+    def backward(i, _, unroll=4):
         if not isinstance(i, int):
             send_rows(i - 1)
+            for u in range(unroll):
+                settle(unroll * (i - 1) + u)
         pending = None
         for u in range(unroll):
             r = unroll * i + u
@@ -857,15 +934,22 @@
                 pending = (r, pair, ge)
             grad_recv[r] = received
         store_unit(*pending)
-
+        if not isinstance(i, int):
+            span = pl.ds(unroll * (i - 1), unroll)
+            pltpu.make_async_copy(own.at[span], own_out.at[span], out_sem).start()
+
+    cells[...] = jnp.zeros_like(cells)
     gather_grads[...] = jnp.zeros_like(gather_grads)
     backward(0, None)
-    lax.fori_loop(1, rows // 2, backward, None)
-    products(rows - 2, 0)
-    products(rows - 1, 1)
-    send_rows(rows // 2 - 1)
-    tail = pl.ds(rows, 2)
-    pltpu.make_async_copy(placed.at[tail], placed_out.at[tail], out_sem).start()
+    lax.fori_loop(1, rows // 4, backward, None)
+    send_rows(rows // 4 - 1)
+    for t in range(rows - 4, rows + 2):
+        settle(t)
+    tail = pl.ds(rows - 4, 6)
+    pltpu.make_async_copy(own.at[tail], own_out.at[tail], out_sem).start()
+    pltpu.make_async_copy(cells, cells_out, out_sem).start()
+    for u in range(4):
+        products(rows - 4 + u, u)
 
     def folded(ref):
         half = ref[:D, : 2 * D] + ref[D:, : 2 * D]
@@ -905,7 +989,7 @@
         block = jnp.where(lane == D + i, vector, block)
     acc[1] = block
     pltpu.make_async_copy(acc, acc_out, out_sem).start()
-    for ref in (fresh, part, grad_recv, placed, staged, acc):
+    for ref in (fresh, part, grad_recv, own.at[pl.ds(0, rows + 2)], cells, staged, acc):
         waits(ref, out_sem)
 
 
@@ -923,11 +1007,12 @@
             shape(D, NBR, rows, LANES),
             shape(rows, *tile),
             shape(rows, *tile),
-            shape(rows + 2, 3, *tile),
+            shape(rows + 2, *tile),
+            shape(2, *tile),
             shape(4, *tile),
         ),
         in_specs=[HBM] * 10,
-        out_specs=[HBM] * 6,
+        out_specs=[HBM] * 7,
         scratch_shapes=[
             vmem(rows, D, wide),
             pltpu.VMEM((rows, 2 * D, wide), BF16),
@@ -935,8 +1020,8 @@
             vmem(rows, D, wide),
             vmem(rows, D, wide),
             vmem(rows, D, wide),
-            vmem(rows + 2, 3, *tile),
-            vmem(rows + 2, *tile),
+            vmem(rows + 6, 3, *tile),
+            vmem(rows + 6, *tile),
             vmem(rows, *tile),
             vmem(2, *tile),
             pltpu.VMEM((rows, 8, LANES), jnp.int32),
@@ -948,12 +1033,13 @@
             vmem(rows, *tile),
             vmem(rows, *tile),
             vmem(rows, *tile),
-            vmem(rows, *tile),
-            vmem(rows, *tile),
+            vmem(rows // 8, D, 8, LANES),
+            vmem(rows // 8, D, 8, LANES),
             vmem(rows, *tile),
             vmem(rows + 2, 3, *tile),
+            vmem(2, *tile),
             vmem(rows, *tile),
-            pltpu.VMEM((2, 4 * D, wide), BF16),
+            pltpu.VMEM((4, 4 * D, wide), BF16),
             vmem(2 * D, 2 * D),
             vmem(2 * D, 2 * D + 16),
             vmem(2 * D, 4 * D),
@@ -973,31 +1059,36 @@
     n_blk,
     n_lon,
     acc_in,
-    placed_in,
+    own_in,
+    cells_in,
     recv_in,
     part_in,
     state_in,
-    cols_in,
+    cols_all,
     pack_in,
     part_out,
     total_out,
     acc,
-    placed,
+    own,
+    cells,
     grad_recv,
     part,
+    natural,
     state,
     cols,
     pack,
-    own,
-    halo,
+    edge_rows,
+    edge_cols,
+    edge_corners,
+    rows_in,
+    cols_in,
+    corners_in,
     acc_send,
     acc_recv,
     packed,
     scattered,
     across,
     gathered,
-    landing,
-    halo_in,
     in_sem,
     row_sem,
     rs_send,
@@ -1033,16 +1124,17 @@
         span = pl.ds(h * half, half)
         span3 = pl.ds(0, half + 1) if h == 0 else pl.ds(half + 1, half + 1)
         for source, target in (
-            (placed_in.at[span3], placed.at[span3]),
+            (own_in.at[span3], own.at[span3]),
             (state_in.at[span3], state.at[span3]),
             (recv_in.at[span], grad_recv.at[span]),
         ):
             pltpu.make_async_copy(source, target, row_sem.at[h]).start()
     small = (
         (pack_in.at[pl.ds(P_SEND_T[0], 2 * D)], pack),
-        (cols_in, cols),
+        (cols_all, cols),
         (acc_in, acc),
         (part_in, part),
+        (cells_in, cells),
     )
     for i, (source, target) in enumerate(small):
         pltpu.make_async_copy(source, target, in_sem.at[i]).start()
@@ -1069,21 +1161,6 @@
     acc_send[...] = jnp.zeros_like(acc_send)
     acc_recv[...] = jnp.zeros_like(acc_recv)
 
-    def settle(t, cells):
-        west_cells, east_cells = cells
-        to_west = placed[t, 0]
-        to_east = placed[t, 2]
-        value = (
-            placed[t, 1]
-            + jnp.where(lane == 0, 0.0, pltpu.roll(to_east, 1, 1))
-            + jnp.where(lane == LANES - 1, 0.0, pltpu.roll(to_west, LANES - 1, 1))
-        )
-        own[t] = value
-        mix = pltpu.roll(jnp.where(lane == 0, to_west, to_east), t, 1)
-        west_cells = jnp.where(lane == t, mix, west_cells)
-        east_cells = jnp.where(lane == lax.rem(t + LANES - 1, LANES), mix, east_cells)
-        return value, (west_cells, east_cells)
-
     def both_halves(value):
         return jnp.concatenate(halves(value), axis=0)
 
@@ -1091,30 +1168,22 @@
         lax.broadcasted_iota(jnp.int32, (16, 4 * LANES), 0) < 1, 1.0, 0.0
     ).astype(BF16)
 
-    def collect(i, cells):
-        values, there, received = [], [], []
-        for u in range(4):
-            t = 1 + 4 * i + u
-            value, cells = settle(t, cells)
-            values.append(value)
-            there.append(state[t])
-            received.append(grad_recv[t - 1])
-        wide = lambda parts: both_halves(jnp.concatenate(parts, axis=1))
-        there = wide(there)
-        acc_send[...] += outer(wide(values), there)
-        acc_recv[...] += outer(wide(received), jnp.concatenate([there, ones_row], axis=0))
-        return cells
-
-    zero = jnp.zeros((D, LANES), F32)
+    def collect(i, _):
+        wide = lambda ref, first: both_halves(
+            jnp.concatenate([ref[first + u] for u in range(4)], axis=1)
+        )
+        there = wide(state, 1 + 4 * i)
+        acc_send[...] += outer(wide(own, 1 + 4 * i), there)
+        acc_recv[...] += outer(
+            wide(grad_recv, 4 * i), jnp.concatenate([there, ones_row], axis=0)
+        )
+
     for h in range(2):
-        span = pl.ds(h * half, half)
-        waits(placed.at[pl.ds(h * (half + 1), half + 1)], row_sem.at[h])
+        waits(own.at[pl.ds(h * (half + 1), half + 1)], row_sem.at[h])
         waits(state.at[pl.ds(h * (half + 1), half + 1)], row_sem.at[h])
-        waits(grad_recv.at[span], row_sem.at[h])
-        if h == 0:
-            _, cells = settle(0, (zero, zero))
-        cells = lax.fori_loop(h * half // 4, (h + 1) * half // 4, collect, cells)
-    _, cells = settle(rows + 1, cells)
+        waits(grad_recv.at[pl.ds(h * half, half)], row_sem.at[h])
+        lax.fori_loop(h * half // 4, (h + 1) * half // 4, collect, None)
+    waits(cells, in_sem.at[4])
     waits(cols, in_sem.at[1])
     edge_values = jnp.concatenate([own[0], own[rows + 1], cells[0], cells[1]], axis=1)
     edge_states = jnp.concatenate([state[0], state[rows + 1], cols[0], cols[1]], axis=1)
@@ -1163,21 +1232,31 @@
     a_recv = pack[D : 2 * D, : 3 * D]
     high, low = halves(edge_values)
     edge_grads = mxu(a_send, jnp.concatenate([high, low, high], axis=0))
-    for i in range(4):
-        halo[i] = edge_grads[:, i * LANES : (i + 1) * LANES]
-    copies = []
-    for slot, (place, source) in enumerate(zip(around, (0, 1, 2, 3, 2, 3, 2, 3))):
-        copies.append(
-            pltpu.make_async_remote_copy(
-                src_ref=halo.at[source],
-                dst_ref=landing.at[slot],
-                send_sem=halo_send.at[slot],
-                recv_sem=halo_recv.at[slot],
-                device_id=place,
-                device_id_type=MESH,
-            )
-        )
-        copies[-1].start()
+    edge_grad = [edge_grads[:, i * LANES : (i + 1) * LANES] for i in range(4)]
+    edge_rows[0], edge_rows[1] = edge_grad[0], edge_grad[1]
+    west_cells, east_cells = edge_grad[2], edge_grad[3]
+    edge_cols[0], edge_cols[1] = pack_column(west_cells), pack_column(east_cells)
+    edge_corners[...] = corner_rows(
+        [
+            west_cells[:, :1],
+            east_cells[:, LANES - 1 :],
+            west_cells[:, rows + 1 : rows + 2],
+            east_cells[:, rows : rows + 1],
+        ]
+    )
+    copies = rim_copies(
+        around,
+        edge_rows,
+        edge_cols,
+        edge_corners,
+        rows_in,
+        cols_in,
+        corners_in,
+        halo_send,
+        halo_recv,
+    )
+    for copy in copies:
+        copy.start()
     waits(part, in_sem.at[3])
 
     def finish(i, _):
@@ -1235,26 +1314,20 @@
     lax.fori_loop(1, size, gather, None)
     for copy in copies:
         copy.wait()
-    halo_in[0] = landing[1]
-    halo_in[1] = landing[0]
-    corner = lambda slot, at, to: jnp.where(
-        lane == to, pltpu.roll(landing[slot], (to - at) % LANES, 1), 0.0
-    )
-    halo_in[2] = (
-        pltpu.roll(jnp.where(lane < rows, landing[3], 0.0), 1, 1)
-        + corner(7, rows, 1)
-        + corner(5, LANES - 1, rows)
-    )
+    west_in = (
+        pltpu.roll(jnp.where(lane < rows, unpack_column(cols_in[1]), 0.0), 1, 1)
+        + corner_at(corners_in.at[3], 3, 1)
+        + corner_at(corners_in.at[1], 1, rows)
+    )
+    east_in = unpack_column(cols_in[0])
     east_in = (
-        jnp.where((lane >= 1) & (lane <= rows), landing[2], 0.0)
-        + corner(6, rows + 1, 1)
-        + corner(4, 0, rows)
-    )
-    west_in = halo_in[2]
-    east_in = pltpu.roll(east_in, LANES - 1, 1)
+        pltpu.roll(jnp.where((lane >= 1) & (lane <= rows), east_in, 0.0), LANES - 1, 1)
+        + corner_at(corners_in.at[2], 2, 0)
+        + corner_at(corners_in.at[0], 0, rows - 1)
+    )
     rim = (lane == 0) | (lane == LANES - 1)
-    part[0] += halo_in[0]
-    part[rows - 1] += halo_in[1]
+    part[0] += rows_in[1]
+    part[rows - 1] += rows_in[0]
 
     def add_columns(i, _):
         for u in range(4):
@@ -1262,12 +1335,13 @@
             mix = pltpu.roll(
                 jnp.where(lane == r + 1, west_in, east_in), LANES - 1 - r, 1
             )
-            part[r] += jnp.where(rim, mix, 0.0)
-        for u in range(4):
-            r = 4 * i + u
-            pltpu.make_async_copy(part.at[r], part_out.at[:, r, :], out_sem).start()
+            write_row(natural.at[r // 8], lax.rem(r, 8), part[r] + jnp.where(rim, mix, 0.0))
 
     lax.fori_loop(0, rows // 4, add_columns, None)
+    for g in range(rows // 8):
+        pltpu.make_async_copy(
+            natural.at[g], part_out.at[:, pl.ds(8 * g, 8), :], out_sem
+        ).start()
     waits(gathered.at[others], ag_recv)
     pltpu.make_async_copy(gathered, total_out, out_sem).start()
     waits(scattered.at[others], rs_send)
@@ -1276,7 +1350,7 @@
         waits(ref, out_sem)
 
 
-def sum_call(n_blk, n_lon, acc, placed, recv, part, state, cols, pack):
+def sum_call(n_blk, n_lon, acc, own, cells, recv, part, state, cols, pack):
     rows = recv.shape[0]
     size = min(32, n_blk * n_lon)
     n_groups = n_blk * n_lon // size
@@ -1289,27 +1363,31 @@
         functools.partial(sum_kernel, n_blk, n_lon),
         name="sums",
         out_shape=(shape(D, rows, LANES), shape(size, *chunk)),
-        in_specs=[HBM] * 7,
+        in_specs=[HBM] * 8,
         out_specs=[HBM] * 2,
         scratch_shapes=[
             vmem(4, *tile),
-            vmem(rows + 2, 3, *tile),
+            vmem(rows + 2, *tile),
+            vmem(2, *tile),
             vmem(rows, *tile),
             vmem(rows, *tile),
+            vmem(rows // 8, D, 8, LANES),
             vmem(rows + 2, *tile),
             vmem(2, *tile),
             pltpu.VMEM((2 * D, P_LANES), BF16),
-            vmem(rows + 2, *tile),
-            vmem(4, *tile),
+            vmem(2, *tile),
+            vmem(2, D // 2, LANES),
+            vmem(8, LANES),
+            vmem(2, *tile),
+            vmem(2, D // 2, LANES),
+            vmem(4, 8, LANES),
             vmem(2 * D, 2 * D),
             vmem(2 * D, 2 * D + 16),
             vmem(size, *chunk),
             vmem(size, *chunk),
             vmem(n_groups, *chunk),
             vmem(size, *chunk),
-            vmem(8, *tile),
-            vmem(3, *tile),
-            dma((4,)),
+            dma((5,)),
             dma((2,)),
             dma,
             dma,
@@ -1324,11 +1402,10 @@
         compiler_params=pltpu.CompilerParams(
             collective_id=1, has_side_effects=True, vmem_limit_bytes=ROOM
         ),
-    )(acc, placed, recv, part, state, cols, pack)
+    )(acc, own, cells, recv, part, state, cols, pack)
 
 
 def final_kernel(
-    kl_weight,
     part_nodes,
     mean,
     logstd,
@@ -1373,7 +1450,7 @@
     for source, target in zip(smalls, small_outs):
         pltpu.make_async_copy(source, target, out_sem).start()
 
-    inside = (kl_weight[0] * columns[C_VALID, 0:1, :]).reshape(1, 1, LANES)
+    inside = columns[C_VALID, 0:1, :].reshape(1, 1, LANES)
     for i, span in enumerate(spans):
         for _, target in pairs:
             waits(target.at[span], in_sem.at[i])
@@ -1390,7 +1467,7 @@
         waits(ref, out_sem)
 
 
-def final_call(kl_weight, part_nodes, mean, logstd, noise, total, columns):
+def final_call(part_nodes, mean, logstd, noise, total, columns):
     shape = lambda *dims: jax.ShapeDtypeStruct(dims, F32)
     vmem = lambda *dims: pltpu.VMEM(dims, F32)
     whole = mean.shape
@@ -1399,7 +1476,7 @@
         final_kernel,
         name="final",
         out_shape=[shape(*dims) for dims in (whole,) * 3 + small],
-        in_specs=[SMEM] + [HBM] * 6,
+        in_specs=[HBM] * 6,
         out_specs=[HBM] * 16,
         scratch_shapes=[vmem(*whole) for _ in range(4)]
         + [vmem(*total.shape), vmem(C_TILES, D, LANES)]
@@ -1410,7 +1487,7 @@
             pltpu.SemaphoreType.DMA,
         ],
         compiler_params=pltpu.CompilerParams(vmem_limit_bytes=ROOM),
-    )(kl_weight, part_nodes, mean, logstd, noise, total, columns)
+    )(part_nodes, mean, logstd, noise, total, columns)
 
 
 def shards(
@@ -1455,6 +1532,7 @@
         n_blk,
         n_lon,
         band_counts,
+        kl_weight,
         nodes,
         latent_mean,
         latent_logstd,
@@ -1463,13 +1541,12 @@
         edge_mask,
         weights,
     )
-    new_states, grad_edges, part, recv, placed, acc = layer_call(
+    new_states, grad_edges, part, recv, own, cells, acc = layer_call(
         edges, cotangent, projected, receiver, sides, codes, valid, pack, columns, state
     )
-    part, total = sum_call(n_blk, n_lon, acc, placed, recv, part, state, cols, pack)
+    part, total = sum_call(n_blk, n_lon, acc, own, cells, recv, part, state, cols, pack)
     grad_nodes, grad_mean, grad_logstd, kl_value, g_w_ei, g_w_eo, g_w_ni, g_w_no, *g_vec = (
         final_call(
-            kl_weight,
             part,
             latent_mean,
             latent_logstd,

time: 70.8 us -> 62.7 us (0.89)
  Pallas kernels: 69.1 us -> 60.9 us
    pallas_call x1, Pallas kernels: 31.8 us -> 28.2 us  [layer_call(): pl.pallas_call(layer_kernel, name='layer', out_shape=(shape(D, rows, LANE...]
    pallas_call x1, Pallas kernels: 18.7 us -> 15.7 us  [sum_call(): pl.pallas_call(functools.partial(sum_kernel, n_blk, n_lon), name='sums',...]
    pallas_call x1, Pallas kernels: 14.3 us -> 12.8 us  [start_call(): pl.pallas_call(functools.partial(start_kernel, n_blk, n_lon), name='start...]
where the time goes in v3:
time: 62.7 us; the launch traced here: 62.4 us
  Pallas kernels  60.9 us (97%)
  between operations  1.49 us (2%)
    pallas_call x1, Pallas kernels, layer_call(): pl.pallas_call(layer_kernel, name='layer', out_shape=(shape(D, rows, LANE...  28.2 us
    pallas_call x1, Pallas kernels, sum_call(): pl.pallas_call(functools.partial(sum_kernel, n_blk, n_lon), name='sums',...  15.7 us
    pallas_call x1, Pallas kernels, start_call(): pl.pallas_call(functools.partial(start_kernel, n_blk, n_lon), name='start...  12.8 us
    pallas_call x1, Pallas kernels, final_call(): pl.pallas_call(final_kernel, name='final', out_shape=[shape(*dims) for di...  4.31 us

profile of v3, /device:TPU:0, one launch (start us, length us, event | category | flops | bytes accessed | tf_op | source)
XLA Modules:
  0.0 62.4 jit_solution(6253484734319124281)
XLA Ops:
  1.3 12.8 %start.1 = (f32[34,64,128]{2,1,0:T(8,128)}, f32[2,64,128]{2,1,0:T(8,128)}, f32[34,64,128]{2,1,0:T(8,128)}, f32[32,64,128]{2,1,0:T(8,128)}, f32[2,64,128]{2,1,0:T...) custom-call(s32[8]{0:T(128)} %counts.1, ...), custom_call_target="tpu_custom_call" | custom-call | tf_op jit(solution)/shard_map/start/pallas_call | solution.py:472
  14.1 28.2 %layer.1 = (f32[64,32,128]{2,1,0:T(8,128)}, f32[64,6,32,128]{3,2,1,0:T(8,128)}, f32[32,64,128]{2,1,0:T(8,128)}, f32[32,64,128]{2,1,0:T(8,128)}, f32[34,64,128]{2...) custom-call(f32[64,6,32,128]{3,2,1,0:T(8,128)} %edges.1, f32[64,32,128]{2,1,0:T(8,128)} %cotangent.1, ...), custom_call_target="tpu_custom_call" | custom-call | tf_op jit(solution)/shard_map/layer/pallas_call | solution.py:1002
  42.3 15.7 %sums.1 = (f32[64,32,128]{2,1,0:T(8,128)}, f32[32,8,128]{2,1,0:T(8,128)}) custom-call(f32[4,64,128]{2,1,0:T(8,128)} %get-tuple-element.61.acc_in, f32[34,64,128]{2,1,0:T(8,128)} %get-tuple-element.62.own_in, f32[2,64,128]{2,1,0:T(8,128)} %get-tuple-element.63.cells_in, f32[32,64,128]{2,1,0:T(8,128)} %get-tuple-element.64.recv_in, ...), custom_call_target="tpu_custom_call" | custom-call | tf_op jit(solution)/shard_map/sums/pallas_call | solution.py:1362
  58.0 4.3 %final.1 = (f32[64,32,128]{2,1,0:T(8,128)}, f32[64,32,128]{2,1,0:T(8,128)}, f32[64,32,128]{2,1,0:T(8,128)}, f32[1,1]{1,0:T(1,128)}, f32[64,192]{1,0:T(8,128)}, /...) custom-call(f32[64,32,128]{2,1,0:T(8,128)} %get-tuple-element.67.par, ...), custom_call_target="tpu_custom_call" | custom-call | tf_op jit(solution)/shard_map/final/pallas_call | solution.py:1475

commit v4 on v3

--- a/solution.py
+++ b/solution.py
@@ -551,10 +551,8 @@
     qo_ref,
     cot,
     fresh,
-    part,
     placed,
     cells,
-    grad_recv,
     gather_grads,
     acc_edge,
     acc_hidden,
@@ -570,10 +568,10 @@
     rows = cotangent.shape[1]
     wide = NBR * LANES
     two = 2 * LANES
+    part, grad_recv, own = receiver, summed, projected
     lane = lane_ids()
 
-    halfway = 14
-    ahead = 8
+    halfway = 10
 
     def load_edges(r):
         for k in range(NBR):
@@ -604,8 +602,7 @@
                 load_edges(r)
             for source, target in first_small[2:]:
                 pltpu.make_async_copy(source, target, in_sem.at[0]).start()
-    for r in range(4, ahead + 4):
-        load_edges(r)
+    lax.fori_loop(4, 12, lambda r, _: load_edges(r), None)
 
     def load_rest():
         rest = pl.ds(P_EDGE[1], P_ROWS - P_EDGE[1])
@@ -617,6 +614,7 @@
             pltpu.make_async_copy(
                 cotangent.at[:, pl.ds(8 * g, 8), :], cot.at[g], in_sem.at[1]
             ).start()
+        lax.fori_loop(12, rows, lambda r, _: load_edges(r), None)
         return (cot, state, columns, pack.at[rest])
 
     ones16 = jnp.where(
@@ -697,12 +695,10 @@
             total = None
         return total
 
-    def forward(i, _, first=0, last=2, more=True):
+    def forward(i, _, first=0, last=2):
         turn = [4 * i + u for u in range(4)]
         if first == 0:
             for r in turn:
-                if more:
-                    load_edges(r + 4 + ahead)
                 waits(staged.at[r + 4], edge_sem.at[r + 4])
             for r in turn:
                 shift(r + 6)
@@ -734,14 +730,12 @@
         waits(staged.at[r], edge_sem.at[r])
         for pair in range(NBR // 2):
             edge_product(r, pair)
+    node_inputs = load_rest()
+    forward(0, None, last=1)
     for ref in parts[1]:
         waits(ref, row_sem.at[1])
-    node_inputs = load_rest()
-    forward(0, None, last=1)
     turns = rows // 4
-    full = turns - 1 - ahead // 4
-    lax.fori_loop(1, full, forward, None)
-    lax.fori_loop(full, turns - 1, functools.partial(forward, more=False), None)
+    lax.fori_loop(1, turns - 1, forward, None)
     forward(turns - 1, None, first=1)
     forward(turns, None, first=2)
 
@@ -889,8 +883,6 @@
         r = jnp.maximum(r, 0)
         acc_hidden[...] += outer(gather_grads[u, : 2 * D], hs[r])
         acc_edge[...] += outer(gather_grads[u, 2 * D :], xs[r])
-
-    own = projected
 
     def settle(t):
         to_west = placed[t, 0]
@@ -1035,10 +1027,8 @@
             vmem(rows, *tile),
             vmem(rows // 8, D, 8, LANES),
             vmem(rows // 8, D, 8, LANES),
-            vmem(rows, *tile),
             vmem(rows + 2, 3, *tile),
             vmem(2, *tile),
-            vmem(rows, *tile),
             pltpu.VMEM((4, 4 * D, wide), BF16),
             vmem(2 * D, 2 * D),
             vmem(2 * D, 2 * D + 16),
@@ -1066,7 +1056,13 @@
     state_in,
     cols_all,
     pack_in,
-    part_out,
+    columns_in,
+    mean,
+    logstd,
+    noise,
+    nodes_out,
+    mean_out,
+    logstd_out,
     total_out,
     acc,
     own,
@@ -1074,6 +1070,10 @@
     grad_recv,
     part,
     natural,
+    mean_v,
+    logstd_v,
+    noise_v,
+    inside,
     state,
     cols,
     pack,
@@ -1099,6 +1099,7 @@
     ag_recv,
     halo_send,
     halo_recv,
+    latent_sem,
     out_sem,
 ):
     rows = recv_in.shape[0]
@@ -1111,10 +1112,14 @@
     lane = lane_ids()
 
     def member(index):
-        return (own_group * per + index // n_lon, lax.rem(index, n_lon))
+        if n_lon & (n_lon - 1):
+            return (own_group * per + index // n_lon, lax.rem(index, n_lon))
+        return (own_group * per + (index >> (n_lon.bit_length() - 1)), index & (n_lon - 1))
 
     def other(step):
-        return lax.rem(me + step, size)
+        if size & (size - 1):
+            return lax.rem(me + step, size)
+        return (me + step) & (size - 1)
 
     def peer(step):
         return (lax.rem(own_group + step, n_groups) * per + lax.rem(blk, per), lon)
@@ -1135,10 +1140,13 @@
         (acc_in, acc),
         (part_in, part),
         (cells_in, cells),
+        (columns_in.at[C_VALID], inside),
     )
     for i, (source, target) in enumerate(small):
         pltpu.make_async_copy(source, target, in_sem.at[i]).start()
 
+    groups = [pl.ds(8 * g, 8) for g in range(rows // 8)]
+    latent = ((mean, mean_v), (logstd, logstd_v), (noise, noise_v))
     barrier = pltpu.get_barrier_semaphore()
 
     def greet(step, _):
@@ -1200,10 +1208,12 @@
         axis=1,
         keepdims=True,
     )
+    columns_t = jnp.where(lane == D, ones_sum, acc[1]).T[D:]
+    vector_rows = jnp.concatenate([jnp.zeros((D, D), F32), columns_t], axis=1)
     chunk = packed.shape[1]
     blocks = (
         jnp.where(left, acc[0], folded(acc_send)),
-        jnp.where(left, folded(acc_recv), jnp.where(lane == D, ones_sum, acc[1])),
+        jnp.where(left, folded(acc_recv), vector_rows),
         acc[2],
         acc[3],
     )
@@ -1211,6 +1221,10 @@
     for i, block in enumerate(blocks):
         for j in range(per_block):
             packed[i * per_block + j] = block[j * chunk : (j + 1) * chunk]
+    for g, span in enumerate(groups):
+        for source, target in latent:
+            pltpu.make_async_copy(source.at[:, span, :], target.at[g], latent_sem).start()
+
     pl.semaphore_wait(barrier, expected)
 
     def scatter(step, _):
@@ -1274,6 +1288,23 @@
 
     lax.fori_loop(0, rows // 4, finish, None)
 
+    waits(inside, in_sem.at[5])
+    for _, target in latent:
+        waits(target, latent_sem)
+    weight = inside[0:1, :].reshape(1, 1, LANES)
+
+    def blocks(i):
+        return i // 8, pl.ds(8 * (i % 8), 8)
+
+    def latent_terms(i, _):
+        at = blocks(i)
+        spread = jnp.exp(logstd_v[at])
+        mean_v[at] = weight * mean_v[at]
+        noise_v[at] = spread * noise_v[at]
+        logstd_v[at] = weight * (spread * spread - 1.0)
+
+    lax.fori_loop(0, rows, latent_terms, None)
+
     others = pl.ds(0, size - 1)
     waits(scattered.at[others], rs_recv)
     mine = scattered[0]
@@ -1338,19 +1369,28 @@
             write_row(natural.at[r // 8], lax.rem(r, 8), part[r] + jnp.where(rim, mix, 0.0))
 
     lax.fori_loop(0, rows // 4, add_columns, None)
-    for g in range(rows // 8):
-        pltpu.make_async_copy(
-            natural.at[g], part_out.at[:, pl.ds(8 * g, 8), :], out_sem
-        ).start()
+
+    def latent_grads(i, _):
+        at = blocks(i)
+        grad = natural[at]
+        mean_v[at] = grad + mean_v[at]
+        logstd_v[at] = grad * noise_v[at] + logstd_v[at]
+
+    lax.fori_loop(0, rows, latent_grads, None)
+    results = ((natural, nodes_out), (mean_v, mean_out), (logstd_v, logstd_out))
+    for g, span in enumerate(groups):
+        for source, target in results:
+            pltpu.make_async_copy(source.at[g], target.at[:, span, :], out_sem).start()
     waits(gathered.at[others], ag_recv)
     pltpu.make_async_copy(gathered, total_out, out_sem).start()
     waits(scattered.at[others], rs_send)
     waits(gathered.at[others], ag_send)
-    for ref in (part, gathered):
+    for ref in (natural, mean_v, logstd_v, gathered):
         waits(ref, out_sem)
 
 
-def sum_call(n_blk, n_lon, acc, own, cells, recv, part, state, cols, pack):
+def sum_call(n_blk, n_lon, *operands):
+    recv = operands[3]
     rows = recv.shape[0]
     size = min(32, n_blk * n_lon)
     n_groups = n_blk * n_lon // size
@@ -1362,9 +1402,9 @@
     return pl.pallas_call(
         functools.partial(sum_kernel, n_blk, n_lon),
         name="sums",
-        out_shape=(shape(D, rows, LANES), shape(size, *chunk)),
-        in_specs=[HBM] * 8,
-        out_specs=[HBM] * 2,
+        out_shape=(shape(D, rows, LANES),) * 3 + (shape(size, *chunk),),
+        in_specs=[HBM] * 12,
+        out_specs=[HBM] * 4,
         scratch_shapes=[
             vmem(4, *tile),
             vmem(rows + 2, *tile),
@@ -1372,6 +1412,10 @@
             vmem(rows, *tile),
             vmem(rows, *tile),
             vmem(rows // 8, D, 8, LANES),
+            vmem(rows // 8, D, 8, LANES),
+            vmem(rows // 8, D, 8, LANES),
+            vmem(rows // 8, D, 8, LANES),
+            vmem(*tile),
             vmem(rows + 2, *tile),
             vmem(2, *tile),
             pltpu.VMEM((2 * D, P_LANES), BF16),
@@ -1387,7 +1431,7 @@
             vmem(size, *chunk),
             vmem(n_groups, *chunk),
             vmem(size, *chunk),
-            dma((5,)),
+            dma((6,)),
             dma((2,)),
             dma,
             dma,
@@ -1398,36 +1442,36 @@
             dma((8,)),
             dma((8,)),
             dma,
+            dma,
         ],
         compiler_params=pltpu.CompilerParams(
             collective_id=1, has_side_effects=True, vmem_limit_bytes=ROOM
         ),
-    )(acc, own, cells, recv, part, state, cols, pack)
-
-
-def final_kernel(
-    part_nodes,
-    mean,
-    logstd,
-    noise,
-    total_in,
-    columns_in,
-    *rest,
-):
-    grad_nodes, grad_mean, grad_logstd = rest[:3]
-    small_outs = rest[3:16]
-    grad, mean_v, logstd_v, noise_v, total, columns = rest[16:22]
-    smalls = rest[22:35]
-    in_sem, small_sem, out_sem = rest[35:]
+    )(*operands)
+
+
+def final_kernel(*refs):
+    large_in, (total_in, columns_in), refs = refs[:3], refs[3:5], refs[5:]
+    large_outs, small_outs, refs = refs[:3], refs[3:16], refs[16:]
+    large, (total, columns), smalls, refs = refs[:3], refs[3:5], refs[5:18], refs[18:]
+    in_sem, small_sem, out_sem = refs
     n_chunks = in_sem.shape[0]
     depth = D // n_chunks
     for i, (source, target) in enumerate(((columns_in, columns), (total_in, total))):
         pltpu.make_async_copy(source, target, small_sem.at[i]).start()
     spans = [pl.ds(i * depth, depth) for i in range(n_chunks)]
-    pairs = ((part_nodes, grad), (mean, mean_v), (logstd, logstd_v), (noise, noise_v))
     for i, span in enumerate(spans):
-        for source, target in pairs:
+        for source, target in zip(large_in, large):
             pltpu.make_async_copy(source.at[span], target.at[span], in_sem.at[i]).start()
+
+    def forward_block(i):
+        for ref in large:
+            waits(ref.at[spans[i]], in_sem.at[i])
+        for source, target in zip(large, large_outs):
+            pltpu.make_async_copy(source.at[spans[i]], target.at[spans[i]], out_sem).start()
+
+    for i in range(2):
+        forward_block(i)
 
     waits(columns, small_sem.at[0])
     waits(total, small_sem.at[1])
@@ -1443,43 +1487,33 @@
     g_w_ni[...] = blocks[2]
     g_w_eo[...] = blocks[3][:, :D]
     g_w_no[...] = pltpu.roll(blocks[3], D, 1)[:, :D]
+    vector_rows = pltpu.roll(blocks[1][:16], D, 1)
     for i in range(8):
-        smalls[5 + i][...] = to_row(blocks[1][:, D + i : D + i + 1])
-    diverged = jnp.sum(blocks[1][:, D + 8 : D + 9], axis=0, keepdims=True)
+        smalls[5 + i][...] = vector_rows[i : i + 1, :D]
+    diverged = jnp.sum(vector_rows[8:9, :D], axis=1, keepdims=True)
     kl_value[...] = diverged / columns[C_COUNT, 0:1, 0:1]
     for source, target in zip(smalls, small_outs):
         pltpu.make_async_copy(source, target, out_sem).start()
 
-    inside = columns[C_VALID, 0:1, :].reshape(1, 1, LANES)
-    for i, span in enumerate(spans):
-        for _, target in pairs:
-            waits(target.at[span], in_sem.at[i])
-        pltpu.make_async_copy(grad.at[span], grad_nodes.at[span], out_sem).start()
-        for f in range(i * depth, (i + 1) * depth):
-            one = pl.ds(f, 1)
-            g = grad[one]
-            spread = jnp.exp(logstd_v[one])
-            mean_v[one] = g + inside * mean_v[one]
-            logstd_v[one] = g * spread * noise_v[one] + inside * (spread * spread - 1.0)
-        pltpu.make_async_copy(mean_v.at[span], grad_mean.at[span], out_sem).start()
-        pltpu.make_async_copy(logstd_v.at[span], grad_logstd.at[span], out_sem).start()
-    for ref in (grad, mean_v, logstd_v, *smalls):
+    for i in range(2, n_chunks):
+        forward_block(i)
+    for ref in (*large, *smalls):
         waits(ref, out_sem)
 
 
-def final_call(part_nodes, mean, logstd, noise, total, columns):
+def final_call(*operands):
     shape = lambda *dims: jax.ShapeDtypeStruct(dims, F32)
     vmem = lambda *dims: pltpu.VMEM(dims, F32)
-    whole = mean.shape
+    whole, total = operands[0].shape, operands[3].shape
     small = ((1, 1), (D, 3 * D), (D, D), (D, 2 * D), (D, D)) + ((1, D),) * 8
     return pl.pallas_call(
         final_kernel,
         name="final",
         out_shape=[shape(*dims) for dims in (whole,) * 3 + small],
-        in_specs=[HBM] * 6,
+        in_specs=[HBM] * 5,
         out_specs=[HBM] * 16,
-        scratch_shapes=[vmem(*whole) for _ in range(4)]
-        + [vmem(*total.shape), vmem(C_TILES, D, LANES)]
+        scratch_shapes=[vmem(*whole) for _ in range(3)]
+        + [vmem(*total), vmem(C_TILES, D, LANES)]
         + [vmem(*dims) for dims in small]
         + [
             pltpu.SemaphoreType.DMA((8,)),
@@ -1487,7 +1521,7 @@
             pltpu.SemaphoreType.DMA,
         ],
         compiler_params=pltpu.CompilerParams(vmem_limit_bytes=ROOM),
-    )(part_nodes, mean, logstd, noise, total, columns)
+    )(*operands)
 
 
 def shards(
@@ -1544,16 +1578,24 @@
     new_states, grad_edges, part, recv, own, cells, acc = layer_call(
         edges, cotangent, projected, receiver, sides, codes, valid, pack, columns, state
     )
-    part, total = sum_call(n_blk, n_lon, acc, own, cells, recv, part, state, cols, pack)
+    grads = sum_call(
+        n_blk,
+        n_lon,
+        acc,
+        own,
+        cells,
+        recv,
+        part,
+        state,
+        cols,
+        pack,
+        columns,
+        latent_mean,
+        latent_logstd,
+        latent_noise,
+    )
     grad_nodes, grad_mean, grad_logstd, kl_value, g_w_ei, g_w_eo, g_w_ni, g_w_no, *g_vec = (
-        final_call(
-            part,
-            latent_mean,
-            latent_logstd,
-            latent_noise,
-            total,
-            columns,
-        )
+        final_call(*grads, columns)
     )
     g_vec = [vector.reshape(D) for vector in g_vec]
     return (

time: 62.7 us -> 62 us (0.989)
  no operation moved by 1% of the time
where the time goes in v4:
time: 62 us; the launch traced here: 61.7 us
  Pallas kernels  60.4 us (97%)
  between operations  1.33 us (2%)
    pallas_call x1, Pallas kernels, layer_call(): pl.pallas_call(layer_kernel, name='layer', out_shape=(shape(D, rows, LANE...  28 us
    pallas_call x1, Pallas kernels, sum_call(): pl.pallas_call(functools.partial(sum_kernel, n_blk, n_lon), name='sums',...  15.8 us
    pallas_call x1, Pallas kernels, start_call(): pl.pallas_call(functools.partial(start_kernel, n_blk, n_lon), name='start...  12.8 us
    pallas_call x1, Pallas kernels, final_call(): pl.pallas_call(final_kernel, name='final', out_shape=[shape(*dims) for di...  3.84 us

profile of v4, /device:TPU:0, one launch (start us, length us, event | category | flops | bytes accessed | tf_op | source)
XLA Modules:
  0.0 61.7 jit_solution(5443167902418548322)
XLA Ops:
  1.3 12.8 %start.1 = (f32[34,64,128]{2,1,0:T(8,128)}, f32[2,64,128]{2,1,0:T(8,128)}, f32[34,64,128]{2,1,0:T(8,128)}, f32[32,64,128]{2,1,0:T(8,128)}, f32[2,64,128]{2,1,0:T...) custom-call(s32[8]{0:T(128)} %counts.1, ...), custom_call_target="tpu_custom_call" | custom-call | tf_op jit(solution)/shard_map/start/pallas_call | solution.py:472
  14.1 28.0 %layer.1 = (f32[64,32,128]{2,1,0:T(8,128)}, f32[64,6,32,128]{3,2,1,0:T(8,128)}, f32[32,64,128]{2,1,0:T(8,128)}, f32[32,64,128]{2,1,0:T(8,128)}, f32[34,64,128]{2...) custom-call(f32[64,6,32,128]{3,2,1,0:T(8,128)} %edges.1, f32[64,32,128]{2,1,0:T(8,128)} %cotangent.1, ...), custom_call_target="tpu_custom_call" | custom-call | tf_op jit(solution)/shard_map/layer/pallas_call | solution.py:994
  42.1 15.8 %sums.1 = (f32[64,32,128]{2,1,0:T(8,128)}, f32[64,32,128]{2,1,0:T(8,128)}, f32[64,32,128]{2,1,0:T(8,128)}, f32[32,8,128]{2,1,0:T(8,128)}) custom-call(f32[4,64,128]{2,1,0:T(8,128)} %get-tuple-element.63.acc_in, f32[34,64,128]{2,1,0:T(8,128)} %get-tuple-element.64.own_in, f32[2,64,128]{2,1,0:T(8,128)} %get-tuple-element.65.cells_in, ...), custom_call_target="tpu_custom_call" | custom-call | tf_op jit(solution)/shard_map/sums/pallas_call | solution.py:1402
  57.9 3.8 %final.1 = (f32[64,32,128]{2,1,0:T(8,128)}, f32[64,32,128]{2,1,0:T(8,128)}, f32[64,32,128]{2,1,0:T(8,128)}, f32[1,1]{1,0:T(1,128)}, f32[64,192]{1,0:T(8,128)}, /...) custom-call(f32[64,32,128]{2,1,0:T(8,128)} %get-tuple-element.69.ref, ...), custom_call_target="tpu_custom_call" | custom-call | tf_op jit(solution)/shard_map/final/pallas_call | solution.py:1509

commit v5 on v4

--- a/solution.py
+++ b/solution.py
@@ -1470,7 +1470,7 @@
         for source, target in zip(large, large_outs):
             pltpu.make_async_copy(source.at[spans[i]], target.at[spans[i]], out_sem).start()
 
-    for i in range(2):
+    for i in range(n_chunks):
         forward_block(i)
 
     waits(columns, small_sem.at[0])
@@ -1494,9 +1494,6 @@
     kl_value[...] = diverged / columns[C_COUNT, 0:1, 0:1]
     for source, target in zip(smalls, small_outs):
         pltpu.make_async_copy(source, target, out_sem).start()
-
-    for i in range(2, n_chunks):
-        forward_block(i)
     for ref in (*large, *smalls):
         waits(ref, out_sem)
 
@@ -1516,7 +1513,7 @@
         + [vmem(*total), vmem(C_TILES, D, LANES)]
         + [vmem(*dims) for dims in small]
         + [
-            pltpu.SemaphoreType.DMA((8,)),
+            pltpu.SemaphoreType.DMA((4,)),
             pltpu.SemaphoreType.DMA((2,)),
             pltpu.SemaphoreType.DMA,
         ],

time: 62 us -> 61 us (0.984)
  Pallas kernels: 60.4 us -> 59.5 us
    pallas_call x1, Pallas kernels: 3.84 us -> 2.92 us  [final_call(): pl.pallas_call(final_kernel, name='final', out_shape=[shape(*dims) for di...]
where the time goes in v5:
time: 61 us; the launch traced here: 60.8 us
  Pallas kernels  59.5 us (98%)
  between operations  1.33 us (2%)
    pallas_call x1, Pallas kernels, layer_call(): pl.pallas_call(layer_kernel, name='layer', out_shape=(shape(D, rows, LANE...  28 us
    pallas_call x1, Pallas kernels, sum_call(): pl.pallas_call(functools.partial(sum_kernel, n_blk, n_lon), name='sums',...  15.8 us
    pallas_call x1, Pallas kernels, start_call(): pl.pallas_call(functools.partial(start_kernel, n_blk, n_lon), name='start...  12.8 us
    pallas_call x1, Pallas kernels, final_call(): pl.pallas_call(final_kernel, name='final', out_shape=[shape(*dims) for di...  2.92 us

profile of v5, /device:TPU:0, one launch (start us, length us, event | category | flops | bytes accessed | tf_op | source)
XLA Modules:
  0.0 60.8 jit_solution(4636855381960536148)
XLA Ops:
  1.3 12.8 %start.1 = (f32[34,64,128]{2,1,0:T(8,128)}, f32[2,64,128]{2,1,0:T(8,128)}, f32[34,64,128]{2,1,0:T(8,128)}, f32[32,64,128]{2,1,0:T(8,128)}, f32[2,64,128]{2,1,0:T...) custom-call(s32[8]{0:T(128)} %counts.1, ...), custom_call_target="tpu_custom_call" | custom-call | tf_op jit(solution)/shard_map/start/pallas_call | solution.py:472
  14.1 28.0 %layer.1 = (f32[64,32,128]{2,1,0:T(8,128)}, f32[64,6,32,128]{3,2,1,0:T(8,128)}, f32[32,64,128]{2,1,0:T(8,128)}, f32[32,64,128]{2,1,0:T(8,128)}, f32[34,64,128]{2...) custom-call(f32[64,6,32,128]{3,2,1,0:T(8,128)} %edges.1, f32[64,32,128]{2,1,0:T(8,128)} %cotangent.1, ...), custom_call_target="tpu_custom_call" | custom-call | tf_op jit(solution)/shard_map/layer/pallas_call | solution.py:994
  42.1 15.8 %sums.1 = (f32[64,32,128]{2,1,0:T(8,128)}, f32[64,32,128]{2,1,0:T(8,128)}, f32[64,32,128]{2,1,0:T(8,128)}, f32[32,8,128]{2,1,0:T(8,128)}) custom-call(f32[4,64,128]{2,1,0:T(8,128)} %get-tuple-element.63.acc_in, f32[34,64,128]{2,1,0:T(8,128)} %get-tuple-element.64.own_in, f32[2,64,128]{2,1,0:T(8,128)} %get-tuple-element.65.cells_in, ...), custom_call_target="tpu_custom_call" | custom-call | tf_op jit(solution)/shard_map/sums/pallas_call | solution.py:1402
  57.9 2.9 %final.1 = (f32[64,32,128]{2,1,0:T(8,128)}, f32[64,32,128]{2,1,0:T(8,128)}, f32[64,32,128]{2,1,0:T(8,128)}, f32[1,1]{1,0:T(1,128)}, f32[64,192]{1,0:T(8,128)}, /...) custom-call(f32[64,32,128]{2,1,0:T(8,128)} %get-tuple-element.69.ref, ...), custom_call_target="tpu_custom_call" | custom-call | tf_op jit(solution)/shard_map/final/pallas_call | solution.py:1506

commit v6 on v5

--- a/solution.py
+++ b/solution.py
@@ -935,13 +935,13 @@
     backward(0, None)
     lax.fori_loop(1, rows // 4, backward, None)
     send_rows(rows // 4 - 1)
+    for u in range(4):
+        products(rows - 4 + u, u)
     for t in range(rows - 4, rows + 2):
         settle(t)
     tail = pl.ds(rows - 4, 6)
     pltpu.make_async_copy(own.at[tail], own_out.at[tail], out_sem).start()
     pltpu.make_async_copy(cells, cells_out, out_sem).start()
-    for u in range(4):
-        products(rows - 4 + u, u)
 
     def folded(ref):
         half = ref[:D, : 2 * D] + ref[D:, : 2 * D]
@@ -1457,7 +1457,7 @@
     in_sem, small_sem, out_sem = refs
     n_chunks = in_sem.shape[0]
     depth = D // n_chunks
-    for i, (source, target) in enumerate(((columns_in, columns), (total_in, total))):
+    for i, (source, target) in enumerate(((columns_in.at[C_COUNT], columns), (total_in, total))):
         pltpu.make_async_copy(source, target, small_sem.at[i]).start()
     spans = [pl.ds(i * depth, depth) for i in range(n_chunks)]
     for i, span in enumerate(spans):
@@ -1491,7 +1491,7 @@
     for i in range(8):
         smalls[5 + i][...] = vector_rows[i : i + 1, :D]
     diverged = jnp.sum(vector_rows[8:9, :D], axis=1, keepdims=True)
-    kl_value[...] = diverged / columns[C_COUNT, 0:1, 0:1]
+    kl_value[...] = diverged / columns[0:1, 0:1]
     for source, target in zip(smalls, small_outs):
         pltpu.make_async_copy(source, target, out_sem).start()
     for ref in (*large, *smalls):
@@ -1510,7 +1510,7 @@
         in_specs=[HBM] * 5,
         out_specs=[HBM] * 16,
         scratch_shapes=[vmem(*whole) for _ in range(3)]
-        + [vmem(*total), vmem(C_TILES, D, LANES)]
+        + [vmem(*total), vmem(D, LANES)]
         + [vmem(*dims) for dims in small]
         + [
             pltpu.SemaphoreType.DMA((4,)),

time: 61 us -> 61 us (level)
  no operation moved by 1% of the time
where the time goes in v6:
time: 61 us; the launch traced here: 60.8 us
  Pallas kernels  59.4 us (97%)
  between operations  1.33 us (2%)
    pallas_call x1, Pallas kernels, layer_call(): pl.pallas_call(layer_kernel, name='layer', out_shape=(shape(D, rows, LANE...  28 us
    pallas_call x1, Pallas kernels, sum_call(): pl.pallas_call(functools.partial(sum_kernel, n_blk, n_lon), name='sums',...  15.8 us
    pallas_call x1, Pallas kernels, start_call(): pl.pallas_call(functools.partial(start_kernel, n_blk, n_lon), name='start...  12.8 us
    pallas_call x1, Pallas kernels, final_call(): pl.pallas_call(final_kernel, name='final', out_shape=[shape(*dims) for di...  2.87 us

profile of v6, /device:TPU:0, one launch (start us, length us, event | category | flops | bytes accessed | tf_op | source)
XLA Modules:
  0.0 60.8 jit_solution(10735782546592301604)
XLA Ops:
  1.3 12.8 %start.1 = (f32[34,64,128]{2,1,0:T(8,128)}, f32[2,64,128]{2,1,0:T(8,128)}, f32[34,64,128]{2,1,0:T(8,128)}, f32[32,64,128]{2,1,0:T(8,128)}, f32[2,64,128]{2,1,0:T...) custom-call(s32[8]{0:T(128)} %counts.1, ...), custom_call_target="tpu_custom_call" | custom-call | tf_op jit(solution)/shard_map/start/pallas_call | solution.py:472
  14.1 28.0 %layer.1 = (f32[64,32,128]{2,1,0:T(8,128)}, f32[64,6,32,128]{3,2,1,0:T(8,128)}, f32[32,64,128]{2,1,0:T(8,128)}, f32[32,64,128]{2,1,0:T(8,128)}, f32[34,64,128]{2...) custom-call(f32[64,6,32,128]{3,2,1,0:T(8,128)} %edges.1, f32[64,32,128]{2,1,0:T(8,128)} %cotangent.1, ...), custom_call_target="tpu_custom_call" | custom-call | tf_op jit(solution)/shard_map/layer/pallas_call | solution.py:994
  42.1 15.8 %sums.1 = (f32[64,32,128]{2,1,0:T(8,128)}, f32[64,32,128]{2,1,0:T(8,128)}, f32[64,32,128]{2,1,0:T(8,128)}, f32[32,8,128]{2,1,0:T(8,128)}) custom-call(f32[4,64,128]{2,1,0:T(8,128)} %get-tuple-element.63.acc_in, f32[34,64,128]{2,1,0:T(8,128)} %get-tuple-element.64.own_in, f32[2,64,128]{2,1,0:T(8,128)} %get-tuple-element.65.cells_in, ...), custom_call_target="tpu_custom_call" | custom-call | tf_op jit(solution)/shard_map/sums/pallas_call | solution.py:1402
  57.9 2.9 %final.1 = (f32[64,32,128]{2,1,0:T(8,128)}, f32[64,32,128]{2,1,0:T(8,128)}, f32[64,32,128]{2,1,0:T(8,128)}, f32[1,1]{1,0:T(1,128)}, f32[64,192]{1,0:T(8,128)}, /...) custom-call(f32[64,32,128]{2,1,0:T(8,128)} %get-tuple-element.69.ref, ...), custom_call_target="tpu_custom_call" | custom-call | tf_op jit(solution)/shard_map/final/pallas_call | solution.py:1506
